TPU v7x, 256 devices: a whole 4x4x8 slice. The times are simulated.
256 devices in a mesh: dp: 16 (over z_hi, x, core), mp: 16 (over z_lo, y).
Axes of the slice: x: 4, y: 4, z: 8 (z_hi: 2, z_lo: 4; z = z_hi * 4 + z_lo), core: 2. Of those that a mesh axis runs over, the one named last changes fastest.
Arguments:
- tokens: bfloat16 [8192, 3072], P(('dp', 'mp')), may hold values from -500 to 500
- gain: float32 [3072], replicated, may hold values from 0.5 to 1.5
- encoder: bfloat16 [3072, 384], P('dp'), may hold values from -0.109375 to 0.109375
- w_up: bfloat16 [3072, 12288], P(None, 'mp'), may hold values from -0.3125 to 0.3125
- w_down: bfloat16 [3072, 12288], P(None, 'mp'), may hold values from -0.0546875 to 0.0546875
- cotangent: bfloat16 [8192, 3072], P(('dp', 'mp')), may hold values from -6 to 6
Outputs:
- grad_tokens: bfloat16 [8192, 3072], P(('dp', 'mp'))
- grad_up: float32 [3072, 12288], P('dp', 'mp')
- grad_down: float32 [3072, 12288], P('dp', 'mp')
- grad_encoder: float32 [3072, 384], P(('dp', 'mp'))
- grad_gain: float32 [3072], P(('dp', 'mp'))
All inputs are finite; a program needn't handle non-finite values.
Results may differ from a plain program's by a relative error of at most 0.035.
Values may be sent and summed in bfloat16 or wider, within the bound.
No kernel may reach another device: no remote copies, remote signals or barrier semaphores. Data moves between devices by JAX's collectives and lax.ppermute only.
A program may use at most 128 MiB of HBM per device.

v0:
```python
import jax
import jax.numpy as jnp
from jax import lax
from jax.sharding import PartitionSpec as P


def gelu_parts(pre_act):
    cdf_part = 0.5 * (1.0 + lax.erf(pre_act * 0.7071067811865476))
    density = jnp.exp(-0.5 * pre_act * pre_act) * 0.3989422804014327
    return (pre_act * cdf_part, cdf_part + pre_act * density)


def on_device(tokens, gain, encoder, w_up, w_down, cotangent):
    full_encoder = lax.all_gather(encoder, "dp", axis=0, tiled=True)
    as_float = tokens.astype(jnp.float32)
    center = as_float - jnp.mean(as_float, axis=1, keepdims=True)
    inv_std = lax.rsqrt(jnp.mean(center * center, axis=1, keepdims=True) + 1e-06)
    unit = center * inv_std
    normed = (unit * gain).astype(jnp.bfloat16)
    code_rows = jnp.dot(normed, full_encoder, preferred_element_type=jnp.float32).astype(
        jnp.bfloat16
    )
    all_codes = lax.all_gather(code_rows, "mp", axis=0, tiled=True)
    decoded = jnp.einsum(
        "tc,dc->td", all_codes, full_encoder, preferred_element_type=jnp.float32
    ).astype(jnp.bfloat16)
    pre_act = jnp.dot(decoded, w_up, preferred_element_type=jnp.float32)
    gelu_val, gelu_slope = gelu_parts(pre_act)
    hidden = gelu_val.astype(jnp.bfloat16)
    upstream = lax.all_gather(cotangent, "mp", axis=0, tiled=True)
    d_hidden = jnp.dot(upstream, w_down, preferred_element_type=jnp.float32)
    d_act = (d_hidden * gelu_slope).astype(jnp.bfloat16)
    down_term = jnp.einsum("td,tf->df", upstream, hidden, preferred_element_type=jnp.float32)
    partial_value = jnp.einsum("tf,df->td", d_act, w_up, preferred_element_type=jnp.float32).astype(
        jnp.bfloat16
    )
    up_term = jnp.einsum("td,tf->df", decoded, d_act, preferred_element_type=jnp.float32)
    grad_up, grad_down = (
        lax.psum_scatter(
            up_term.astype(jnp.bfloat16), "dp", scatter_dimension=0, tiled=True
        ).astype(jnp.float32),
        lax.psum_scatter(
            down_term.astype(jnp.bfloat16), "dp", scatter_dimension=0, tiled=True
        ).astype(jnp.float32),
    )
    summed = lax.psum_scatter(partial_value, "mp", scatter_dimension=0, tiled=True).astype(
        jnp.float32
    )
    grad_codes = jnp.dot(
        summed, full_encoder.astype(jnp.float32), precision=lax.Precision.HIGHEST
    ).astype(jnp.bfloat16)
    decode_term = jnp.einsum(
        "td,tc->dc", summed, code_rows.astype(jnp.float32), precision=lax.Precision.HIGHEST
    )
    d_normed = jnp.einsum("tc,dc->td", grad_codes, full_encoder, preferred_element_type=jnp.float32)
    encode_term = jnp.einsum("td,tc->dc", normed, grad_codes, preferred_element_type=jnp.float32)
    gain_term = jnp.sum(d_normed * unit, axis=0)
    dx_hat = d_normed * gain
    mean_one = jnp.mean(dx_hat, axis=1, keepdims=True)
    mean_two = jnp.mean(dx_hat * unit, axis=1, keepdims=True)
    grad_tokens = (
        cotangent.astype(jnp.float32) + inv_std * (dx_hat - mean_one - unit * mean_two)
    ).astype(jnp.bfloat16)
    grad_encoder, grad_gain = (
        lax.psum_scatter(encode_term + decode_term, ("dp", "mp"), scatter_dimension=0, tiled=True),
        lax.psum_scatter(gain_term, ("dp", "mp"), scatter_dimension=0, tiled=True),
    )
    return (grad_tokens, grad_up, grad_down, grad_encoder, grad_gain)


def solution(mesh):
    placed = (
        P(("dp", "mp"), None),
        P(),
        P("dp", None),
        P(None, "mp"),
        P(None, "mp"),
        P(("dp", "mp"), None),
    )
    return jax.shard_map(
        on_device,
        mesh=mesh,
        in_specs=placed,
        out_specs=(
            P(("dp", "mp"), None),
            P("dp", "mp"),
            P("dp", "mp"),
            P(("dp", "mp"), None),
            P(("dp", "mp")),
        ),
        check_vma=False,
    )
```

profile of v0, /device:TPU:2, one launch (start us, length us, event | category | flops | bytes accessed | tf_op | source)
XLA Modules:
  0.0 1574.4 jit_solution(705065401206876088)
XLA Ops:
  10.9 67.3 %all-gather.5.cloned.1.call-done = bf16[3072,384]{1,0:T(8,128)(2,1)} async-done(((bf16[192,384]{1,0:T(8,128)(2,1)}), bf16[3072,384]{1,0:T(8,128)(2,1)}) %all-gather.5.cloned.1.call-update) | async-done | bytes 2359312 | tf_op jit(solution)/shard_map/all_gather | solution.py:14
  80.5 42.7 %all_gather.11 = bf16[512,384]{1,0:T(8,128)(2,1)S(1)} all-gather(bf16[32,384]{1,0:T(8,128)(2,1)S(1)} %convolution_convert_fusion.5), channel_id=1, replica_groups=mesh['dp'=16,'mp'=16] {'mp'}, dimensions={0}, use_global_device_ids=true | all-gather | bytes 417792 | tf_op jit(solution)/shard_map/all_gather | solution.py:23
  123.3 3.6 convolution_convert_fusion.3
  131.0 31.9 %all-gather.3.cloned.1.call-done = bf16[512,3072]{1,0:T(8,128)(2,1)} async-done(((bf16[32,3072]{1,0:T(8,128)(2,1)}), bf16[512,3072]{1,0:T(8,128)(2,1)}) %all-gather.3.cloned.1.call-update) | async-done | bytes 3145744 | tf_op jit(solution)/shard_map/all_gather | solution.py:30
  162.9 6.1 fusion.7
  169.1 6.4 convolution_convert_fusion.2
  175.6 6.3 fusion.1
  181.9 6.6 copy.13
  188.8 6.7 convolution_convert_fusion.1
  195.6 69.6 %reduce-scatter.8.cloned.1.call-done = bf16[32,3072]{1,0:T(8,128)(2,1)} async-done(((bf16[512,3072]{1,0:T(8,128)(2,1)}), bf16[32,3072]{1,0:T(8,128)(2,1)}) %reduce-scatter.8.cloned.1.call-update) | async-done | bytes 196624 | tf_op jit(solution)/shard_map/reduce_scatter | solution.py:46
  267.6 3.0 convolution_add_fusion
  270.6 655.0 %fusion = f32[16,384]{1,0:T(8,128)S(1)} fusion(f32[3072,384]{1,0:T(8,128)} %convolution_add_fusion), kind=kCustom, calls=%all-reduce-scatter | all-reduce-scatter fusion | flops 1572865 | bytes 4743168
  925.7 6.0 collective-permute-start.62
  934.2 5.2 collective-permute-start.63
  942.7 17.9 %collective-permute-start.57 = (f32[16,384]{1,0:T(8,128)S(1)}, f32[16,384]{1,0:T(8,128)S(1)}, u32[]{:S(2)}, u32[]{:S(2)}) collective-permute-start(f32[16,384]{1,0:T(8,128)S(1)} %fusion), channel_id=1, source_target_pairs={{0,58},{1,59},{2,60},{3,61},{4,62},{5,63},{6,64},{7,65},{8,66},{9,... | collective-permute-start | bytes 73736
  960.5 7.7 collective-permute-start.56
  968.3 8.7 collective-permute-start.55
  977.0 7.1 collective-permute-start.54
  984.1 17.4 %collective-permute-start.53 = (f32[16,384]{1,0:T(8,128)S(1)}, f32[16,384]{1,0:T(8,128)S(1)}, u32[]{:S(2)}, u32[]{:S(2)}) collective-permute-start(f32[16,384]{1,0:T(8,128)S(1)} %fusion), channel_id=1, source_target_pairs={{0,54},{1,55},{2,56},{3,57},{4,58},{5,59},{6,60},{7,61},{8,62},{9,... | collective-permute-start | bytes 73736
  1001.4 7.4 collective-permute-start.52
  1008.8 3.6 collective-permute-start.51
  1012.5 4.7 collective-permute-start.50
  1017.2 4.9 collective-permute-start.49
  1025.1 3.8 collective-permute-start.46
  1039.3 4.3 collective-permute-start.38
  1043.7 4.2 collective-permute-start.37
  1047.8 2.9 collective-permute-start.36
  1050.7 3.3 collective-permute-start.35
  1056.1 3.6 collective-permute-start.33
  1059.7 3.4 collective-permute-start.32
  1063.1 3.6 collective-permute-start.31
  1066.7 6.4 collective-permute-start.30
  1073.2 3.3 collective-permute-start.29
  1076.6 13.1 collective-permute-start.28
  1089.7 13.1 collective-permute-start.27
  1102.9 13.1 collective-permute-start.26
  1116.0 13.1 collective-permute-start.25
  1129.2 13.1 collective-permute-start.24
  1142.3 13.1 collective-permute-start.23
  1155.5 13.1 collective-permute-start.22
  1168.6 13.1 collective-permute-start.21
  1181.8 13.1 collective-permute-start.20
  1194.9 13.1 collective-permute-start.19
  1208.1 13.1 collective-permute-start.18
  1221.2 13.1 collective-permute-start.17
  1234.4 13.1 collective-permute-start.16
  1247.5 13.1 collective-permute-start.15
  1260.8 13.1 collective-permute-start.14
  1274.0 13.1 collective-permute-start.13
  1287.1 13.1 collective-permute-start.12
  1300.2 13.1 collective-permute-start.11
  1313.4 13.1 collective-permute-start.10
  1327.5 13.1 collective-permute-start.9
  1340.6 13.1 collective-permute-start.8
  1353.8 13.1 collective-permute-start.7
  1366.9 13.1 collective-permute-start.6
  1380.1 13.1 collective-permute-start.5
  1393.2 13.1 collective-permute-start.4
  1406.4 13.1 collective-permute-start.3
  1419.5 13.1 collective-permute-start.2
  1432.7 13.1 collective-permute-start.1
  1445.8 13.1 collective-permute-start
  1459.8 77.8 %all-reduce.1 = f32[3072]{0:T(1024)S(1)} all-reduce(f32[3072]{0:T(1024)S(1)} %get-tuple-element.15), channel_id=6, replica_groups=mesh['dp'=16,'mp'=16] {'dp','mp'}, use_global_device_ids=true, to_apply=%region_9.0.clone | all-reduce | flops 3072 | bytes 24576
  1538.3 25.1 %concatenate = f32[1036,384]{1,0:T(8,128)S(1)} concatenate(f32[12,384]{1,0:T(8,128)S(1)} %collective-permute-done.63, f32[16,384]{1,0:T(8,128)S(1)} %collective-permute-done.62, f32[16,384]{1,0:T(8,128)S(1)} %collective-permute-done.61, f32[16,384]{1,0:T(8,128)S(1)} %collective-permute-done.60, f32[16,384]{1,0:T(8,128)S(1)} %collective-permute-done.59, ...), dimensions={0} | concatenate | bytes 3182592
  (164 shorter events, 41.3 us)
Async XLA Ops:
  7.2 71.0 %all-gather.5.cloned.1.call-start = ((), (), s32[]{:S(2)}) async-start(), calls=%async_computation.4 | async-start | bytes 2506752 | tf_op jit(solution)/shard_map/all_gather | solution.py:14
  7.9 155.0 %all-gather.3.cloned.1.call-start = ((), (), s32[]{:S(2)}) async-start(), calls=%async_computation.3 | async-start | bytes 3342336 | tf_op jit(solution)/shard_map/all_gather | solution.py:30
  8.6 256.5 %reduce-scatter.8.cloned.1.call-start = ((), (), s32[]{:S(2)}) async-start(), calls=%async_computation.5 | async-start | bytes 3342336 | tf_op jit(solution)/shard_map/reduce_scatter | solution.py:46
  175.5 1388.5 %reduce-scatter.12.cloned.1.call-start = ((), (), s32[]{:S(2)}) async-start(), calls=%async_computation.7 | async-start | bytes 5013504
  188.6 1377.5 %reduce-scatter.10.cloned.1.call-start = ((), (), s32[]{:S(2)}) async-start(), calls=%async_computation.6 | async-start | bytes 5013504 | tf_op jit(solution)/shard_map/reduce_scatter | solution.py:39
  925.7 17.0 %collective-permute-start.62 = (f32[16,384]{1,0:T(8,128)S(1)}, f32[16,384]{1,0:T(8,128)S(1)}, u32[]{:S(2)}, u32[]{:S(2)}) collective-permute-start(f32[16,384]{1,0:T(8,128)S(1)} %fusion), channel_id=1, source_target_pairs={{0,63},{1,64},{2,65},{3,66},{4,67},{5,68},{6,69},{7,70},{8,71},{9,... | collective-permute-start | bytes 73736
  931.6 28.9 %collective-permute-start.61 = (f32[16,384]{1,0:T(8,128)S(1)}, f32[16,384]{1,0:T(8,128)S(1)}, u32[]{:S(2)}, u32[]{:S(2)}) collective-permute-start(f32[16,384]{1,0:T(8,128)S(1)} %fusion), channel_id=1, source_target_pairs={{0,62},{1,63},{2,64},{3,65},{4,66},{5,67},{6,68},{7,69},{8,70},{9,... | collective-permute-start | bytes 73736
  932.9 35.4 %collective-permute-start.60 = (f32[16,384]{1,0:T(8,128)S(1)}, f32[16,384]{1,0:T(8,128)S(1)}, u32[]{:S(2)}, u32[]{:S(2)}) collective-permute-start(f32[16,384]{1,0:T(8,128)S(1)} %fusion), channel_id=1, source_target_pairs={{0,61},{1,62},{2,63},{3,64},{4,65},{5,66},{6,67},{7,68},{8,69},{9,... | collective-permute-start | bytes 73736
  939.4 37.5 %collective-permute-start.59 = (f32[16,384]{1,0:T(8,128)S(1)}, f32[16,384]{1,0:T(8,128)S(1)}, u32[]{:S(2)}, u32[]{:S(2)}) collective-permute-start(f32[16,384]{1,0:T(8,128)S(1)} %fusion), channel_id=1, source_target_pairs={{0,60},{1,61},{2,62},{3,63},{4,64},{5,65},{6,66},{7,67},{8,68},{9,... | collective-permute-start | bytes 73736
  941.0 43.0 %collective-permute-start.58 = (f32[16,384]{1,0:T(8,128)S(1)}, f32[16,384]{1,0:T(8,128)S(1)}, u32[]{:S(2)}, u32[]{:S(2)}) collective-permute-start(f32[16,384]{1,0:T(8,128)S(1)} %fusion), channel_id=1, source_target_pairs={{0,59},{1,60},{2,61},{3,62},{4,63},{5,64},{6,65},{7,66},{8,67},{9,... | collective-permute-start | bytes 73736
  942.7 58.8 %collective-permute-start.57 = (f32[16,384]{1,0:T(8,128)S(1)}, f32[16,384]{1,0:T(8,128)S(1)}, u32[]{:S(2)}, u32[]{:S(2)}) collective-permute-start(f32[16,384]{1,0:T(8,128)S(1)} %fusion), channel_id=1, source_target_pairs={{0,58},{1,59},{2,60},{3,61},{4,62},{5,63},{6,64},{7,65},{8,66},{9,... | collective-permute-start | bytes 73736
  960.5 48.3 %collective-permute-start.56 = (f32[16,384]{1,0:T(8,128)S(1)}, f32[16,384]{1,0:T(8,128)S(1)}, u32[]{:S(2)}, u32[]{:S(2)}) collective-permute-start(f32[16,384]{1,0:T(8,128)S(1)} %fusion), channel_id=1, source_target_pairs={{0,57},{1,58},{2,59},{3,60},{4,61},{5,62},{6,63},{7,64},{8,65},{9,... | collective-permute-start | bytes 73736
  968.3 44.2 %collective-permute-start.55 = (f32[16,384]{1,0:T(8,128)S(1)}, f32[16,384]{1,0:T(8,128)S(1)}, u32[]{:S(2)}, u32[]{:S(2)}) collective-permute-start(f32[16,384]{1,0:T(8,128)S(1)} %fusion), channel_id=1, source_target_pairs={{0,56},{1,57},{2,58},{3,59},{4,60},{5,61},{6,62},{7,63},{8,64},{9,... | collective-permute-start | bytes 73736
  977.0 40.2 %collective-permute-start.54 = (f32[16,384]{1,0:T(8,128)S(1)}, f32[16,384]{1,0:T(8,128)S(1)}, u32[]{:S(2)}, u32[]{:S(2)}) collective-permute-start(f32[16,384]{1,0:T(8,128)S(1)} %fusion), channel_id=1, source_target_pairs={{0,55},{1,56},{2,57},{3,58},{4,59},{5,60},{6,61},{7,62},{8,63},{9,... | collective-permute-start | bytes 73736
  984.1 38.0 %collective-permute-start.53 = (f32[16,384]{1,0:T(8,128)S(1)}, f32[16,384]{1,0:T(8,128)S(1)}, u32[]{:S(2)}, u32[]{:S(2)}) collective-permute-start(f32[16,384]{1,0:T(8,128)S(1)} %fusion), channel_id=1, source_target_pairs={{0,54},{1,55},{2,56},{3,57},{4,58},{5,59},{6,60},{7,61},{8,62},{9,... | collective-permute-start | bytes 73736
  1001.4 22.0 %collective-permute-start.52 = (f32[16,384]{1,0:T(8,128)S(1)}, f32[16,384]{1,0:T(8,128)S(1)}, u32[]{:S(2)}, u32[]{:S(2)}) collective-permute-start(f32[16,384]{1,0:T(8,128)S(1)} %fusion), channel_id=1, source_target_pairs={{0,53},{1,54},{2,55},{3,56},{4,57},{5,58},{6,59},{7,60},{8,61},{9,... | collective-permute-start | bytes 73736
  1008.8 16.2 %collective-permute-start.51 = (f32[16,384]{1,0:T(8,128)S(1)}, f32[16,384]{1,0:T(8,128)S(1)}, u32[]{:S(2)}, u32[]{:S(2)}) collective-permute-start(f32[16,384]{1,0:T(8,128)S(1)} %fusion), channel_id=1, source_target_pairs={{0,52},{1,53},{2,54},{3,55},{4,56},{5,57},{6,58},{7,59},{8,60},{9,... | collective-permute-start | bytes 73736
  1012.5 16.4 %collective-permute-start.50 = (f32[16,384]{1,0:T(8,128)S(1)}, f32[16,384]{1,0:T(8,128)S(1)}, u32[]{:S(2)}, u32[]{:S(2)}) collective-permute-start(f32[16,384]{1,0:T(8,128)S(1)} %fusion), channel_id=1, source_target_pairs={{0,51},{1,52},{2,53},{3,54},{4,55},{5,56},{6,57},{7,58},{8,59},{9,... | collective-permute-start | bytes 73736
  1017.2 13.0 collective-permute-start.49
  1023.4 10.2 collective-permute-start.47
  1025.1 9.8 collective-permute-start.46
  1033.6 10.0 collective-permute-start.42
  1034.9 12.9 collective-permute-start.41
  1036.2 14.5 collective-permute-start.40
  1037.5 16.5 %collective-permute-start.39 = (f32[16,384]{1,0:T(8,128)S(1)}, f32[16,384]{1,0:T(8,128)S(1)}, u32[]{:S(2)}, u32[]{:S(2)}) collective-permute-start(f32[16,384]{1,0:T(8,128)S(1)} %fusion), channel_id=1, source_target_pairs={{0,40},{1,41},{2,42},{3,43},{4,44},{5,45},{6,46},{7,47},{8,48},{9,... | collective-permute-start | bytes 73736
  1039.3 16.8 %collective-permute-start.38 = (f32[16,384]{1,0:T(8,128)S(1)}, f32[16,384]{1,0:T(8,128)S(1)}, u32[]{:S(2)}, u32[]{:S(2)}) collective-permute-start(f32[16,384]{1,0:T(8,128)S(1)} %fusion), channel_id=1, source_target_pairs={{0,39},{1,40},{2,41},{3,42},{4,43},{5,44},{6,45},{7,46},{8,47},{9,... | collective-permute-start | bytes 73736
  1043.7 16.1 %collective-permute-start.37 = (f32[16,384]{1,0:T(8,128)S(1)}, f32[16,384]{1,0:T(8,128)S(1)}, u32[]{:S(2)}, u32[]{:S(2)}) collective-permute-start(f32[16,384]{1,0:T(8,128)S(1)} %fusion), channel_id=1, source_target_pairs={{0,38},{1,39},{2,40},{3,41},{4,42},{5,43},{6,44},{7,45},{8,46},{9,... | collective-permute-start | bytes 73736
  1047.8 15.3 collective-permute-start.36
  1050.7 16.0 %collective-permute-start.35 = (f32[16,384]{1,0:T(8,128)S(1)}, f32[16,384]{1,0:T(8,128)S(1)}, u32[]{:S(2)}, u32[]{:S(2)}) collective-permute-start(f32[16,384]{1,0:T(8,128)S(1)} %fusion), channel_id=1, source_target_pairs={{0,36},{1,37},{2,38},{3,39},{4,40},{5,41},{6,42},{7,43},{8,44},{9,... | collective-permute-start | bytes 73736
  1054.0 19.2 %collective-permute-start.34 = (f32[16,384]{1,0:T(8,128)S(1)}, f32[16,384]{1,0:T(8,128)S(1)}, u32[]{:S(2)}, u32[]{:S(2)}) collective-permute-start(f32[16,384]{1,0:T(8,128)S(1)} %fusion), channel_id=1, source_target_pairs={{0,35},{1,36},{2,37},{3,38},{4,39},{5,40},{6,41},{7,42},{8,43},{9,... | collective-permute-start | bytes 73736
  1056.1 20.4 %collective-permute-start.33 = (f32[16,384]{1,0:T(8,128)S(1)}, f32[16,384]{1,0:T(8,128)S(1)}, u32[]{:S(2)}, u32[]{:S(2)}) collective-permute-start(f32[16,384]{1,0:T(8,128)S(1)} %fusion), channel_id=1, source_target_pairs={{0,34},{1,35},{2,36},{3,37},{4,38},{5,39},{6,40},{7,41},{8,42},{9,... | collective-permute-start | bytes 73736
  1059.7 30.0 %collective-permute-start.32 = (f32[16,384]{1,0:T(8,128)S(1)}, f32[16,384]{1,0:T(8,128)S(1)}, u32[]{:S(2)}, u32[]{:S(2)}) collective-permute-start(f32[16,384]{1,0:T(8,128)S(1)} %fusion), channel_id=1, source_target_pairs={{0,33},{1,34},{2,35},{3,36},{4,37},{5,38},{6,39},{7,40},{8,41},{9,... | collective-permute-start | bytes 73736
  1063.1 39.7 %collective-permute-start.31 = (f32[16,384]{1,0:T(8,128)S(1)}, f32[16,384]{1,0:T(8,128)S(1)}, u32[]{:S(2)}, u32[]{:S(2)}) collective-permute-start(f32[16,384]{1,0:T(8,128)S(1)} %fusion), channel_id=1, source_target_pairs={{0,32},{1,33},{2,34},{3,35},{4,36},{5,37},{6,38},{7,39},{8,40},{9,... | collective-permute-start | bytes 73736
  1066.7 49.3 %collective-permute-start.30 = (f32[16,384]{1,0:T(8,128)S(1)}, f32[16,384]{1,0:T(8,128)S(1)}, u32[]{:S(2)}, u32[]{:S(2)}) collective-permute-start(f32[16,384]{1,0:T(8,128)S(1)} %fusion), channel_id=1, source_target_pairs={{0,31},{1,32},{2,33},{3,34},{4,35},{5,36},{6,37},{7,38},{8,39},{9,... | collective-permute-start | bytes 73736
  1073.2 55.9 %collective-permute-start.29 = (f32[16,384]{1,0:T(8,128)S(1)}, f32[16,384]{1,0:T(8,128)S(1)}, u32[]{:S(2)}, u32[]{:S(2)}) collective-permute-start(f32[16,384]{1,0:T(8,128)S(1)} %fusion), channel_id=1, source_target_pairs={{0,30},{1,31},{2,32},{3,33},{4,34},{5,35},{6,36},{7,37},{8,38},{9,... | collective-permute-start | bytes 73736
  1076.6 65.7 %collective-permute-start.28 = (f32[16,384]{1,0:T(8,128)S(1)}, f32[16,384]{1,0:T(8,128)S(1)}, u32[]{:S(2)}, u32[]{:S(2)}) collective-permute-start(f32[16,384]{1,0:T(8,128)S(1)} %fusion), channel_id=1, source_target_pairs={{0,29},{1,30},{2,31},{3,32},{4,33},{5,34},{6,35},{7,36},{8,37},{9,... | collective-permute-start | bytes 73736
  1089.7 65.7 %collective-permute-start.27 = (f32[16,384]{1,0:T(8,128)S(1)}, f32[16,384]{1,0:T(8,128)S(1)}, u32[]{:S(2)}, u32[]{:S(2)}) collective-permute-start(f32[16,384]{1,0:T(8,128)S(1)} %fusion), channel_id=1, source_target_pairs={{0,28},{1,29},{2,30},{3,31},{4,32},{5,33},{6,34},{7,35},{8,36},{9,... | collective-permute-start | bytes 73736
  1102.9 65.7 %collective-permute-start.26 = (f32[16,384]{1,0:T(8,128)S(1)}, f32[16,384]{1,0:T(8,128)S(1)}, u32[]{:S(2)}, u32[]{:S(2)}) collective-permute-start(f32[16,384]{1,0:T(8,128)S(1)} %fusion), channel_id=1, source_target_pairs={{0,27},{1,28},{2,29},{3,30},{4,31},{5,32},{6,33},{7,34},{8,35},{9,... | collective-permute-start | bytes 73736
  1116.0 65.7 %collective-permute-start.25 = (f32[16,384]{1,0:T(8,128)S(1)}, f32[16,384]{1,0:T(8,128)S(1)}, u32[]{:S(2)}, u32[]{:S(2)}) collective-permute-start(f32[16,384]{1,0:T(8,128)S(1)} %fusion), channel_id=1, source_target_pairs={{0,26},{1,27},{2,28},{3,29},{4,30},{5,31},{6,32},{7,33},{8,34},{9,... | collective-permute-start | bytes 73736
  1129.2 65.7 %collective-permute-start.24 = (f32[16,384]{1,0:T(8,128)S(1)}, f32[16,384]{1,0:T(8,128)S(1)}, u32[]{:S(2)}, u32[]{:S(2)}) collective-permute-start(f32[16,384]{1,0:T(8,128)S(1)} %fusion), channel_id=1, source_target_pairs={{0,25},{1,26},{2,27},{3,28},{4,29},{5,30},{6,31},{7,32},{8,33},{9,... | collective-permute-start | bytes 73736
  1142.3 65.7 %collective-permute-start.23 = (f32[16,384]{1,0:T(8,128)S(1)}, f32[16,384]{1,0:T(8,128)S(1)}, u32[]{:S(2)}, u32[]{:S(2)}) collective-permute-start(f32[16,384]{1,0:T(8,128)S(1)} %fusion), channel_id=1, source_target_pairs={{0,24},{1,25},{2,26},{3,27},{4,28},{5,29},{6,30},{7,31},{8,32},{9,... | collective-permute-start | bytes 73736
  1155.5 65.7 %collective-permute-start.22 = (f32[16,384]{1,0:T(8,128)S(1)}, f32[16,384]{1,0:T(8,128)S(1)}, u32[]{:S(2)}, u32[]{:S(2)}) collective-permute-start(f32[16,384]{1,0:T(8,128)S(1)} %fusion), channel_id=1, source_target_pairs={{0,23},{1,24},{2,25},{3,26},{4,27},{5,28},{6,29},{7,30},{8,31},{9,... | collective-permute-start | bytes 73736
  1168.6 65.7 %collective-permute-start.21 = (f32[16,384]{1,0:T(8,128)S(1)}, f32[16,384]{1,0:T(8,128)S(1)}, u32[]{:S(2)}, u32[]{:S(2)}) collective-permute-start(f32[16,384]{1,0:T(8,128)S(1)} %fusion), channel_id=1, source_target_pairs={{0,22},{1,23},{2,24},{3,25},{4,26},{5,27},{6,28},{7,29},{8,30},{9,... | collective-permute-start | bytes 73736
  1181.8 65.7 %collective-permute-start.20 = (f32[16,384]{1,0:T(8,128)S(1)}, f32[16,384]{1,0:T(8,128)S(1)}, u32[]{:S(2)}, u32[]{:S(2)}) collective-permute-start(f32[16,384]{1,0:T(8,128)S(1)} %fusion), channel_id=1, source_target_pairs={{0,21},{1,22},{2,23},{3,24},{4,25},{5,26},{6,27},{7,28},{8,29},{9,... | collective-permute-start | bytes 73736
  1194.9 65.9 %collective-permute-start.19 = (f32[16,384]{1,0:T(8,128)S(1)}, f32[16,384]{1,0:T(8,128)}, u32[]{:S(2)}, u32[]{:S(2)}) collective-permute-start(f32[16,384]{1,0:T(8,128)S(1)} %fusion), channel_id=1, source_target_pairs={{0,20},{1,21},{2,22},{3,23},{4,24},{5,25},{6,26},{7,27},{8,28},{9,... | collective-permute-start | bytes 73736
  1208.1 65.9 %collective-permute-start.18 = (f32[16,384]{1,0:T(8,128)S(1)}, f32[16,384]{1,0:T(8,128)}, u32[]{:S(2)}, u32[]{:S(2)}) collective-permute-start(f32[16,384]{1,0:T(8,128)S(1)} %fusion), channel_id=1, source_target_pairs={{0,19},{1,20},{2,21},{3,22},{4,23},{5,24},{6,25},{7,26},{8,27},{9,... | collective-permute-start | bytes 73736
  1221.2 65.9 %collective-permute-start.17 = (f32[16,384]{1,0:T(8,128)S(1)}, f32[16,384]{1,0:T(8,128)}, u32[]{:S(2)}, u32[]{:S(2)}) collective-permute-start(f32[16,384]{1,0:T(8,128)S(1)} %fusion), channel_id=1, source_target_pairs={{0,18},{1,19},{2,20},{3,21},{4,22},{5,23},{6,24},{7,25},{8,26},{9,... | collective-permute-start | bytes 73736
  1234.4 65.9 %collective-permute-start.16 = (f32[16,384]{1,0:T(8,128)S(1)}, f32[16,384]{1,0:T(8,128)}, u32[]{:S(2)}, u32[]{:S(2)}) collective-permute-start(f32[16,384]{1,0:T(8,128)S(1)} %fusion), channel_id=1, source_target_pairs={{0,17},{1,18},{2,19},{3,20},{4,21},{5,22},{6,23},{7,24},{8,25},{9,... | collective-permute-start | bytes 73736
  1247.5 65.8 %collective-permute-start.15 = (f32[16,384]{1,0:T(8,128)S(1)}, f32[16,384]{1,0:T(8,128)}, u32[]{:S(2)}, u32[]{:S(2)}) collective-permute-start(f32[16,384]{1,0:T(8,128)S(1)} %fusion), channel_id=1, source_target_pairs={{0,16},{1,17},{2,18},{3,19},{4,20},{5,21},{6,22},{7,23},{8,24},{9,... | collective-permute-start | bytes 73736
  1260.8 66.7 %collective-permute-start.14 = (f32[16,384]{1,0:T(8,128)S(1)}, f32[16,384]{1,0:T(8,128)S(1)}, u32[]{:S(2)}, u32[]{:S(2)}) collective-permute-start(f32[16,384]{1,0:T(8,128)S(1)} %fusion), channel_id=1, source_target_pairs={{0,15},{1,16},{2,17},{3,18},{4,19},{5,20},{6,21},{7,22},{8,23},{9,... | collective-permute-start | bytes 73736
  1274.0 66.7 %collective-permute-start.13 = (f32[16,384]{1,0:T(8,128)S(1)}, f32[16,384]{1,0:T(8,128)S(1)}, u32[]{:S(2)}, u32[]{:S(2)}) collective-permute-start(f32[16,384]{1,0:T(8,128)S(1)} %fusion), channel_id=1, source_target_pairs={{0,14},{1,15},{2,16},{3,17},{4,18},{5,19},{6,20},{7,21},{8,22},{9,... | collective-permute-start | bytes 73736
  1287.1 66.7 %collective-permute-start.12 = (f32[16,384]{1,0:T(8,128)S(1)}, f32[16,384]{1,0:T(8,128)S(1)}, u32[]{:S(2)}, u32[]{:S(2)}) collective-permute-start(f32[16,384]{1,0:T(8,128)S(1)} %fusion), channel_id=1, source_target_pairs={{0,13},{1,14},{2,15},{3,16},{4,17},{5,18},{6,19},{7,20},{8,21},{9,... | collective-permute-start | bytes 73736
  1300.2 66.7 %collective-permute-start.11 = (f32[16,384]{1,0:T(8,128)S(1)}, f32[16,384]{1,0:T(8,128)S(1)}, u32[]{:S(2)}, u32[]{:S(2)}) collective-permute-start(f32[16,384]{1,0:T(8,128)S(1)} %fusion), channel_id=1, source_target_pairs={{0,12},{1,13},{2,14},{3,15},{4,16},{5,17},{6,18},{7,19},{8,20},{9,... | collective-permute-start | bytes 73736
  1313.4 66.7 %collective-permute-start.10 = (f32[16,384]{1,0:T(8,128)S(1)}, f32[16,384]{1,0:T(8,128)S(1)}, u32[]{:S(2)}, u32[]{:S(2)}) collective-permute-start(f32[16,384]{1,0:T(8,128)S(1)} %fusion), channel_id=1, source_target_pairs={{0,11},{1,12},{2,13},{3,14},{4,15},{5,16},{6,17},{7,18},{8,19},{9,... | collective-permute-start | bytes 73736
  1327.5 65.7 %collective-permute-start.9 = (f32[16,384]{1,0:T(8,128)S(1)}, f32[16,384]{1,0:T(8,128)S(1)}, u32[]{:S(2)}, u32[]{:S(2)}) collective-permute-start(f32[16,384]{1,0:T(8,128)S(1)} %fusion), channel_id=1, source_target_pairs={{0,10},{1,11},{2,12},{3,13},{4,14},{5,15},{6,16},{7,17},{8,18},{9,... | collective-permute-start | bytes 73736
  1340.6 65.7 %collective-permute-start.8 = (f32[16,384]{1,0:T(8,128)S(1)}, f32[16,384]{1,0:T(8,128)S(1)}, u32[]{:S(2)}, u32[]{:S(2)}) collective-permute-start(f32[16,384]{1,0:T(8,128)S(1)} %fusion), channel_id=1, source_target_pairs={{0,9},{1,10},{2,11},{3,12},{4,13},{5,14},{6,15},{7,16},{8,17},{9,1... | collective-permute-start | bytes 73736
  1353.8 65.7 %collective-permute-start.7 = (f32[16,384]{1,0:T(8,128)S(1)}, f32[16,384]{1,0:T(8,128)S(1)}, u32[]{:S(2)}, u32[]{:S(2)}) collective-permute-start(f32[16,384]{1,0:T(8,128)S(1)} %fusion), channel_id=1, source_target_pairs={{0,8},{1,9},{2,10},{3,11},{4,12},{5,13},{6,14},{7,15},{8,16},{9,17... | collective-permute-start | bytes 73736
  1366.9 65.7 %collective-permute-start.6 = (f32[16,384]{1,0:T(8,128)S(1)}, f32[16,384]{1,0:T(8,128)S(1)}, u32[]{:S(2)}, u32[]{:S(2)}) collective-permute-start(f32[16,384]{1,0:T(8,128)S(1)} %fusion), channel_id=1, source_target_pairs={{0,7},{1,8},{2,9},{3,10},{4,11},{5,12},{6,13},{7,14},{8,15},{9,16}... | collective-permute-start | bytes 73736
  1380.1 65.7 %collective-permute-start.5 = (f32[16,384]{1,0:T(8,128)S(1)}, f32[16,384]{1,0:T(8,128)S(1)}, u32[]{:S(2)}, u32[]{:S(2)}) collective-permute-start(f32[16,384]{1,0:T(8,128)S(1)} %fusion), channel_id=1, source_target_pairs={{0,6},{1,7},{2,8},{3,9},{4,10},{5,11},{6,12},{7,13},{8,14},{9,15},... | collective-permute-start | bytes 73736
  1393.2 145.0 %collective-permute-start.4 = (f32[16,384]{1,0:T(8,128)S(1)}, f32[16,384]{1,0:T(8,128)S(1)}, u32[]{:S(2)}, u32[]{:S(2)}) collective-permute-start(f32[16,384]{1,0:T(8,128)S(1)} %fusion), channel_id=1, source_target_pairs={{0,5},{1,6},{2,7},{3,8},{4,9},{5,10},{6,11},{7,12},{8,13},{9,14},{... | collective-permute-start | bytes 73736
  1406.4 131.9 %collective-permute-start.3 = (f32[16,384]{1,0:T(8,128)S(1)}, f32[16,384]{1,0:T(8,128)S(1)}, u32[]{:S(2)}, u32[]{:S(2)}) collective-permute-start(f32[16,384]{1,0:T(8,128)S(1)} %fusion), channel_id=1, source_target_pairs={{0,4},{1,5},{2,6},{3,7},{4,8},{5,9},{6,10},{7,11},{8,12},{9,13},{1... | collective-permute-start | bytes 73736
  1419.5 118.7 %collective-permute-start.2 = (f32[16,384]{1,0:T(8,128)S(1)}, f32[16,384]{1,0:T(8,128)S(1)}, u32[]{:S(2)}, u32[]{:S(2)}) collective-permute-start(f32[16,384]{1,0:T(8,128)S(1)} %fusion), channel_id=1, source_target_pairs={{0,3},{1,4},{2,5},{3,6},{4,7},{5,8},{6,9},{7,10},{8,11},{9,12},{10... | collective-permute-start | bytes 73736
  1432.7 105.6 %collective-permute-start.1 = (f32[16,384]{1,0:T(8,128)S(1)}, f32[16,384]{1,0:T(8,128)S(1)}, u32[]{:S(2)}, u32[]{:S(2)}) collective-permute-start(f32[16,384]{1,0:T(8,128)S(1)} %fusion), channel_id=1, source_target_pairs={{0,2},{1,3},{2,4},{3,5},{4,6},{5,7},{6,8},{7,9},{8,10},{9,11},{10,... | collective-permute-start | bytes 73736
  1445.8 92.5 %collective-permute-start = (f32[16,384]{1,0:T(8,128)S(1)}, f32[16,384]{1,0:T(8,128)S(1)}, u32[]{:S(2)}, u32[]{:S(2)}) collective-permute-start(f32[16,384]{1,0:T(8,128)S(1)} %fusion), channel_id=1, source_target_pairs={{0,1},{1,2},{2,3},{3,4},{4,5},{5,6},{6,7},{7,8},{8,9},{9,10},{10,1... | collective-permute-start | bytes 73736
  (33 other events, 3582.3 us)
Sparse Core Ops, SparseCore 0:
  10.7 67.4 all-gather.4
  80.0 82.9 all-gather.2
  175.7 89.4 reduce-scatter.7
  269.4 103.9 reduce-scatter.11
  378.2 109.0 reduce-scatter.9
where the time goes:
time: 1580 us; the launch traced here: 1570 us
  blocking collectives  776 us (49%)
  starting transfers between devices  531 us (34%)
  waiting for transfers between devices  171 us (11%)
  matrix products  40.4 us (3%)
  local copies, waits for them, and re-layouts  36.8 us (2%)
    unnamed x2, blocking collectives  733 us
    unnamed x65, starting transfers between devices  531 us
    reduce_scatter x1, waiting for transfers between devices, on_device(): lax.psum_scatter(partial_value, 'mp', scatter_dimension=0, tiled=True)  69.6 us
    all_gather x1, waiting for transfers between devices, on_device(): full_encoder = lax.all_gather(encoder, 'dp', axis=0, tiled=True)  67.3 us
    all_gather x1, blocking collectives, on_device(): all_codes = lax.all_gather(code_rows, 'mp', axis=0, tiled=True)  42.7 us
    unnamed x63, local copies, waits for them, and re-layouts  36.8 us
    all_gather x1, waiting for transfers between devices, on_device(): upstream = lax.all_gather(cotangent, 'mp', axis=0, tiled=True)  31.9 us
  transfers between devices with their start and end apart: 69, of which 4 were waited for; matrix products, arithmetic and copies ran while one was open for 46% of the time, Pallas kernels for 0%

commit v1 on v0

v1 whole, which is shorter than its diff:
```python
import jax
import jax.numpy as jnp
from jax import lax
from jax.sharding import PartitionSpec as P

F32 = jnp.float32
BF16 = jnp.bfloat16


def gelu_parts(pre_act):
    cdf_part = 0.5 * (1.0 + lax.erf(pre_act * 0.7071067811865476))
    density = jnp.exp(-0.5 * pre_act * pre_act) * 0.3989422804014327
    return (pre_act * cdf_part, cdf_part + pre_act * density)


def on_device(tokens, gain, encoder, w_up, w_down, cotangent):
    rows = encoder.shape[0]
    own = rows // lax.axis_size("mp")
    dp_at = lax.axis_index("dp")
    mp_at = lax.axis_index("mp")
    full_encoder = lax.all_gather(encoder, "dp", axis=0, tiled=True)
    as_float = tokens.astype(F32)
    center = as_float - jnp.mean(as_float, axis=1, keepdims=True)
    inv_std = lax.rsqrt(jnp.mean(center * center, axis=1, keepdims=True) + 1e-06)
    unit = center * inv_std
    normed = (unit * gain).astype(BF16)
    code_rows = jnp.dot(normed, full_encoder, preferred_element_type=F32).astype(BF16)
    all_codes = lax.all_gather(code_rows, "mp", axis=0, tiled=True)
    tied_up = jnp.einsum("dc,df->cf", full_encoder, w_up, preferred_element_type=F32).astype(BF16)
    pre_act = jnp.dot(all_codes, tied_up, preferred_element_type=F32)
    gelu_val, gelu_slope = gelu_parts(pre_act)
    hidden = gelu_val.astype(BF16)
    upstream = lax.all_gather(cotangent, "mp", axis=0, tiled=True)
    d_hidden = jnp.dot(upstream, w_down, preferred_element_type=F32)
    d_act = (d_hidden * gelu_slope).astype(BF16)
    down_term = jnp.einsum("td,tf->df", upstream, hidden, preferred_element_type=F32)
    grad_down = lax.psum_scatter(
        down_term.astype(BF16), "dp", scatter_dimension=0, tiled=True
    ).astype(F32)
    codes_part = jnp.einsum("tf,cf->tc", d_act, tied_up, preferred_element_type=F32)
    grad_codes = lax.psum_scatter(codes_part, "mp", scatter_dimension=0, tiled=True).astype(BF16)
    inner = jnp.einsum("tc,tf->cf", all_codes, d_act, preferred_element_type=F32)
    inner = lax.psum(inner, "dp").astype(BF16)
    grad_up = jnp.dot(encoder, inner, preferred_element_type=F32)
    up_rows = lax.dynamic_slice_in_dim(w_up, dp_at * rows, rows, 0)
    decode_part = jnp.einsum("df,cf->dc", up_rows, inner, preferred_element_type=F32)
    unit_cols = lax.all_to_all(unit.astype(BF16), "dp", split_axis=1, concat_axis=0, tiled=True)
    codes_cols = lax.all_gather(grad_codes, "dp", axis=0, tiled=True)
    encode_part = jnp.einsum("td,tc->dc", unit_cols, codes_cols, preferred_element_type=F32)
    both = lax.psum_scatter(
        jnp.concatenate([encode_part, decode_part], axis=1), "mp", scatter_dimension=0, tiled=True
    )
    width = encoder.shape[1]
    own_encoder = lax.dynamic_slice_in_dim(encoder, mp_at * own, own, 0).astype(F32)
    own_gain = lax.dynamic_slice_in_dim(gain, dp_at * rows + mp_at * own, own, 0)
    grad_encoder = own_gain[:, None] * both[:, :width] + both[:, width:]
    grad_gain = jnp.sum(own_encoder * both[:, :width], axis=1)
    d_normed = jnp.einsum("tc,dc->td", grad_codes, full_encoder, preferred_element_type=F32)
    dx_hat = d_normed * gain
    mean_one = jnp.mean(dx_hat, axis=1, keepdims=True)
    mean_two = jnp.mean(dx_hat * unit, axis=1, keepdims=True)
    grad_tokens = (
        cotangent.astype(F32) + inv_std * (dx_hat - mean_one - unit * mean_two)
    ).astype(BF16)
    return (grad_tokens, grad_up, grad_down, grad_encoder, grad_gain)


def solution(mesh):
    placed = (
        P(("dp", "mp"), None),
        P(),
        P("dp", None),
        P(None, "mp"),
        P(None, "mp"),
        P(("dp", "mp"), None),
    )
    return jax.shard_map(
        on_device,
        mesh=mesh,
        in_specs=placed,
        out_specs=(
            P(("dp", "mp"), None),
            P("dp", "mp"),
            P("dp", "mp"),
            P(("dp", "mp"), None),
            P(("dp", "mp")),
        ),
        check_vma=False,
    )
```

time: 1580 us -> 598 us (0.38)
  blocking collectives: 776 us -> 158 us
  starting transfers between devices: 531 us -> 15.1 us
  waiting for transfers between devices: 171 us -> 357 us
  local copies, waits for them, and re-layouts: 36.8 us -> 12.9 us
    unnamed x2 -> x0, blocking collectives: 733 us -> none
    unnamed x65 -> x2, starting transfers between devices: 531 us -> 0.08 us
    unnamed x70 -> x7, waiting for transfers between devices: 1.9 us -> 257 us
    psum x0 -> x1, blocking collectives: none -> 88.9 us  [on_device(): inner = lax.psum(inner, 'dp').astype(BF16)]
    reduce_scatter x2 -> x1, waiting for transfers between devices: 69.6 us -> 0.02 us  [on_device(): lax.psum_scatter(codes_part, 'mp', scatter_dimension=0, tiled=True)]
    all_gather x0 -> x1, blocking collectives: none -> 26.3 us  [on_device(): codes_cols = lax.all_gather(grad_codes, 'dp', axis=0, tiled=True)]
    unnamed x63 -> x32, local copies, waits for them, and re-layouts: 36.8 us -> 10.8 us
  transfers between devices with their start and end apart: 69 -> 6, of which waited for: 4 -> 4; matrix products, arithmetic and copies ran while one was open for 46% -> 5% of each run, Pallas kernels for 0% -> 0%
where the time goes in v1:
time: 598 us; the launch traced here: 597 us
  waiting for transfers between devices  357 us (60%)
  blocking collectives  158 us (26%)
  matrix products  32.1 us (5%)
  starting transfers between devices  15.1 us (3%)
  between operations  14.6 us (2%)
  local copies, waits for them, and re-layouts  12.9 us (2%)
  other arithmetic  6.86 us (1%)
    unnamed x7, waiting for transfers between devices  257 us
    psum x1, blocking collectives, on_device(): inner = lax.psum(inner, 'dp').astype(BF16)  88.9 us
    all_gather x1, waiting for transfers between devices, on_device(): full_encoder = lax.all_gather(encoder, 'dp', axis=0, tiled=True)  67.3 us
    all_gather x1, blocking collectives, on_device(): all_codes = lax.all_gather(code_rows, 'mp', axis=0, tiled=True)  42.6 us
    all_gather x1, waiting for transfers between devices, on_device(): upstream = lax.all_gather(cotangent, 'mp', axis=0, tiled=True)  33.6 us
    all_gather x1, blocking collectives, on_device(): codes_cols = lax.all_gather(grad_codes, 'dp', axis=0, tiled=True)  26.3 us
    all_to_all x1, starting transfers between devices, on_device(): lax.all_to_all(unit.astype(BF16), 'dp', split_axis=1, concat_axis=0, tile...  14.9 us
  transfers between devices with their start and end apart: 6, of which 4 were waited for; matrix products, arithmetic and copies ran while one was open for 5% of the time, Pallas kernels for 0%

profile of v1, /device:TPU:2, one launch (start us, length us, event | category | flops | bytes accessed | tf_op | source)
XLA Modules:
  0.0 596.7 jit_solution(14437708161539697439)
XLA Ops:
  7.2 0.0 all-gather.5.cloned.1.call-start
  7.2 0.7 all-gather.5.cloned.1.call-update
  7.9 0.0 all-gather.3.cloned.1.call-start
  7.9 0.7 all-gather.3.cloned.1.call-update
  8.6 0.0 reduce-scatter.5.cloned.1.call-start
  8.7 1.1 convert_reduce_fusion
  9.8 1.2 fusion.19
  10.9 0.0 copy-start.9
  10.9 67.3 %all-gather.5.cloned.1.call-done = bf16[3072,384]{1,0:T(8,128)(2,1)} async-done(((bf16[192,384]{1,0:T(8,128)(2,1)}), bf16[3072,384]{1,0:T(8,128)(2,1)}) %all-gather.5.cloned.1.call-update) | async-done | bytes 2359312 | tf_op jit(solution)/shard_map/all_gather | solution.py:21
  78.2 0.0 copy-done.9
  78.2 2.4 convolution_convert_fusion.2
  80.6 42.6 %all_gather.14 = bf16[512,384]{1,0:T(8,128)(2,1)S(1)} all-gather(bf16[32,384]{1,0:T(8,128)(2,1)S(1)} %convolution_convert_fusion.2), channel_id=1, replica_groups=mesh['dp'=16,'mp'=16] {'mp'}, dimensions={0}, use_global_device_ids=true | all-gather | bytes 417792 | tf_op jit(solution)/shard_map/all_gather | solution.py:28
  123.3 0.0 copy-done
  123.3 4.4 convolution_convert_fusion.1
  127.6 1.7 fusion.30
  129.4 33.6 %all-gather.3.cloned.1.call-done = bf16[512,3072]{1,0:T(8,128)(2,1)} async-done(((bf16[32,3072]{1,0:T(8,128)(2,1)}), bf16[512,3072]{1,0:T(8,128)(2,1)}) %all-gather.3.cloned.1.call-update) | async-done | bytes 3145744 | tf_op jit(solution)/shard_map/all_gather | solution.py:33
  162.9 6.6 %fusion.6 = bf16[512,768]{1,0:T(8,128)(2,1)S(1)} fusion(f32[512,768]{1,0:T(8,128)} %fusion.30, bf16[512,3072]{1,0:T(8,128)(2,1)} %all-gather.3.cloned.1.call-done, bf16[3072,768]{1,0:T(8,128)(2,1)} %param.10), kind=kOutput, calls=%fused_computation.9 | convolution fusion | flops 2419851264 | bytes 10223616 | tf_op jit(solution)/shard_map/dot_general | solution.py:34
  169.5 0.0 copy-start.2
  169.5 0.9 copy-done.2
  170.4 1.5 fusion.31
  171.9 0.0 reduce-scatter.5.cloned.1.call-update
  171.9 0.0 copy-start.1
  171.9 0.0 copy-start.8
  171.9 2.7 fusion.32
  174.7 88.9 %all-reduce.5 = bf16[384,768]{1,0:T(8,128)(2,1)S(1)} all-reduce(f32[384,768]{1,0:T(8,128)} %fusion.32), channel_id=1, replica_groups=mesh['dp'=16,'mp'=16] {'dp'}, use_global_device_ids=true, to_apply=%region_5.0 | all-reduce | flops 294912 | bytes 1769472 | tf_op jit(solution)/shard_map/psum | solution.py:43
  263.6 0.0 reduce-scatter.5.cloned.1.call-done
  263.6 0.8 convert_element_type.51
  264.4 0.0 copy-done.1
  264.4 0.0 copy-done.8
  264.4 0.0 copy-start.6
  264.4 2.8 fusion.29
  267.2 0.0 copy-done.6
  267.2 1.3 all_to_all.14
  268.5 0.8 copy.14
  269.3 14.9 %all-to-all-start = ((bf16[32,16,192]{2,0,1:T(8,128)(2,1)}), bf16[32,16,192]{2,0,1:T(8,128)(2,1)}, u32[]{:S(2)}, u32[]{:S(2)}) async-start(bf16[32,16,192]{2,0,1:T(8,128)(2,1)} %copy.14), calls=%async_computation.1 | async-start | bytes 524288 | tf_op jit(solution)/shard_map/all_to_all | solution.py:47
  284.1 0.0 all-reduce.4.cloned.1.call-start
  284.2 1.3 fusion.20
  285.5 0.0 copy-done.7
  285.5 0.0 copy-start.3
  285.5 26.3 %all_gather.15 = bf16[512,384]{1,0:T(8,128)(2,1)S(1)} all-gather(bf16[32,384]{1,0:T(8,128)(2,1)S(1)} %copy-done.7), channel_id=1, replica_groups=mesh['dp'=16,'mp'=16] {'dp'}, dimensions={0}, use_global_device_ids=true | all-gather | bytes 417792 | tf_op jit(solution)/shard_map/all_gather | solution.py:48
  311.8 0.0 all-to-all-done
  311.8 1.2 fusion.33
  313.1 0.9 pad_maximum_fusion
  313.9 0.0 all-reduce.4.cloned.1.call-update
  313.9 0.0 reduce-scatter.7.cloned.1.call-start
  314.0 0.0 copy-done.3
  314.0 6.3 %fusion = bf16[3072,768]{0,1:T(8,128)(2,1)} fusion(bf16[512,3072]{1,0:T(8,128)(2,1)} %all-gather.3.cloned.1.call-done, f32[512,768]{1,0:T(8,128)S(1)} %copy-done.3), kind=kOutput, calls=%fused_computation.1 | convolution fusion | flops 2420244480 | bytes 9437184 | tf_op jit(solution)/shard_map/td,tf->df/dot_general | solution.py:36
  320.3 6.6 %copy.16 = bf16[3072,768]{1,0:T(8,128)(2,1)} copy(bf16[3072,768]{0,1:T(8,128)(2,1)} %fusion) | data formatting | bytes 9437184
  327.0 0.0 copy-start.4
  327.0 0.0 copy-start.10
  327.0 0.0 reduce-scatter.7.cloned.1.call-update
  327.0 0.1 dynamic_slice.9
  327.1 0.5 copy-done.13
  327.6 0.6 dynamic-slice
  328.9 0.0 copy-done.5
  328.9 1.1 convolution_bitcast_fusion
  330.0 0.0 copy-done.11
  330.0 0.0 copy-done.12
  330.0 0.9 fusion.18
  330.9 147.3 %all-reduce.4.cloned.1.call-done = f32[192,768]{1,0:T(8,128)} async-done(((f32[192,768]{1,0:T(8,128)}), f32[192,768]{1,0:T(8,128)}) %all-reduce.4.cloned.1.call-update) | async-done | bytes 589840
  478.2 2.1 multiply_reduce_fusion
  480.3 107.8 %reduce-scatter.7.cloned.1.call-done = bf16[192,768]{1,0:T(8,128)(2,1)} async-done(((bf16[3072,768]{1,0:T(8,128)(2,1)}), bf16[192,768]{1,0:T(8,128)(2,1)}) %reduce-scatter.7.cloned.1.call-update) | async-done | bytes 294928
  588.1 1.1 copy.17
  589.2 1.0 copy.15
  (11 shorter events, 0.0 us)
Async XLA Ops:
  7.2 71.0 %all-gather.5.cloned.1.call-start = ((), (), s32[]{:S(2)}) async-start(), calls=%async_computation.4 | async-start | bytes 2506752 | tf_op jit(solution)/shard_map/all_gather | solution.py:21
  7.9 155.0 %all-gather.3.cloned.1.call-start = ((), (), s32[]{:S(2)}) async-start(), calls=%async_computation.3 | async-start | bytes 3342336 | tf_op jit(solution)/shard_map/all_gather | solution.py:33
  8.6 254.9 %reduce-scatter.5.cloned.1.call-start = ((), (), s32[]{:S(2)}) async-start(), calls=%async_computation.5 | async-start | bytes 835584 | tf_op jit(solution)/shard_map/reduce_scatter | solution.py:41
  10.9 67.3 %copy-start.9 = (f32[32]{0:T(128)}, f32[32]{0:T(128)S(1)}, u32[]{:S(2)}) copy-start(f32[32]{0:T(128)S(1)} %add_rsqrt_fusion) | copy-start | bytes 388
  78.2 45.1 %copy-start = (bf16[3072,384]{1,0:T(8,128)(2,1)S(1)}, bf16[3072,384]{1,0:T(8,128)(2,1)}, u32[]{:S(2)}) copy-start(bf16[3072,384]{1,0:T(8,128)(2,1)} %all-gather.5.cloned.1.call-done) | copy-start | bytes 7077892
  169.5 0.9 copy-start.2
  171.9 92.5 %copy-start.1 = (bf16[32,3072]{1,0:T(8,128)(2,1)S(1)}, bf16[32,3072]{1,0:T(8,128)(2,1)}, u32[]{:S(2)}) copy-start(bf16[32,3072]{1,0:T(8,128)(2,1)} %param.6) | copy-start | bytes 589828
  171.9 92.5 %copy-start.8 = (f32[3072]{0:T(1024)S(1)}, f32[3072]{0:T(1024)}, u32[]{:S(2)}) copy-start(f32[3072]{0:T(1024)} %param.7) | copy-start | bytes 36868
  264.4 2.8 copy-start.6
  267.2 18.3 %copy-start.7 = (bf16[32,384]{1,0:T(8,128)(2,1)S(1)}, bf16[32,384]{1,0:T(8,128)(2,1)}, u32[]{:S(2)}) copy-start(bf16[32,384]{1,0:T(8,128)(2,1)} %copy-done.6) | copy-start | bytes 73732
  269.3 42.6 %all-to-all-start = ((bf16[32,16,192]{2,0,1:T(8,128)(2,1)}), bf16[32,16,192]{2,0,1:T(8,128)(2,1)}, u32[]{:S(2)}, u32[]{:S(2)}) async-start(bf16[32,16,192]{2,0,1:T(8,128)(2,1)} %copy.14), calls=%async_computation.1 | async-start | bytes 524288 | tf_op jit(solution)/shard_map/all_to_all | solution.py:47
  284.1 194.1 %all-reduce.4.cloned.1.call-start = ((), (), s32[]{:S(2)}) async-start(), calls=%async_computation.7 | async-start | bytes 1179648
  285.5 28.5 %copy-start.3 = (f32[512,768]{1,0:T(8,128)S(1)}, f32[512,768]{1,0:T(8,128)}, u32[]{:S(2)}) copy-start(f32[512,768]{1,0:T(8,128)} %fusion.30) | copy-start | bytes 4718596
  313.9 274.1 %reduce-scatter.7.cloned.1.call-start = ((), (), s32[]{:S(2)}) async-start(), calls=%async_computation.6 | async-start | bytes 5013504
  326.9 0.7 copy-start.13
  326.9 1.9 copy-start.5
  326.9 3.1 copy-start.11
  327.0 3.1 copy-start.12
  327.0 3.1 copy-start.4
  327.0 3.1 copy-start.10
Sparse Core Ops, SparseCore 0:
  10.7 67.4 all-gather.4
  80.0 82.8 all-gather.2
  172.0 82.9 reduce-scatter.4
  314.1 164.0 all-reduce.3
  482.4 105.6 reduce-scatter.6

commit v2 on v1

v2 whole, which is shorter than its diff:
```python
import jax
import jax.numpy as jnp
from jax import lax
from jax.experimental import pallas as pl
from jax.experimental.pallas import tpu as pltpu
from jax.sharding import PartitionSpec as P

F32 = jnp.float32
BF16 = jnp.bfloat16


def step_core(i):
    return i ^ 1


def step_far(i):
    return i ^ 8


def step_x(k):
    return lambda i: (i & 9) | ((((i >> 1) + k) & 3) << 1)


def step_y(k):
    return lambda i: (i & 12) | ((i + k) & 3)


def step_z(k):
    return lambda i: ((((i >> 2) + k) & 3) << 2) | (i & 3)


def send(value, axis, target):
    return lax.ppermute(value, axis, [(i, target(i)) for i in range(16)])


def gather_parts(value, axis, step):
    return [value] + [send(value, axis, step(-k)) for k in (1, 2, 3)]


def in_order(parts, at):
    n = len(parts)
    twice = jnp.stack(parts + parts[:-1])
    return lax.dynamic_slice_in_dim(twice, (n - at) % n, n, 0)


def pair_in_order(mine, other, at):
    first = jnp.where(at == 0, mine, other)
    second = jnp.where(at == 0, other, mine)
    return first, second


def pick(value, at, axis):
    return lax.dynamic_index_in_dim(value, at, axis, keepdims=False)


def gelu_parts(pre_act):
    cdf_part = 0.5 * (1.0 + lax.erf(pre_act * 0.7071067811865476))
    density = jnp.exp(-0.5 * pre_act * pre_act) * 0.3989422804014327
    return (pre_act * cdf_part, cdf_part + pre_act * density)


def add(a, b):
    return a.astype(F32) + b.astype(F32)


def join_encoder(along, across, core):
    full = jnp.stack(pair_in_order(along, across, core), axis=2)
    return full.transpose(1, 0, 2, 3, 4).reshape(-1, along.shape[-1])


def gather_codes(code_rows):
    count, width = code_rows.shape
    return lax.all_to_all(
        jnp.broadcast_to(code_rows, (16, count, width)), "mp", split_axis=0, concat_axis=0
    )


def scatter_codes(part):
    got = lax.all_to_all(part, "mp", split_axis=0, concat_axis=0)
    return jnp.sum(got.astype(F32), axis=0)


STEPS = 6
VMEM = 20 * 1024 * 1024


def hidden_kernel(
    at, codes, tied, w_down, p0, p1, p2, p3, p4, hidden, codes_part, inner, rows, slope, total
):
    step = pl.program_id(0)
    z, y, core, x = at[0], at[1], at[2], at[3]
    count = codes.shape[1]

    def block(k):
        return ((z + k % 4) % 4) * 4 + (y + k // 4) % 4

    @pl.when(step == 0)
    def _():
        for k in range(16):
            rows[k * count : (k + 1) * count, :] = codes[block(k)]
        pre_act = jnp.dot(rows[...], tied[...], preferred_element_type=F32)
        value, grade = gelu_parts(pre_act)
        hidden[...] = value.astype(BF16)
        slope[...] = grade
        total[...] = jnp.zeros_like(total)

    part = jnp.concatenate([p0[...], p1[...], p2[...], p3[...], p4[...]], axis=0)
    total[...] += jnp.dot(part, w_down[...], preferred_element_type=F32)

    @pl.when(step == STEPS - 1)
    def _():
        d_act = (total[...] * slope[...]).astype(BF16)
        back = lax.dot_general(
            d_act, tied[...], (((1,), (1,)), ((), ())), preferred_element_type=F32
        ).astype(BF16)
        for k in range(16):
            codes_part[block(k)] = back[k * count : (k + 1) * count, :]
        outer = lax.dot_general(
            rows[...], d_act, (((0,), (0,)), ((), ())), preferred_element_type=F32
        ).astype(BF16)
        piece = outer.shape[0] // 8
        for k in range(8):
            to_core = (k // 4 + core) % 2
            inner[to_core, (k % 4 + 4 - x) % 4] = outer[k * piece : (k + 1) * piece, :]


def hidden_call(at, codes, tied, w_down, pieces):
    features, units = w_down.shape
    tokens = sum(p.shape[0] for p in pieces)
    width = tied.shape[0]
    span = features // STEPS
    whole = lambda shape: pl.BlockSpec(shape, lambda i, at: (0,) * len(shape))
    out = [
        jax.ShapeDtypeStruct((tokens, units), BF16),
        jax.ShapeDtypeStruct(codes.shape, BF16),
        jax.ShapeDtypeStruct((2, 4, width // 8, units), BF16),
    ]
    return pl.pallas_call(
        hidden_kernel,
        grid_spec=pltpu.PrefetchScalarGridSpec(
            num_scalar_prefetch=1,
            grid=(STEPS,),
            in_specs=[
                whole(codes.shape),
                whole(tied.shape),
                pl.BlockSpec((span, units), lambda i, at: (i, 0)),
            ]
            + [pl.BlockSpec((p.shape[0], span), lambda i, at: (0, i)) for p in pieces],
            out_specs=[whole(o.shape) for o in out],
            scratch_shapes=[
                pltpu.VMEM((tokens, width), BF16),
                pltpu.VMEM((tokens, units), F32),
                pltpu.VMEM((tokens, units), F32),
            ],
        ),
        out_shape=out,
        compiler_params=pltpu.CompilerParams(vmem_limit_bytes=VMEM),
        cost_estimate=pl.CostEstimate(
            flops=2 * tokens * units * (features + 3 * width),
            bytes_accessed=2 * (features * units + tokens * features),
            transcendentals=2 * tokens * units,
        ),
    )(at, codes, tied, w_down, *pieces)


def term_kernel(at, hidden, p0, p1, p2, p3, p4, keep, give):
    part = jnp.concatenate([p0[...], p1[...], p2[...], p3[...], p4[...]], axis=0)
    term = lax.dot_general(
        part, hidden[...], (((0,), (0,)), ((), ())), preferred_element_type=F32
    ).astype(BF16)
    half = term.shape[0] // 2
    first, second = term[:half], term[half:]

    @pl.when(at[2] == 0)
    def _():
        keep[0, 0] = first
        give[0, 0] = second

    @pl.when(at[2] != 0)
    def _():
        keep[0, 0] = second
        give[0, 0] = first


def term_call(at, hidden, pieces):
    tokens, units = hidden.shape
    features = pieces[0].shape[1]
    span = features // 8

    def place(i, at):
        return ((i % 4 + 4 - at[3]) % 4, (i // 4 + at[4]) % 2, 0, 0)

    out = [jax.ShapeDtypeStruct((4, 2, span // 2, units), BF16)] * 2
    return pl.pallas_call(
        term_kernel,
        grid_spec=pltpu.PrefetchScalarGridSpec(
            num_scalar_prefetch=1,
            grid=(8,),
            in_specs=[pl.BlockSpec((tokens, units), lambda i, at: (0, 0))]
            + [pl.BlockSpec((p.shape[0], span), lambda i, at: (0, i)) for p in pieces],
            out_specs=[pl.BlockSpec((1, 1, span // 2, units), place)] * 2,
        ),
        out_shape=out,
        compiler_params=pltpu.CompilerParams(vmem_limit_bytes=VMEM),
        cost_estimate=pl.CostEstimate(
            flops=2 * tokens * units * features,
            bytes_accessed=2 * (features * units + tokens * features),
            transcendentals=0,
        ),
    )(at, hidden, *pieces)


def on_device(tokens, gain, encoder, w_up, w_down, cotangent):
    rows, width = encoder.shape
    own = rows // 16
    dp_at = lax.axis_index("dp")
    mp_at = lax.axis_index("mp")
    core, x, far = dp_at % 2, (dp_at // 2) % 4, dp_at // 8

    z, y = mp_at // 4, mp_at % 4
    tie = lax.optimization_barrier

    other = send(encoder, "dp", step_far)
    as_float = tokens.astype(F32)
    center = as_float - jnp.mean(as_float, axis=1, keepdims=True)
    inv_std = lax.rsqrt(jnp.mean(center * center, axis=1, keepdims=True) + 1e-06)
    unit = center * inv_std
    normed = (unit * gain).astype(BF16)
    other, normed, late_cotangent = tie((other, normed, cotangent))
    parts = gather_parts(jnp.stack(pair_in_order(encoder, other, far)), "dp", step_x)
    line = gather_parts(late_cotangent, "mp", step_z)
    *parts, line = tie((*parts, jnp.concatenate(line)))
    along = in_order(parts, x)
    across = send(along, "dp", step_core)
    after = send(line, "mp", step_y(-1))
    before = send(line, "mp", step_y(1))
    full_encoder = join_encoder(along, across, core)
    code_rows = jnp.dot(normed, full_encoder, preferred_element_type=F32).astype(BF16)
    all_codes = gather_codes(code_rows)
    after, before, _ = tie((after, before, code_rows))
    half = line.shape[0] // 2
    far_a = send(after[:half], "mp", step_y(-1))
    far_b = send(before[half:], "mp", step_y(1))
    tied_up = jnp.einsum("dc,df->cf", full_encoder, w_up, preferred_element_type=F32).astype(BF16)
    all_codes, late_normed = tie((all_codes, normed))
    normed_cols = lax.all_to_all(late_normed, "dp", split_axis=1, concat_axis=0, tiled=True)
    all_codes, tied_up, normed_cols, far_a, far_b = tie(
        (all_codes, tied_up, normed_cols, far_a, far_b)
    )
    at = jnp.stack([z, y, core, x, far]).astype(jnp.int32)
    pieces = (line, after, far_a, far_b, before)
    hidden, codes_part, inner = hidden_call(at, all_codes, tied_up, w_down, pieces)
    grad_codes = scatter_codes(codes_part).astype(BF16)
    keep, give = term_call(at, hidden, pieces)
    term = add(keep, send(give, "dp", step_core)).astype(BF16)
    inner = add(inner[0], send(inner[1], "dp", step_core)).astype(BF16)
    term, inner = tie((term, inner))
    got_a = send(term[2, 0], "dp", step_x(1))
    got_b = send(term[2, 1], "dp", step_x(-1))
    got = [send(inner[k], "dp", step_x(k)) for k in (1, 2, 3)]
    inner = (inner[0].astype(F32) + sum(g.astype(F32) for g in got)).astype(BF16)
    got_a, got_b, inner, grad_codes = tie((got_a, got_b, inner, grad_codes))
    up = jnp.stack([add(term[1, 0], got_a).astype(BF16), term[1, 1]])
    down = jnp.stack([term[3, 0], add(term[3, 1], got_b).astype(BF16)])
    count, cols = inner.shape
    mine = jnp.concatenate([inner, grad_codes.reshape(-1, cols)])
    up, down, mine = tie((up, down, mine))
    other = send(mine, "dp", step_far)
    up = send(up, "dp", step_x(1))
    down = send(down, "dp", step_x(-1))
    inner = add(inner, other[:count]).astype(BF16)
    mine = jnp.concatenate([inner, *pair_in_order(mine[count:], other[count:], far)])
    parts = gather_parts(mine, "dp", step_x)
    up, down, *parts = tie((up, down, *parts))
    total = [term[0, k].astype(F32) + up[k].astype(F32) + down[k].astype(F32) for k in (0, 1)]
    grad_down = total[0] + send(total[1].astype(BF16), "dp", step_far).astype(F32)
    mine = in_order(parts, x)
    both = jnp.stack(pair_in_order(mine, send(mine, "dp", step_core), core))
    inner = both[:, :, :count].reshape(-1, cols)
    codes_cols = both[:, :, count:].reshape(-1, width)
    up_rows = lax.dynamic_slice_in_dim(w_up, dp_at * rows, rows, 0)
    decode_part = jnp.einsum("df,cf->dc", up_rows, inner, preferred_element_type=F32)
    count = tokens.shape[0]
    normed_cols = normed_cols.reshape(2, 4, 2, count, rows).transpose(2, 1, 0, 3, 4)
    normed_cols = normed_cols.reshape(16 * count, rows)
    encode_part = jnp.einsum("td,tc->dc", normed_cols, codes_cols, preferred_element_type=F32)
    both = jnp.concatenate([encode_part, decode_part], axis=1).astype(BF16)
    both = lax.all_to_all(both.reshape(16, own, 2 * width), "mp", split_axis=0, concat_axis=0)
    both = jnp.sum(both.astype(F32), axis=0)
    grad_up = jnp.dot(encoder, inner, preferred_element_type=F32)
    own_encoder = lax.dynamic_slice_in_dim(encoder, mp_at * own, own, 0).astype(F32)
    own_gain = lax.dynamic_slice_in_dim(gain, dp_at * rows + mp_at * own, own, 0)
    grad_encoder = both[:, :width] + both[:, width:]
    grad_gain = jnp.sum(own_encoder * both[:, :width], axis=1) / own_gain
    d_normed = jnp.einsum("tc,dc->td", grad_codes, full_encoder, preferred_element_type=F32)
    dx_hat = d_normed * gain
    mean_one = jnp.mean(dx_hat, axis=1, keepdims=True)
    mean_two = jnp.mean(dx_hat * unit, axis=1, keepdims=True)
    grad_tokens = (
        cotangent.astype(F32) + inv_std * (dx_hat - mean_one - unit * mean_two)
    ).astype(BF16)
    return (grad_tokens, grad_up, grad_down, grad_encoder, grad_gain)


def solution(mesh):
    placed = (
        P(("dp", "mp"), None),
        P(),
        P("dp", None),
        P(None, "mp"),
        P(None, "mp"),
        P(("dp", "mp"), None),
    )
    return jax.shard_map(
        on_device,
        mesh=mesh,
        in_specs=placed,
        out_specs=(
            P(("dp", "mp"), None),
            P("dp", "mp"),
            P("dp", "mp"),
            P(("dp", "mp"), None),
            P(("dp", "mp")),
        ),
        check_vma=False,
    )
```

time: 598 us -> 201 us (0.34)
  waiting for transfers between devices: 357 us -> 55.3 us
  blocking collectives: 158 us -> 0 us
  starting transfers between devices: 15.1 us -> 77.4 us
  matrix products: 32.1 us -> 11.6 us
  Pallas kernels: 0 us -> 16.3 us
  other arithmetic: 6.86 us -> 21.3 us
  between operations: 14.6 us -> 1.24 us
    unnamed x7 -> x0, waiting for transfers between devices: 257 us -> none
    all_gather x2 -> x0, waiting for transfers between devices: 101 us -> none  [the longest x1 67.3 us: on_device(): full_encoder = lax.all_gather(encoder, 'dp', axis=0, tiled=True)]
    psum x1 -> x0, blocking collectives: 88.9 us -> none  [on_device(): inner = lax.psum(inner, 'dp').astype(BF16)]
    all_gather x2 -> x0, blocking collectives: 68.9 us -> none  [the longest x1 42.6 us: on_device(): all_codes = lax.all_gather(code_rows, 'mp', axis=0, tiled=True)]
    ppermute x0 -> x27, starting transfers between devices: none -> 45.5 us  [send(): return lax.ppermute(value, axis, [(i, target(i)) for i in range(16)])]
    ppermute x0 -> x27, waiting for transfers between devices: none -> 38.2 us  [send(): return lax.ppermute(value, axis, [(i, target(i)) for i in range(16)])]
    dot_general x6 -> x1, matrix products: 20.1 us -> 0.26 us  [on_device(): jnp.einsum('td,tc->dc', normed_cols, codes_cols, preferred_element_type=F32)]
    all_to_all x1 -> x4, waiting for transfers between devices: 0.01 us -> 17 us  [the longest x1 11.8 us: on_device(): lax.all_to_all(both.reshape(16, own, 2 * width), 'mp', split_axis=0, conc...]
  transfers between devices with their start and end apart: 6 -> 31, of which waited for: 4 -> 16; matrix products, arithmetic and copies ran while one was open for 5% -> 19% of each run, Pallas kernels for 0% -> 0%
where the time goes in v2:
time: 201 us; the launch traced here: 199 us
  starting transfers between devices  77.4 us (39%)
  waiting for transfers between devices  55.3 us (28%)
  other arithmetic  21.3 us (11%)
  Pallas kernels  16.3 us (8%)
  local copies, waits for them, and re-layouts  15.9 us (8%)
  matrix products  11.6 us (6%)
    ppermute x27, starting transfers between devices, send(): return lax.ppermute(value, axis, [(i, target(i)) for i in range(16)])  45.5 us
    ppermute x27, waiting for transfers between devices, send(): return lax.ppermute(value, axis, [(i, target(i)) for i in range(16)])  38.2 us
    all_to_all x1, waiting for transfers between devices, on_device(): lax.all_to_all(both.reshape(16, own, 2 * width), 'mp', split_axis=0, conc...  11.8 us
    all_to_all x1, starting transfers between devices, on_device(): lax.all_to_all(late_normed, 'dp', split_axis=1, concat_axis=0, tiled=True)  9.89 us
    pallas_call x1, Pallas kernels, hidden_call(): pl.pallas_call(hidden_kernel, grid_spec=pltpu.PrefetchScalarGridSpec(num_...  8.33 us
    pallas_call x1, Pallas kernels, term_call(): pl.pallas_call(term_kernel, grid_spec=pltpu.PrefetchScalarGridSpec(num_sc...  8.01 us
    all_to_all x1, starting transfers between devices, gather_codes(): lax.all_to_all(jnp.broadcast_to(code_rows, (16, count, width)), 'mp', spl...  7.86 us
    all_to_all x1, starting transfers between devices, scatter_codes(): got = lax.all_to_all(part, 'mp', split_axis=0, concat_axis=0)  7.13 us
  transfers between devices with their start and end apart: 31, of which 16 were waited for; matrix products, arithmetic and copies ran while one was open for 19% of the time, Pallas kernels for 0%

profile of v2, /device:TPU:2, one launch (start us, length us, event | category | flops | bytes accessed | tf_op | source)
XLA Modules:
  0.0 198.9 jit_solution(2449923783157303930)
XLA Ops:
  0.6 7.3 %collective-permute-start = (bf16[192,384]{1,0:T(8,128)(2,1)}, bf16[192,384]{1,0:T(8,128)(2,1)S(1)}, u32[]{:S(2)}, u32[]{:S(2)}) collective-permute-start(bf16[192,384]{1,0:T(8,128)(2,1)} %param.8), channel_id=1, source_target_pairs={{0,128},{16,144},{32,160},{48,176},{64,192},{80,208},{96,224},{112... | collective-permute-start | bytes 442376 | tf_op jit(solution)/shard_map/ppermute | solution.py:33
  7.9 1.1 convert_reduce_fusion.1
  9.0 1.2 fusion.17
  10.2 1.1 fusion.11
  11.3 0.8 collective-permute-done
  12.1 5.0 %collective-permute-start.4 = (bf16[32,3072]{1,0:T(8,128)(2,1)}, bf16[32,3072]{1,0:T(8,128)(2,1)S(1)}, u32[]{:S(2)}, u32[]{:S(2)}) collective-permute-start(bf16[32,3072]{1,0:T(8,128)(2,1)} %param.11), channel_id=1, source_target_pairs={{0,12},{1,13},{2,14},{3,15},{4,0},{5,1},{6,2},{7,3},{8,4},{9,5},{1... | collective-permute-start | bytes 589832 | tf_op jit(solution)/shard_map/ppermute | solution.py:33
  17.7 1.4 collective-permute-start.6
  19.0 0.9 select_bitcast_fusion.5
  20.6 2.4 %collective-permute-start.2 = (bf16[2,192,384]{2,1,0:T(8,128)(2,1)S(1)}, bf16[2,192,384]{2,1,0:T(8,128)(2,1)S(1)}, u32[]{:S(2)}, u32[]{:S(2)}) collective-permute-start(bf16[2,192,384]{2,1,0:T(8,128)(2,1)S(1)} %pad_maximum_fusion.5), channel_id=1, source_target_pairs={{0,64},{16,80},{32,96},{48,112},{64,0},{80,16},{96,32},{112,48},{1... | collective-permute-start | bytes 884744 | tf_op jit(solution)/shard_map/ppermute | solution.py:33
  23.1 1.8 collective-permute-start.3
  24.9 9.6 %collective-permute-done.5 = bf16[32,3072]{1,0:T(8,128)(2,1)S(1)} collective-permute-done((bf16[32,3072]{1,0:T(8,128)(2,1)}, bf16[32,3072]{1,0:T(8,128)(2,1)S(1)}, u32[]{:S(2)}, u32[]{:S(2)}) %collective-permute-start.5) | collective-permute-done | bytes 196640 | tf_op jit(solution)/shard_map/ppermute | solution.py:33
  34.6 0.9 collective-permute-done.3
  35.9 1.3 copy-done.7
  37.3 1.1 constant_dynamic-slice_fusion.2
  38.4 3.0 %collective-permute-start.8 = (bf16[128,3072]{1,0:T(8,128)(2,1)S(1)}, bf16[128,3072]{1,0:T(8,128)(2,1)S(1)}, u32[]{:S(2)}, u32[]{:S(2)}) collective-permute-start(bf16[128,3072]{1,0:T(8,128)(2,1)S(1)} %pad_maximum_fusion.1.p0), channel_id=1, source_target_pairs={{0,3},{1,0},{2,1},{3,2},{4,7},{5,4},{6,5},{7,6},{8,11},{9,8},{10,9... | collective-permute-start | bytes 2359304 | tf_op jit(solution)/shard_map/ppermute | solution.py:33
  41.6 1.8 select_bitcast_fusion.1
  43.5 1.7 pad_maximum_fusion
  45.2 2.1 %convolution_convert_fusion.3 = bf16[32,384]{1,0:T(8,128)(2,1)S(1)} fusion(bf16[32,3072]{1,0:T(8,128)(2,1)S(1)} %fusion.11, bf16[3072,384]{1,0:T(8,128)(2,1)} %bitcast.20), kind=kOutput, calls=%fused_computation.9 | convolution fusion | flops 75509760 | bytes 2580480 | tf_op jit(solution)/shard_map/dot_general | solution.py:238
  47.3 0.8 broadcast_in_dim.2
  48.0 7.9 %all-to-all-start = ((bf16[16,32,384]{2,1,0:T(8,128)(2,1)}), bf16[16,32,384]{2,1,0:T(8,128)(2,1)S(1)}, u32[]{:S(2)}, u32[]{:S(2)}) async-start(bf16[16,32,384]{2,1,0:T(8,128)(2,1)} %broadcast_in_dim.2), calls=%async_computation | async-start | bytes 786432 | tf_op jit(solution)/shard_map/all_to_all | solution.py:73
  56.0 4.5 %collective-permute-done.8.p1 = bf16[128,3072]{1,0:T(8,128)(2,1)S(1)} collective-permute-done((bf16[128,3072]{1,0:T(8,128)(2,1)S(1)}, bf16[128,3072]{1,0:T(8,128)(2,1)S(1)}, u32[]{:S(2)}, u32[]{:S(2)}) %collective-permute-start.8) | collective-permute-done | bytes 786464 | tf_op jit(solution)/shard_map/ppermute | solution.py:33
  60.5 4.5 %collective-permute-done.9.p4 = bf16[128,3072]{1,0:T(8,128)(2,1)S(1)} collective-permute-done((bf16[128,3072]{1,0:T(8,128)(2,1)S(1)}, bf16[128,3072]{1,0:T(8,128)(2,1)S(1)}, u32[]{:S(2)}, u32[]{:S(2)}) %collective-permute-start.9) | collective-permute-done | bytes 786464 | tf_op jit(solution)/shard_map/ppermute | solution.py:33
  65.1 0.8 slice.82
  66.7 2.0 %collective-permute-start.11 = (bf16[64,3072]{1,0:T(8,128)(2,1)}, bf16[64,3072]{1,0:T(8,128)(2,1)}, u32[]{:S(2)}, u32[]{:S(2)}) collective-permute-start(bf16[64,3072]{1,0:T(8,128)(2,1)} %slice.83), channel_id=1, source_target_pairs={{0,1},{1,2},{2,3},{3,0},{4,5},{5,6},{6,7},{7,4},{8,9},{9,10},{10,1... | collective-permute-start | bytes 1179656 | tf_op jit(solution)/shard_map/ppermute | solution.py:33
  69.7 0.8 copy.28
  70.4 9.9 %all-to-all-start.1 = ((bf16[32,16,192]{2,0,1:T(8,128)(2,1)}), bf16[32,16,192]{2,0,1:T(8,128)(2,1)}, u32[]{:S(2)}, u32[]{:S(2)}) async-start(bf16[32,16,192]{2,0,1:T(8,128)(2,1)} %copy.28), calls=%async_computation.1 | async-start | bytes 524288 | tf_op jit(solution)/shard_map/all_to_all | solution.py:246
  80.3 5.1 %convolution_convert_fusion.tied = bf16[384,768]{1,0:T(8,128)(2,1)S(1)} fusion(bf16[3072,384]{1,0:T(8,128)(2,1)} %bitcast.20, bf16[3072,768]{1,0:T(8,128)(2,1)} %param.9), kind=kOutput, calls=%fused_computation.3 | convolution fusion | flops 1812234240 | bytes 7667712 | tf_op jit(solution)/shard_map/dc,df->cf/dot_general | solution.py:244
  85.4 4.5 %all-to-all-done.1 = bf16[32,16,192]{2,0,1:T(8,128)(2,1)} async-done(((bf16[32,16,192]{2,0,1:T(8,128)(2,1)}), bf16[32,16,192]{2,0,1:T(8,128)(2,1)}, u32[]{:S(2)}, u32[]{:S(2)}) %all-to-all-start.1) | async-done | bytes 196640 | tf_op jit(solution)/shard_map/all_to_all | solution.py:246
  90.0 2.3 %copy-done.5 = bf16[3072,768]{1,0:T(8,128)(2,1)S(1)} copy-done((bf16[3072,768]{1,0:T(8,128)(2,1)S(1)}, bf16[3072,768]{1,0:T(8,128)(2,1)}, u32[]{:S(2)}) %copy-start.5) | copy-done | bytes 4718616
  92.3 8.3 %shard_map.101 = (bf16[512,768]{1,0:T(8,128)(2,1)S(1)}, bf16[16,32,384]{2,1,0:T(8,128)(2,1)}, bf16[2,4,48,768]{3,2,1,0:T(8,128)(2,1)S(1)}) custom-call(s32[5]{0:T(128)S(1)} %stack.98.at, bf16[16,32,384]{2,1,0:T(8,128)(2,1)S(1)} %all-to-all-done.codes, bf16[384,768]{1,0:T(8,128)(2,1)S(1)} %convolution_convert_fusion.tied, bf16[3072,768]{1,0:T(8,128)(2,1)S(1)} %copy-done.5, ...), custom_call_target="tpu_custom_call" | custom-call | flops 3321888768 | bytes 7864320 | tf_op jit(solution)/shard_map/pallas_call | solution.py:138
  100.6 1.3 copy-done.2
  102.0 1.1 copy-done.4
  103.1 8.0 %shard_map.102 = (bf16[4,2,192,768]{3,2,1,0:T(8,128)(2,1)S(1)}, bf16[4,2,192,768]{3,2,1,0:T(8,128)(2,1)}) custom-call(s32[5]{0:T(128)S(1)} %stack.98.at, bf16[512,768]{1,0:T(8,128)(2,1)S(1)} %get-tuple-element.58.hidden, bf16[128,3072]{1,0:T(8,128)(2,1)S(1)} %pad_maximum_fusion.1.p0, bf16[128,3072]{1,0:T(8,128)(2,1)S(1)} %copy-done.2, ...), custom_call_target="tpu_custom_call" | custom-call | flops 2415919104 | bytes 7864320 | tf_op jit(solution)/shard_map/pallas_call | solution.py:194
  111.9 7.1 %all-to-all-start.2 = ((bf16[16,32,384]{2,1,0:T(8,128)(2,1)}), bf16[16,32,384]{2,1,0:T(8,128)(2,1)S(1)}, u32[]{:S(2)}, u32[]{:S(2)}) async-start(bf16[16,32,384]{2,1,0:T(8,128)(2,1)} %get-tuple-element.64), calls=%async_computation.2 | async-start | bytes 786432 | tf_op jit(solution)/shard_map/all_to_all | solution.py:79
  119.1 1.0 fusion.5
  120.1 3.7 %add_convert_fusion = bf16[4,2,192,768]{3,2,1,0:T(8,128)(2,1)} fusion(bf16[4,2,192,768]{3,2,1,0:T(8,128)(2,1)} %collective-permute-done.12, bf16[4,2,192,768]{3,2,1,0:T(8,128)(2,1)S(1)} %get-tuple-element.59), kind=kLoop, calls=%fused_computation | loop fusion | flops 4718592 | bytes 7077888 | tf_op jit(solution)/shard_map/convert_element_type | solution.py:255
  123.8 0.9 collective-permute-start.16
  124.7 3.4 %collective-permute-start.17 = (bf16[48,768]{1,0:T(8,128)(2,1)S(1)}, bf16[48,768]{1,0:T(8,128)(2,1)S(1)}, u32[]{:S(2)}, u32[]{:S(2)}) collective-permute-start(bf16[48,768]{1,0:T(8,128)(2,1)S(1)} %get-tuple-element.93), channel_id=1, source_target_pairs={{0,64},{16,80},{32,96},{48,112},{64,0},{80,16},{96,32},{112,48},{1... | collective-permute-start | bytes 221192 | tf_op jit(solution)/shard_map/ppermute | solution.py:33
  128.1 0.8 collective-permute-start.18
  128.9 1.3 slice_bitcast_fusion
  130.2 1.3 collective-permute-start.14
  131.5 0.8 collective-permute-start.15
  132.5 5.7 %collective-permute-done.14 = bf16[192,768]{1,0:T(8,128)(2,1)S(1)} collective-permute-done((bf16[192,768]{1,0:T(8,128)(2,1)S(1)}, bf16[192,768]{1,0:T(8,128)(2,1)S(1)}, u32[]{:S(2)}, u32[]{:S(2)}) %collective-permute-start.14) | collective-permute-done | bytes 294944 | tf_op jit(solution)/shard_map/ppermute | solution.py:33
  138.2 0.9 collective-permute-done.15
  139.1 1.2 fusion.19
  140.3 1.1 pad_maximum_fusion.2
  142.4 1.7 collective-permute-start.20
  144.1 6.0 %collective-permute-done.21 = bf16[64,768]{1,0:T(8,128)(2,1)S(1)} collective-permute-done((bf16[64,768]{1,0:T(8,128)(2,1)S(1)}, bf16[64,768]{1,0:T(8,128)(2,1)S(1)}, u32[]{:S(2)}, u32[]{:S(2)}) %collective-permute-start.21) | collective-permute-done | bytes 98336 | tf_op jit(solution)/shard_map/ppermute | solution.py:33
  150.1 1.0 collective-permute-start.22
  151.1 1.9 collective-permute-start.23
  153.0 2.5 %collective-permute-start.24 = (bf16[80,768]{1,0:T(8,128)(2,1)S(1)}, bf16[80,768]{1,0:T(8,128)(2,1)S(1)}, u32[]{:S(2)}, u32[]{:S(2)}) collective-permute-start(bf16[80,768]{1,0:T(8,128)(2,1)S(1)} %pad_maximum_fusion.7), channel_id=1, source_target_pairs={{0,32},{16,48},{32,64},{48,80},{64,96},{80,112},{96,0},{112,16},{1... | collective-permute-start | bytes 368648 | tf_op jit(solution)/shard_map/ppermute | solution.py:33
  155.5 1.0 constant_dynamic-slice_fusion
  156.6 1.0 copy.29
  157.8 2.6 %collective-permute-done.22 = bf16[80,768]{1,0:T(8,128)(2,1)S(1)} collective-permute-done((bf16[80,768]{1,0:T(8,128)(2,1)S(1)}, bf16[80,768]{1,0:T(8,128)(2,1)S(1)}, u32[]{:S(2)}, u32[]{:S(2)}) %collective-permute-start.22) | collective-permute-done | bytes 122912 | tf_op jit(solution)/shard_map/ppermute | solution.py:33
  160.3 2.5 %collective-permute-done.23 = bf16[80,768]{1,0:T(8,128)(2,1)S(1)} collective-permute-done((bf16[80,768]{1,0:T(8,128)(2,1)S(1)}, bf16[80,768]{1,0:T(8,128)(2,1)S(1)}, u32[]{:S(2)}, u32[]{:S(2)}) %collective-permute-start.23) | collective-permute-done | bytes 122912 | tf_op jit(solution)/shard_map/ppermute | solution.py:33
  163.2 2.6 %fusion.23 = (f32[32]{0:T(128)S(1)}, f32[32]{0:T(128)S(1)}, f32[32,3072]{1,0:T(8,128)S(1)}) fusion(f32[32]{0:T(128)S(1)} %add_rsqrt_fusion, f32[32]{0:T(128)S(1)} %broadcast_multiply_fusion.2, bf16[32,3072]{1,0:T(8,128)(2,1)S(1)} %copy-done.6, f32[3072]{0:T(1024)S(1)} %copy-done.12, bf16[32,384]{1,0:T(8,128)(2,1)S(1)} %reduce_sum.68, ...), kind=kOutput, calls=%fused_computation.93 | convolution fusion | flops 76185536 | bytes 2986496 | tf_op jit(solution)/shard_map/tc,dc->td/dot_general | solution.py:295
  165.8 1.8 fusion.1
  167.6 5.3 %collective-permute-start.26 = (bf16[192,768]{1,0:T(8,128)(2,1)}, bf16[192,768]{1,0:T(8,128)(2,1)S(1)}, u32[]{:S(2)}, u32[]{:S(2)}) collective-permute-start(bf16[192,768]{1,0:T(8,128)(2,1)} %fusion.1), channel_id=1, source_target_pairs={{0,128},{16,144},{32,160},{48,176},{64,192},{80,208},{96,224},{112... | collective-permute-start | bytes 884744 | tf_op jit(solution)/shard_map/ppermute | solution.py:33
  173.9 0.8 copy.33
  174.8 6.9 %all-to-all-start.3 = ((bf16[16,12,768]{2,1,0:T(8,128)(2,1)}), bf16[16,12,768]{2,1,0:T(8,128)(2,1)S(1)}, u32[]{:S(2)}, u32[]{:S(2)}) async-start(bf16[16,12,768]{2,1,0:T(8,128)(2,1)} %copy.33), calls=%async_computation.3 | async-start | bytes 786432 | tf_op jit(solution)/shard_map/all_to_all | solution.py:288
  181.7 0.9 fusion.16
  182.6 2.0 %fusion.2 = f32[192,768]{1,0:T(8,128)} fusion(bf16[192,768]{1,0:T(8,128)(2,1)S(1)} %collective-permute-done.26, bf16[2,192,768]{2,1,0:T(8,128)(2,1)} %copy-done.11, bf16[2,192,768]{2,1,0:T(8,128)(2,1)S(1)} %collective-permute-done.19, bf16[4,2,192,768]{3,2,1,0:T(8,128)(2,1)} %add_convert_fusion), kind=kLoop, calls=%fused_computation.21 | loop fusion | flops 1032192 | bytes 1769472 | tf_op jit(solution)/shard_map/add | solution.py:276
  184.6 1.1 convolution_bitcast_fusion
  185.7 11.8 %all-to-all-done.3 = bf16[16,12,768]{2,1,0:T(8,128)(2,1)S(1)} async-done(((bf16[16,12,768]{2,1,0:T(8,128)(2,1)}), bf16[16,12,768]{2,1,0:T(8,128)(2,1)S(1)}, u32[]{:S(2)}, u32[]{:S(2)}) %all-to-all-start.3) | async-done | bytes 294944 | tf_op jit(solution)/shard_map/all_to_all | solution.py:288
  (96 shorter events, 8.6 us)
Async XLA Ops:
  0.6 33.9 %copy-start.8 = (bf16[32,3072]{1,0:T(8,128)(2,1)S(1)}, bf16[32,3072]{1,0:T(8,128)(2,1)}, u32[]{:S(2)}) copy-start(bf16[32,3072]{1,0:T(8,128)(2,1)} %param.11) | copy-start | bytes 589828
  0.6 11.4 %collective-permute-start = (bf16[192,384]{1,0:T(8,128)(2,1)}, bf16[192,384]{1,0:T(8,128)(2,1)S(1)}, u32[]{:S(2)}, u32[]{:S(2)}) collective-permute-start(bf16[192,384]{1,0:T(8,128)(2,1)} %param.8), channel_id=1, source_target_pairs={{0,128},{16,144},{32,160},{48,176},{64,192},{80,208},{96,224},{112... | collective-permute-start | bytes 442376 | tf_op jit(solution)/shard_map/ppermute | solution.py:33
  12.1 11.0 %collective-permute-start.4 = (bf16[32,3072]{1,0:T(8,128)(2,1)}, bf16[32,3072]{1,0:T(8,128)(2,1)S(1)}, u32[]{:S(2)}, u32[]{:S(2)}) collective-permute-start(bf16[32,3072]{1,0:T(8,128)(2,1)} %param.11), channel_id=1, source_target_pairs={{0,12},{1,13},{2,14},{3,15},{4,0},{5,1},{6,2},{7,3},{8,4},{9,5},{1... | collective-permute-start | bytes 589832 | tf_op jit(solution)/shard_map/ppermute | solution.py:33
  17.1 17.4 %collective-permute-start.5 = (bf16[32,3072]{1,0:T(8,128)(2,1)}, bf16[32,3072]{1,0:T(8,128)(2,1)S(1)}, u32[]{:S(2)}, u32[]{:S(2)}) collective-permute-start(bf16[32,3072]{1,0:T(8,128)(2,1)} %param.11), channel_id=1, source_target_pairs={{0,8},{1,9},{2,10},{3,11},{4,12},{5,13},{6,14},{7,15},{8,0},{9,1},... | collective-permute-start | bytes 589832 | tf_op jit(solution)/shard_map/ppermute | solution.py:33
  17.7 16.8 %collective-permute-start.6 = (bf16[32,3072]{1,0:T(8,128)(2,1)}, bf16[32,3072]{1,0:T(8,128)(2,1)S(1)}, u32[]{:S(2)}, u32[]{:S(2)}) collective-permute-start(bf16[32,3072]{1,0:T(8,128)(2,1)} %param.11), channel_id=1, source_target_pairs={{0,4},{1,5},{2,6},{3,7},{4,8},{5,9},{6,10},{7,11},{8,12},{9,13},{1... | collective-permute-start | bytes 589832 | tf_op jit(solution)/shard_map/ppermute | solution.py:33
  20.0 14.5 %collective-permute-start.1 = (bf16[2,192,384]{2,1,0:T(8,128)(2,1)S(1)}, bf16[2,192,384]{2,1,0:T(8,128)(2,1)S(1)}, u32[]{:S(2)}, u32[]{:S(2)}) collective-permute-start(bf16[2,192,384]{2,1,0:T(8,128)(2,1)S(1)} %pad_maximum_fusion.5), channel_id=1, source_target_pairs={{0,96},{16,112},{32,0},{48,16},{64,32},{80,48},{96,64},{112,80},{1... | collective-permute-start | bytes 884744 | tf_op jit(solution)/shard_map/ppermute | solution.py:33
  20.6 14.0 %collective-permute-start.2 = (bf16[2,192,384]{2,1,0:T(8,128)(2,1)S(1)}, bf16[2,192,384]{2,1,0:T(8,128)(2,1)S(1)}, u32[]{:S(2)}, u32[]{:S(2)}) collective-permute-start(bf16[2,192,384]{2,1,0:T(8,128)(2,1)S(1)} %pad_maximum_fusion.5), channel_id=1, source_target_pairs={{0,64},{16,80},{32,96},{48,112},{64,0},{80,16},{96,32},{112,48},{1... | collective-permute-start | bytes 884744 | tf_op jit(solution)/shard_map/ppermute | solution.py:33
  23.1 12.5 %collective-permute-start.3 = (bf16[2,192,384]{2,1,0:T(8,128)(2,1)S(1)}, bf16[2,192,384]{2,1,0:T(8,128)(2,1)S(1)}, u32[]{:S(2)}, u32[]{:S(2)}) collective-permute-start(bf16[2,192,384]{2,1,0:T(8,128)(2,1)S(1)} %pad_maximum_fusion.5), channel_id=1, source_target_pairs={{0,32},{16,48},{32,64},{48,80},{64,96},{80,112},{96,0},{112,16},{1... | collective-permute-start | bytes 884744 | tf_op jit(solution)/shard_map/ppermute | solution.py:33
  35.9 1.4 copy-start.7
  38.4 3.2 %collective-permute-start.7 = (bf16[4,2,192,384]{3,2,0,1:T(8,128)(2,1)}, bf16[4,2,192,384]{3,2,0,1:T(8,128)(2,1)}, u32[]{:S(2)}, u32[]{:S(2)}) collective-permute-start(bf16[4,2,192,384]{3,2,0,1:T(8,128)(2,1)} %constant_dynamic-slice_fusion.2), channel_id=1, source_target_pairs={{0,16},{16,0},{32,48},{48,32},{64,80},{80,64},{96,112},{112,96},{1... | collective-permute-start | bytes 3538952 | tf_op jit(solution)/shard_map/ppermute | solution.py:33
  38.4 22.1 %collective-permute-start.8 = (bf16[128,3072]{1,0:T(8,128)(2,1)S(1)}, bf16[128,3072]{1,0:T(8,128)(2,1)S(1)}, u32[]{:S(2)}, u32[]{:S(2)}) collective-permute-start(bf16[128,3072]{1,0:T(8,128)(2,1)S(1)} %pad_maximum_fusion.1.p0), channel_id=1, source_target_pairs={{0,3},{1,0},{2,1},{3,2},{4,7},{5,4},{6,5},{7,6},{8,11},{9,8},{10,9... | collective-permute-start | bytes 2359304 | tf_op jit(solution)/shard_map/ppermute | solution.py:33
  41.4 23.6 %collective-permute-start.9 = (bf16[128,3072]{1,0:T(8,128)(2,1)S(1)}, bf16[128,3072]{1,0:T(8,128)(2,1)S(1)}, u32[]{:S(2)}, u32[]{:S(2)}) collective-permute-start(bf16[128,3072]{1,0:T(8,128)(2,1)S(1)} %pad_maximum_fusion.1.p0), channel_id=1, source_target_pairs={{0,1},{1,2},{2,3},{3,0},{4,5},{5,6},{6,7},{7,4},{8,9},{9,10},{10,1... | collective-permute-start | bytes 2359304 | tf_op jit(solution)/shard_map/ppermute | solution.py:33
  48.0 21.3 %all-to-all-start = ((bf16[16,32,384]{2,1,0:T(8,128)(2,1)}), bf16[16,32,384]{2,1,0:T(8,128)(2,1)S(1)}, u32[]{:S(2)}, u32[]{:S(2)}) async-start(bf16[16,32,384]{2,1,0:T(8,128)(2,1)} %broadcast_in_dim.2), calls=%async_computation | async-start | bytes 786432 | tf_op jit(solution)/shard_map/all_to_all | solution.py:73
  60.5 29.4 %copy-start.1 = (bf16[128,3072]{1,0:T(8,128)(2,1)}, bf16[128,3072]{1,0:T(8,128)(2,1)S(1)}, u32[]{:S(2)}) copy-start(bf16[128,3072]{1,0:T(8,128)(2,1)S(1)} %collective-permute-done.8.p1) | copy-start | bytes 2359300
  65.1 24.9 %copy-start.3 = (bf16[128,3072]{1,0:T(8,128)(2,1)}, bf16[128,3072]{1,0:T(8,128)(2,1)S(1)}, u32[]{:S(2)}) copy-start(bf16[128,3072]{1,0:T(8,128)(2,1)S(1)} %collective-permute-done.9.p4) | copy-start | bytes 2359300
  65.9 19.5 %collective-permute-start.10 = (bf16[64,3072]{1,0:T(8,128)(2,1)}, bf16[64,3072]{1,0:T(8,128)(2,1)}, u32[]{:S(2)}, u32[]{:S(2)}) collective-permute-start(bf16[64,3072]{1,0:T(8,128)(2,1)} %slice.82), channel_id=1, source_target_pairs={{0,3},{1,0},{2,1},{3,2},{4,7},{5,4},{6,5},{7,6},{8,11},{9,8},{10,9... | collective-permute-start | bytes 1179656 | tf_op jit(solution)/shard_map/ppermute | solution.py:33
  66.7 18.8 %collective-permute-start.11 = (bf16[64,3072]{1,0:T(8,128)(2,1)}, bf16[64,3072]{1,0:T(8,128)(2,1)}, u32[]{:S(2)}, u32[]{:S(2)}) collective-permute-start(bf16[64,3072]{1,0:T(8,128)(2,1)} %slice.83), channel_id=1, source_target_pairs={{0,1},{1,2},{2,3},{3,0},{4,5},{5,6},{6,7},{7,4},{8,9},{9,10},{10,1... | collective-permute-start | bytes 1179656 | tf_op jit(solution)/shard_map/ppermute | solution.py:33
  70.4 19.5 %all-to-all-start.1 = ((bf16[32,16,192]{2,0,1:T(8,128)(2,1)}), bf16[32,16,192]{2,0,1:T(8,128)(2,1)}, u32[]{:S(2)}, u32[]{:S(2)}) async-start(bf16[32,16,192]{2,0,1:T(8,128)(2,1)} %copy.28), calls=%async_computation.1 | async-start | bytes 524288 | tf_op jit(solution)/shard_map/all_to_all | solution.py:246
  90.0 2.3 %copy-start.5 = (bf16[3072,768]{1,0:T(8,128)(2,1)S(1)}, bf16[3072,768]{1,0:T(8,128)(2,1)}, u32[]{:S(2)}) copy-start(bf16[3072,768]{1,0:T(8,128)(2,1)} %w_down.1) | copy-start | bytes 14155780
  100.6 11.2 %copy-start = (bf16[2,4,48,768]{3,2,1,0:T(8,128)(2,1)}, bf16[2,4,48,768]{3,2,1,0:T(8,128)(2,1)S(1)}, u32[]{:S(2)}) copy-start(bf16[2,4,48,768]{3,2,1,0:T(8,128)(2,1)S(1)} %get-tuple-element.61) | copy-start | bytes 1769476
  100.6 1.3 copy-start.2
  102.0 1.1 copy-start.4
  111.1 9.0 %collective-permute-start.12 = (bf16[4,2,192,768]{3,2,1,0:T(8,128)(2,1)}, bf16[4,2,192,768]{3,2,1,0:T(8,128)(2,1)}, u32[]{:S(2)}, u32[]{:S(2)}) collective-permute-start(bf16[4,2,192,768]{3,2,1,0:T(8,128)(2,1)} %get-tuple-element.60), channel_id=1, source_target_pairs={{0,16},{16,0},{32,48},{48,32},{64,80},{80,64},{96,112},{112,96},{1... | collective-permute-start | bytes 7077896 | tf_op jit(solution)/shard_map/ppermute | solution.py:33
  111.8 7.2 %collective-permute-start.13 = (bf16[4,48,768]{2,1,0:T(8,128)(2,1)S(1)}, bf16[4,48,768]{2,1,0:T(8,128)(2,1)S(1)}, u32[]{:S(2)}, u32[]{:S(2)}) collective-permute-start(bf16[4,48,768]{2,1,0:T(8,128)(2,1)S(1)} %slice_bitcast_fusion.4), channel_id=1, source_target_pairs={{0,16},{16,0},{32,48},{48,32},{64,80},{80,64},{96,112},{112,96},{1... | collective-permute-start | bytes 884744 | tf_op jit(solution)/shard_map/ppermute | solution.py:33
  111.9 20.5 %all-to-all-start.2 = ((bf16[16,32,384]{2,1,0:T(8,128)(2,1)}), bf16[16,32,384]{2,1,0:T(8,128)(2,1)S(1)}, u32[]{:S(2)}, u32[]{:S(2)}) async-start(bf16[16,32,384]{2,1,0:T(8,128)(2,1)} %get-tuple-element.64), calls=%async_computation.2 | async-start | bytes 786432 | tf_op jit(solution)/shard_map/all_to_all | solution.py:79
  123.8 8.7 %collective-permute-start.16 = (bf16[48,768]{1,0:T(8,128)(2,1)S(1)}, bf16[48,768]{1,0:T(8,128)(2,1)S(1)}, u32[]{:S(2)}, u32[]{:S(2)}) collective-permute-start(bf16[48,768]{1,0:T(8,128)(2,1)S(1)} %get-tuple-element.91), channel_id=1, source_target_pairs={{0,32},{16,48},{32,64},{48,80},{64,96},{80,112},{96,0},{112,16},{1... | collective-permute-start | bytes 221192 | tf_op jit(solution)/shard_map/ppermute | solution.py:33
  124.7 7.8 %collective-permute-start.17 = (bf16[48,768]{1,0:T(8,128)(2,1)S(1)}, bf16[48,768]{1,0:T(8,128)(2,1)S(1)}, u32[]{:S(2)}, u32[]{:S(2)}) collective-permute-start(bf16[48,768]{1,0:T(8,128)(2,1)S(1)} %get-tuple-element.93), channel_id=1, source_target_pairs={{0,64},{16,80},{32,96},{48,112},{64,0},{80,16},{96,32},{112,48},{1... | collective-permute-start | bytes 221192 | tf_op jit(solution)/shard_map/ppermute | solution.py:33
  128.1 4.4 %collective-permute-start.18 = (bf16[48,768]{1,0:T(8,128)(2,1)S(1)}, bf16[48,768]{1,0:T(8,128)(2,1)S(1)}, u32[]{:S(2)}, u32[]{:S(2)}) collective-permute-start(bf16[48,768]{1,0:T(8,128)(2,1)S(1)} %get-tuple-element.92), channel_id=1, source_target_pairs={{0,96},{16,112},{32,0},{48,16},{64,32},{80,48},{96,64},{112,80},{1... | collective-permute-start | bytes 221192 | tf_op jit(solution)/shard_map/ppermute | solution.py:33
  130.2 8.0 %collective-permute-start.14 = (bf16[192,768]{1,0:T(8,128)(2,1)S(1)}, bf16[192,768]{1,0:T(8,128)(2,1)S(1)}, u32[]{:S(2)}, u32[]{:S(2)}) collective-permute-start(bf16[192,768]{1,0:T(8,128)(2,1)S(1)} %get-tuple-element.84), channel_id=1, source_target_pairs={{0,32},{16,48},{32,64},{48,80},{64,96},{80,112},{96,0},{112,16},{1... | collective-permute-start | bytes 884744 | tf_op jit(solution)/shard_map/ppermute | solution.py:33
  131.5 7.6 %collective-permute-start.15 = (bf16[192,768]{1,0:T(8,128)(2,1)S(1)}, bf16[192,768]{1,0:T(8,128)(2,1)S(1)}, u32[]{:S(2)}, u32[]{:S(2)}) collective-permute-start(bf16[192,768]{1,0:T(8,128)(2,1)S(1)} %get-tuple-element.83), channel_id=1, source_target_pairs={{0,96},{16,112},{32,0},{48,16},{64,32},{80,48},{96,64},{112,80},{1... | collective-permute-start | bytes 884744 | tf_op jit(solution)/shard_map/ppermute | solution.py:33
  141.4 8.6 %collective-permute-start.21 = (bf16[64,768]{1,0:T(8,128)(2,1)S(1)}, bf16[64,768]{1,0:T(8,128)(2,1)S(1)}, u32[]{:S(2)}, u32[]{:S(2)}) collective-permute-start(bf16[64,768]{1,0:T(8,128)(2,1)S(1)} %pad_maximum_fusion.8), channel_id=1, source_target_pairs={{0,128},{16,144},{32,160},{48,176},{64,192},{80,208},{96,224},{112... | collective-permute-start | bytes 294920 | tf_op jit(solution)/shard_map/ppermute | solution.py:33
  142.0 20.8 %collective-permute-start.19 = (bf16[2,192,768]{2,1,0:T(8,128)(2,1)}, bf16[2,192,768]{2,1,0:T(8,128)(2,1)S(1)}, u32[]{:S(2)}, u32[]{:S(2)}) collective-permute-start(bf16[2,192,768]{2,1,0:T(8,128)(2,1)} %get-tuple-element.69), channel_id=1, source_target_pairs={{0,32},{16,48},{32,64},{48,80},{64,96},{80,112},{96,0},{112,16},{1... | collective-permute-start | bytes 1769480 | tf_op jit(solution)/shard_map/ppermute | solution.py:33
  142.4 20.4 %collective-permute-start.20 = (bf16[2,192,768]{2,1,0:T(8,128)(2,1)}, bf16[2,192,768]{2,1,0:T(8,128)(2,1)S(1)}, u32[]{:S(2)}, u32[]{:S(2)}) collective-permute-start(bf16[2,192,768]{2,1,0:T(8,128)(2,1)} %get-tuple-element.70), channel_id=1, source_target_pairs={{0,96},{16,112},{32,0},{48,16},{64,32},{80,48},{96,64},{112,80},{1... | collective-permute-start | bytes 1769480 | tf_op jit(solution)/shard_map/ppermute | solution.py:33
  150.1 10.2 %collective-permute-start.22 = (bf16[80,768]{1,0:T(8,128)(2,1)S(1)}, bf16[80,768]{1,0:T(8,128)(2,1)S(1)}, u32[]{:S(2)}, u32[]{:S(2)}) collective-permute-start(bf16[80,768]{1,0:T(8,128)(2,1)S(1)} %pad_maximum_fusion.7), channel_id=1, source_target_pairs={{0,96},{16,112},{32,0},{48,16},{64,32},{80,48},{96,64},{112,80},{1... | collective-permute-start | bytes 368648 | tf_op jit(solution)/shard_map/ppermute | solution.py:33
  151.1 11.7 %collective-permute-start.23 = (bf16[80,768]{1,0:T(8,128)(2,1)S(1)}, bf16[80,768]{1,0:T(8,128)(2,1)S(1)}, u32[]{:S(2)}, u32[]{:S(2)}) collective-permute-start(bf16[80,768]{1,0:T(8,128)(2,1)S(1)} %pad_maximum_fusion.7), channel_id=1, source_target_pairs={{0,64},{16,80},{32,96},{48,112},{64,0},{80,16},{96,32},{112,48},{1... | collective-permute-start | bytes 368648 | tf_op jit(solution)/shard_map/ppermute | solution.py:33
  153.0 9.9 %collective-permute-start.24 = (bf16[80,768]{1,0:T(8,128)(2,1)S(1)}, bf16[80,768]{1,0:T(8,128)(2,1)S(1)}, u32[]{:S(2)}, u32[]{:S(2)}) collective-permute-start(bf16[80,768]{1,0:T(8,128)(2,1)S(1)} %pad_maximum_fusion.7), channel_id=1, source_target_pairs={{0,32},{16,48},{32,64},{48,80},{64,96},{80,112},{96,0},{112,16},{1... | collective-permute-start | bytes 368648 | tf_op jit(solution)/shard_map/ppermute | solution.py:33
  156.6 6.6 %copy-start.6 = (bf16[32,3072]{1,0:T(8,128)(2,1)S(1)}, bf16[32,3072]{1,0:T(8,128)(2,1)}, u32[]{:S(2)}) copy-start(bf16[32,3072]{1,0:T(8,128)(2,1)} %param.6) | copy-start | bytes 589828
  156.6 6.6 %copy-start.12 = (f32[3072]{0:T(1024)S(1)}, f32[3072]{0:T(1024)}, u32[]{:S(2)}) copy-start(f32[3072]{0:T(1024)} %param.7) | copy-start | bytes 36868
  162.8 2.9 %copy-start.11 = (bf16[2,192,768]{2,1,0:T(8,128)(2,1)}, bf16[2,192,768]{2,1,0:T(8,128)(2,1)S(1)}, u32[]{:S(2)}) copy-start(bf16[2,192,768]{2,1,0:T(8,128)(2,1)S(1)} %collective-permute-done.20) | copy-start | bytes 1769476
  163.0 9.8 %collective-permute-start.25 = (bf16[4,80,768]{2,1,0:T(8,128)(2,1)S(1)}, bf16[4,80,768]{2,1,0:T(8,128)(2,1)S(1)}, u32[]{:S(2)}, u32[]{:S(2)}) collective-permute-start(bf16[4,80,768]{2,1,0:T(8,128)(2,1)S(1)} %constant_dynamic-slice_fusion.1), channel_id=1, source_target_pairs={{0,16},{16,0},{32,48},{48,32},{64,80},{80,64},{96,112},{112,96},{1... | collective-permute-start | bytes 1474568 | tf_op jit(solution)/shard_map/ppermute | solution.py:33
  167.6 15.0 %collective-permute-start.26 = (bf16[192,768]{1,0:T(8,128)(2,1)}, bf16[192,768]{1,0:T(8,128)(2,1)S(1)}, u32[]{:S(2)}, u32[]{:S(2)}) collective-permute-start(bf16[192,768]{1,0:T(8,128)(2,1)} %fusion.1), channel_id=1, source_target_pairs={{0,128},{16,144},{32,160},{48,176},{64,192},{80,208},{96,224},{112... | collective-permute-start | bytes 884744 | tf_op jit(solution)/shard_map/ppermute | solution.py:33
  173.2 8.5 %copy-start.9 = (bf16[32,3072]{1,0:T(8,128)(2,1)S(1)}, bf16[32,3072]{1,0:T(8,128)(2,1)}, u32[]{:S(2)}) copy-start(bf16[32,3072]{1,0:T(8,128)(2,1)} %param.11) | copy-start | bytes 589828
  173.9 10.7 %copy-start.10 = (bf16[192,384]{1,0:T(8,128)(2,1)S(1)}, bf16[192,384]{1,0:T(8,128)(2,1)}, u32[]{:S(2)}) copy-start(bf16[192,384]{1,0:T(8,128)(2,1)} %param.8) | copy-start | bytes 442372
  174.8 22.8 %all-to-all-start.3 = ((bf16[16,12,768]{2,1,0:T(8,128)(2,1)}), bf16[16,12,768]{2,1,0:T(8,128)(2,1)S(1)}, u32[]{:S(2)}, u32[]{:S(2)}) async-start(bf16[16,12,768]{2,1,0:T(8,128)(2,1)} %copy.33), calls=%async_computation.3 | async-start | bytes 786432 | tf_op jit(solution)/shard_map/all_to_all | solution.py:288

commit v3 on v2

v3 whole, which is shorter than its diff:
```python
import jax
import jax.numpy as jnp
from jax import lax
from jax.experimental import pallas as pl
from jax.experimental.pallas import tpu as pltpu
from jax.sharding import PartitionSpec as P

F32 = jnp.float32
BF16 = jnp.bfloat16


def step_core(i):
    return i ^ 1


def step_far(i):
    return i ^ 8


def step_x(k):
    return lambda i: (i & 9) | ((((i >> 1) + k) & 3) << 1)


def step_y(k):
    return lambda i: (i & 12) | ((i + k) & 3)


def step_z(k):
    return lambda i: ((((i >> 2) + k) & 3) << 2) | (i & 3)


def send(value, axis, target):
    return lax.ppermute(value, axis, [(i, target(i)) for i in range(16)])


def gather_parts(value, axis, step):
    return [value] + [send(value, axis, step(-k)) for k in (1, 2, 3)]


def in_order(parts, at):
    n = len(parts)
    twice = jnp.stack(parts + parts[:-1])
    return lax.dynamic_slice_in_dim(twice, (n - at) % n, n, 0)


def pair_in_order(mine, other, at):
    first = jnp.where(at == 0, mine, other)
    second = jnp.where(at == 0, other, mine)
    return first, second


def pick(value, at, axis):
    return lax.dynamic_index_in_dim(value, at, axis, keepdims=False)


def gelu_parts(pre_act):
    cdf_part = 0.5 * (1.0 + lax.erf(pre_act * 0.7071067811865476))
    density = jnp.exp(-0.5 * pre_act * pre_act) * 0.3989422804014327
    return (pre_act * cdf_part, cdf_part + pre_act * density)


def add(a, b):
    return a.astype(F32) + b.astype(F32)


def join_encoder(along, across, core):
    width = along.shape[1]
    full = jnp.stack(pair_in_order(along, across, core)).reshape(2, 4, 2, -1, width)
    return full.transpose(2, 1, 0, 3, 4).reshape(-1, width)


def gather_codes(code_rows):
    count, width = code_rows.shape
    return lax.all_to_all(
        jnp.broadcast_to(code_rows, (16, count, width)), "mp", split_axis=0, concat_axis=0
    )


def scatter_codes(part):
    got = lax.all_to_all(part, "mp", split_axis=0, concat_axis=0)
    return jnp.sum(got.astype(F32), axis=0)


VMEM = 58 * 1024 * 1024
SMALL = 16 * 1024 * 1024


def token_block(k, at):
    return ((at[0] + k % 4) % 4) * 4 + (at[1] + k // 4) % 4


def fill_rows(at, codes, rows):
    count = codes.shape[1]
    for k in range(16):
        rows[k * count : (k + 1) * count, :] = codes[token_block(k, at)]


def row_copies(pieces, rows, sems):
    copies, start = [], 0
    for k, piece in enumerate(pieces):
        count = piece.shape[0]
        copies.append(
            pltpu.make_async_copy(piece, rows.at[pl.ds(start, count), :], sems.at[k])
        )
        start += count
    return copies


def whole(shape):
    return pl.BlockSpec(shape, lambda i, at: (0,) * len(shape))


def mlp_kernel(at, codes, tied, w_down, *refs):
    pieces, (keep, give, codes_part, inner) = refs[:5], refs[5:9]
    rows, hidden, slope, total, upstream, weights, sems = refs[9:]
    step = pl.program_id(0)
    span = 2 * keep.shape[2]
    here = pl.ds(pl.multiple_of(step * span, span), span)

    def weight_copy(k):
        part = pl.ds(pl.multiple_of(k * span, span), span)
        return pltpu.make_async_copy(w_down.at[part, :], weights.at[part, :], sems.at[5 + k])

    @pl.when(step == 0)
    def _():
        copies = row_copies(pieces, upstream, sems)
        for c in copies:
            c.start()
        for k in range(8):
            weight_copy(k).start()
        fill_rows(at, codes, rows)
        pre_act = jnp.dot(rows[...], tied[...], preferred_element_type=F32)
        value, grade = gelu_parts(pre_act)
        hidden[...] = value.astype(BF16)
        slope[...] = grade
        total[...] = jnp.zeros_like(total)
        for c in copies:
            c.wait()

    weight_copy(step).wait()
    part = upstream[:, here]
    total[...] += jnp.dot(part, weights[here, :], preferred_element_type=F32)
    term = lax.dot_general(
        part, hidden[...], (((0,), (0,)), ((), ())), preferred_element_type=F32
    ).astype(BF16)
    half = term.shape[0] // 2
    first, second = term[:half], term[half:]

    @pl.when(at[2] == 0)
    def _():
        keep[0, 0] = first
        give[0, 0] = second

    @pl.when(at[2] != 0)
    def _():
        keep[0, 0] = second
        give[0, 0] = first

    @pl.when(step == 7)
    def _():
        d_act = (total[...] * slope[...]).astype(BF16)
        back = lax.dot_general(
            d_act, tied[...], (((1,), (1,)), ((), ())), preferred_element_type=F32
        ).astype(BF16)
        count = codes.shape[1]
        for k in range(16):
            codes_part[token_block(k, at)] = back[k * count : (k + 1) * count, :]
        outer = lax.dot_general(
            rows[...], d_act, (((0,), (0,)), ((), ())), preferred_element_type=F32
        ).astype(BF16)
        piece = outer.shape[0] // 8
        for k in range(8):
            to_core = (k // 4 + at[2]) % 2
            inner[to_core, (k % 4 + 4 - at[3]) % 4] = outer[k * piece : (k + 1) * piece, :]


def mlp_call(at, codes, tied, w_down, pieces):
    width, units = tied.shape
    tokens = codes.shape[0] * codes.shape[1]
    features = w_down.shape[0]
    span = features // 8

    def place(i, at):
        return ((i % 4 + 4 - at[3]) % 4, (i // 4 + at[4]) % 2, 0, 0)

    out = [jax.ShapeDtypeStruct((4, 2, span // 2, units), BF16)] * 2
    out += [
        jax.ShapeDtypeStruct(codes.shape, BF16),
        jax.ShapeDtypeStruct((2, 4, width // 8, units), BF16),
    ]
    return pl.pallas_call(
        mlp_kernel,
        grid_spec=pltpu.PrefetchScalarGridSpec(
            num_scalar_prefetch=1,
            grid=(8,),
            in_specs=[whole(codes.shape), whole(tied.shape)]
            + [pl.BlockSpec(memory_space=pltpu.HBM)]
            + [pl.BlockSpec(memory_space=pltpu.HBM)] * 5,
            out_specs=[pl.BlockSpec((1, 1, span // 2, units), place)] * 2
            + [whole(o.shape) for o in out[2:]],
            scratch_shapes=[
                pltpu.VMEM((tokens, width), BF16),
                pltpu.VMEM((tokens, units), BF16),
                pltpu.VMEM((tokens, units), F32),
                pltpu.VMEM((tokens, units), F32),
                pltpu.VMEM((tokens, features), BF16),
                pltpu.VMEM((features, units), BF16),
                pltpu.SemaphoreType.DMA((13,)),
            ],
        ),
        out_shape=out,
        compiler_params=pltpu.CompilerParams(vmem_limit_bytes=VMEM),
        cost_estimate=pl.CostEstimate(
            flops=4 * tokens * units * (features + width),
            bytes_accessed=2 * (3 * features * units + tokens * features),
            transcendentals=2 * tokens * units,
        ),
    )(at, codes, tied, w_down, *pieces)


def tied_kernel(at, along, across, w_up, out, total):
    step = pl.program_id(0)
    mine, other = along[0], across[0]
    lower = at[2] == 0
    block = jnp.concatenate(
        [jnp.where(lower, mine, other), jnp.where(lower, other, mine)], axis=0
    )
    part = lax.dot_general(
        block, w_up[...], (((0,), (0,)), ((), ())), preferred_element_type=F32
    )

    @pl.when(step == 0)
    def _():
        total[...] = part

    @pl.when(step != 0)
    def _():
        total[...] += part

    @pl.when(step == 7)
    def _():
        out[...] = total[...].astype(BF16)


def tied_call(at, along, across, w_up):
    rows, width = along.shape[0] // 8, along.shape[1]
    units = w_up.shape[1]
    block = pl.BlockSpec((1, rows, width), lambda i, at: (i, 0, 0))
    return pl.pallas_call(
        tied_kernel,
        grid_spec=pltpu.PrefetchScalarGridSpec(
            num_scalar_prefetch=1,
            grid=(8,),
            in_specs=[
                block,
                block,
                pl.BlockSpec((2 * rows, units), lambda i, at: (i % 2 * 4 + i // 2, 0)),
            ],
            out_specs=whole((width, units)),
            scratch_shapes=[pltpu.VMEM((width, units), F32)],
        ),
        out_shape=jax.ShapeDtypeStruct((width, units), BF16),
        compiler_params=pltpu.CompilerParams(vmem_limit_bytes=SMALL),
        cost_estimate=pl.CostEstimate(
            flops=32 * rows * width * units, bytes_accessed=64 * rows * units, transcendentals=0
        ),
    )(at, along.reshape(8, rows, width), across.reshape(8, rows, width), w_up)


def rows_kernel(at, normed, w_up, encoder, *refs):
    parts, (both, grad_up, inner, codes, sums) = (refs[:4], refs[4:8]), refs[8:]
    width = encoder.shape[1]
    units = w_up.shape[1]
    count = inner.shape[0] // 8
    for c in range(2):
        for k in range(4):
            part = parts[c][k]
            place = ((at[2] + c) % 2 * 4 + (at[3] + k) % 4) * count
            inner[pl.ds(pl.multiple_of(place, count), count), :] = part[:count, :]
            place = (c * 4 + (4 - k) % 4) * 64
            for j in range(4):
                codes[place + 16 * j : place + 16 * (j + 1), :] = part[
                    count + 16 * (j // 2) : count + 16 * (j // 2 + 1),
                    width * (j % 2) : width * (j % 2 + 1),
                ]
    sums[:, :width] = lax.dot_general(
        normed[...], codes[...], (((0,), (0,)), ((), ())), preferred_element_type=F32
    )
    sums[:, width:] = lax.dot_general(
        w_up[...], inner[...], (((1,), (1,)), ((), ())), preferred_element_type=F32
    )
    own = both.shape[1]
    for k in range(16):
        both[k] = sums[k * own : (k + 1) * own, :].astype(BF16)
    grad_up[...] = jnp.dot(encoder[...], inner[...], preferred_element_type=F32)


def rows_call(at, normed, w_up, encoder, parts, others):
    tokens, rows = normed.shape
    width, units = encoder.shape[1], w_up.shape[1]
    out = [
        jax.ShapeDtypeStruct((16, rows // 16, 2 * width), BF16),
        jax.ShapeDtypeStruct((rows, units), F32),
    ]
    return pl.pallas_call(
        rows_kernel,
        grid_spec=pltpu.PrefetchScalarGridSpec(
            num_scalar_prefetch=1,
            grid=(1,),
            in_specs=[
                whole(normed.shape),
                pl.BlockSpec((rows, units), lambda i, at: (at[5], 0)),
                whole(encoder.shape),
            ]
            + [whole(parts[0].shape)] * 8,
            out_specs=[whole(o.shape) for o in out],
            scratch_shapes=[
                pltpu.VMEM((width, units), BF16),
                pltpu.VMEM((tokens, width), BF16),
                pltpu.VMEM((rows, 2 * width), F32),
            ],
        ),
        out_shape=out,
        compiler_params=pltpu.CompilerParams(vmem_limit_bytes=SMALL),
        cost_estimate=pl.CostEstimate(
            flops=2 * rows * width * (tokens + 2 * units),
            bytes_accessed=2 * rows * (tokens + 3 * units),
            transcendentals=0,
        ),
    )(at, normed, w_up, encoder, *parts, *others)


def on_device(tokens, gain, encoder, w_up, w_down, cotangent):
    rows, width = encoder.shape
    own = rows // 16
    dp_at = lax.axis_index("dp")
    mp_at = lax.axis_index("mp")
    core, x, far = dp_at % 2, (dp_at // 2) % 4, dp_at // 8

    z, y = mp_at // 4, mp_at % 4
    tie = lax.optimization_barrier

    other = send(encoder, "dp", step_far)
    as_float = tokens.astype(F32)
    center = as_float - jnp.mean(as_float, axis=1, keepdims=True)
    inv_std = lax.rsqrt(jnp.mean(center * center, axis=1, keepdims=True) + 1e-06)
    unit = center * inv_std
    normed = (unit * gain).astype(BF16)
    spread = normed.reshape(-1, 2, 4, 2, rows).transpose(3, 0, 2, 1, 4).reshape(2, -1, 8 * rows)
    mine, theirs = pick(spread, core, 0), pick(spread, 1 - core, 0)
    other, normed, late_cotangent = tie((other, normed, cotangent))
    parts = gather_parts(jnp.stack(pair_in_order(encoder, other, far)), "dp", step_x)
    line = gather_parts(late_cotangent, "mp", step_z)
    blocks = normed.reshape(-1, 2, 4, 2, rows).transpose(3, 2, 1, 0, 4)
    got = send(pick(blocks, 1 - core, 0), "dp", step_core)
    along = in_order(parts, x).reshape(8 * rows, width)
    along, line, got = tie((along, jnp.concatenate(line), got))
    across = send(along, "dp", step_core)
    after = send(line, "mp", step_y(-1))
    before = send(line, "mp", step_y(1))
    code_rows = jnp.dot(mine, along, preferred_element_type=F32)
    code_rows += jnp.dot(theirs, across, preferred_element_type=F32)
    code_rows = code_rows.astype(BF16)
    all_codes = gather_codes(code_rows)
    blocks = jnp.stack([pick(blocks, core, 0), got], axis=2)
    got = [send(pick(blocks, (x + k) % 4, 0), "dp", step_x(k)) for k in (1, 2, 3)]
    after, before, _, *got = tie((after, before, code_rows, *got))
    blocks = jnp.stack([pick(blocks, x, 0), *got], axis=2)
    half = line.shape[0] // 2
    far_a = send(after[:half], "mp", step_y(-1))
    far_b = send(before[half:], "mp", step_y(1))
    got = send(pick(blocks, 1 - far, 0), "dp", step_far)
    at = jnp.stack([z, y, core, x, far, dp_at]).astype(jnp.int32)
    tied_up = tied_call(at, along, across, w_up)
    all_codes, tied_up, far_a, far_b, got = tie((all_codes, tied_up, far_a, far_b, got))
    normed_cols = jnp.stack([pick(blocks, far, 0), got], axis=2).reshape(-1, rows)
    pieces = (line, after, far_a, far_b, before)
    keep, give, codes_part, inner = mlp_call(at, all_codes, tied_up, w_down, pieces)
    sent = send(give, "dp", step_core)
    grad_codes = scatter_codes(codes_part).astype(BF16)
    inner = add(inner[0], send(inner[1], "dp", step_core)).astype(BF16)
    first, second = [add(keep[2, k], sent[2, k]).astype(BF16) for k in (0, 1)]
    first, second, inner = tie((first, second, inner))
    got_a = send(first, "dp", step_x(1))
    got_b = send(second, "dp", step_x(-1))
    got = [send(inner[k], "dp", step_x(k)) for k in (1, 2, 3)]
    inner = (inner[0].astype(F32) + sum(g.astype(F32) for g in got)).astype(BF16)
    got_a, got_b, inner, grad_codes = tie((got_a, got_b, inner, grad_codes))
    up = [add(keep[1, 0], sent[1, 0]) + got_a.astype(F32), add(keep[1, 1], sent[1, 1])]
    down = [add(keep[3, 0], sent[3, 0]), add(keep[3, 1], sent[3, 1]) + got_b.astype(F32)]
    up = jnp.stack([u.astype(BF16) for u in up])
    down = jnp.stack([d.astype(BF16) for d in down])
    count, cols = inner.shape
    halves = jnp.split(grad_codes, 2)
    mine = jnp.concatenate([inner, jnp.concatenate(halves, axis=1)])
    up, down, mine = tie((up, down, mine))
    other = send(mine, "dp", step_far)
    up = send(up, "dp", step_x(1))
    down = send(down, "dp", step_x(-1))
    inner = add(inner, other[:count]).astype(BF16)
    mine = jnp.concatenate([inner, mine[count:], other[count:]])
    parts = gather_parts(mine, "dp", step_x)
    up, down, *parts = tie((up, down, *parts))
    total = [add(keep[0, k], sent[0, k]) + add(up[k], down[k]) for k in (0, 1)]
    grad_down = total[0] + send(total[1].astype(BF16), "dp", step_far).astype(F32)
    others = [send(p, "dp", step_core) for p in parts]
    both, grad_up = rows_call(at, normed_cols, w_up, encoder, parts, others)
    both = lax.all_to_all(both, "mp", split_axis=0, concat_axis=0)
    both = jnp.sum(both.astype(F32), axis=0)
    own_encoder = lax.dynamic_slice_in_dim(encoder, mp_at * own, own, 0).astype(F32)
    own_gain = lax.dynamic_slice_in_dim(gain, dp_at * rows + mp_at * own, own, 0)
    grad_encoder = both[:, :width] + both[:, width:]
    grad_gain = jnp.sum(own_encoder * both[:, :width], axis=1) / own_gain
    full_encoder = join_encoder(along, across, core)
    d_normed = jnp.einsum("tc,dc->td", grad_codes, full_encoder, preferred_element_type=F32)
    dx_hat = d_normed * gain
    mean_one = jnp.mean(dx_hat, axis=1, keepdims=True)
    mean_two = jnp.mean(dx_hat * unit, axis=1, keepdims=True)
    grad_tokens = (
        cotangent.astype(F32) + inv_std * (dx_hat - mean_one - unit * mean_two)
    ).astype(BF16)
    return (grad_tokens, grad_up, grad_down, grad_encoder, grad_gain)


def solution(mesh):
    placed = (
        P(("dp", "mp"), None),
        P(),
        P("dp", None),
        P(None, "mp"),
        P(None, "mp"),
        P(("dp", "mp"), None),
    )
    return jax.shard_map(
        on_device,
        mesh=mesh,
        in_specs=placed,
        out_specs=(
            P(("dp", "mp"), None),
            P("dp", "mp"),
            P("dp", "mp"),
            P(("dp", "mp"), None),
            P(("dp", "mp")),
        ),
        check_vma=False,
    )
```

time: 201 us -> 187 us (0.930)
  matrix products: 11.6 us -> 2.28 us
  waiting for transfers between devices: 55.3 us -> 46.8 us
  Pallas kernels: 16.3 us -> 22.1 us
  local copies, waits for them, and re-layouts: 15.9 us -> 13.4 us
    ppermute x27 -> x35, starting transfers between devices: 45.5 us -> 57.9 us  [send(): return lax.ppermute(value, axis, [(i, target(i)) for i in range(16)])]
    all_to_all x2 -> x1, starting transfers between devices: 16.8 us -> 7.06 us  [on_device(): both = lax.all_to_all(both, 'mp', split_axis=0, concat_axis=0)]
    dot_general x5 -> x2, matrix products: 8.95 us -> 0.59 us  [the longest x1 0.3 us: on_device(): code_rows = jnp.dot(mine, along, preferred_element_type=F32)]
    pallas_call x2 -> x3, Pallas kernels: 16.3 us -> 22.1 us  [the longest x1 14.4 us: mlp_call(): pl.pallas_call(mlp_kernel, grid_spec=pltpu.PrefetchScalarGridSpec(num_sca...]
    ppermute x27 -> x35, waiting for transfers between devices: 38.2 us -> 33.4 us  [send(): return lax.ppermute(value, axis, [(i, target(i)) for i in range(16)])]
    all_to_all x2 -> x1, waiting for transfers between devices: 16.3 us -> 11.7 us  [on_device(): both = lax.all_to_all(both, 'mp', split_axis=0, concat_axis=0)]
    another operation x7 -> x5, other arithmetic: 6 us -> 2.04 us  [the longest x1 1.77 us: on_device(): down = jnp.stack([d.astype(BF16) for d in down])]
    unnamed x38 -> x52, local copies, waits for them, and re-layouts: 6.55 us -> 5.22 us
  transfers between devices with their start and end apart: 31 -> 38, of which waited for: 16 -> 13; matrix products, arithmetic and copies ran while one was open for 19% -> 14% of each run, Pallas kernels for 0% -> 4%
where the time goes in v3:
time: 187 us; the launch traced here: 184 us
  starting transfers between devices  78.4 us (42%)
  waiting for transfers between devices  46.8 us (25%)
  Pallas kernels  22.1 us (12%)
  other arithmetic  19.3 us (10%)
  local copies, waits for them, and re-layouts  13.4 us (7%)
  matrix products  2.28 us (1%)
    ppermute x35, starting transfers between devices, send(): return lax.ppermute(value, axis, [(i, target(i)) for i in range(16)])  57.9 us
    ppermute x35, waiting for transfers between devices, send(): return lax.ppermute(value, axis, [(i, target(i)) for i in range(16)])  33.4 us
    pallas_call x1, Pallas kernels, mlp_call(): pl.pallas_call(mlp_kernel, grid_spec=pltpu.PrefetchScalarGridSpec(num_sca...  14.4 us
    all_to_all x1, waiting for transfers between devices, on_device(): both = lax.all_to_all(both, 'mp', split_axis=0, concat_axis=0)  11.7 us
    all_to_all x1, starting transfers between devices, on_device(): both = lax.all_to_all(both, 'mp', split_axis=0, concat_axis=0)  7.06 us
    all_to_all x1, starting transfers between devices, gather_codes(): lax.all_to_all(jnp.broadcast_to(code_rows, (16, count, width)), 'mp', spl...  6.73 us
    all_to_all x1, starting transfers between devices, scatter_codes(): got = lax.all_to_all(part, 'mp', split_axis=0, concat_axis=0)  6.7 us
    pallas_call x1, Pallas kernels, tied_call(): pl.pallas_call(tied_kernel, grid_spec=pltpu.PrefetchScalarGridSpec(num_sc...  5.61 us
  transfers between devices with their start and end apart: 38, of which 13 were waited for; matrix products, arithmetic and copies ran while one was open for 14% of the time, Pallas kernels for 4%

profile of v3, /device:TPU:2, one launch (start us, length us, event | category | flops | bytes accessed | tf_op | source)
XLA Modules:
  0.0 183.8 jit_solution(2090984960912040534)
XLA Ops:
  0.6 7.3 %collective-permute-start = (bf16[192,384]{1,0:T(8,128)(2,1)}, bf16[192,384]{1,0:T(8,128)(2,1)S(1)}, u32[]{:S(2)}, u32[]{:S(2)}) collective-permute-start(bf16[192,384]{1,0:T(8,128)(2,1)} %encoder.1), channel_id=1, source_target_pairs={{0,128},{16,144},{32,160},{48,176},{64,192},{80,208},{96,224},{112... | collective-permute-start | bytes 442376 | tf_op jit(solution)/shard_map/ppermute | solution.py:33
  7.9 1.1 convert_reduce_fusion.1
  9.0 1.2 fusion.17
  10.2 1.1 fusion.11
  11.3 0.7 collective-permute-done
  12.1 4.1 %collective-permute-start.6 = (bf16[32,3072]{1,0:T(8,128)(2,1)}, bf16[32,3072]{1,0:T(8,128)(2,1)S(1)}, u32[]{:S(2)}, u32[]{:S(2)}) collective-permute-start(bf16[32,3072]{1,0:T(8,128)(2,1)} %param.11), channel_id=1, source_target_pairs={{0,4},{1,5},{2,6},{3,7},{4,8},{5,9},{6,10},{7,11},{8,12},{9,13},{1... | collective-permute-start | bytes 589832 | tf_op jit(solution)/shard_map/ppermute | solution.py:33
  16.2 1.5 collective-permute-start.5
  17.6 2.3 %collective-permute-start.4 = (bf16[32,3072]{1,0:T(8,128)(2,1)}, bf16[32,3072]{1,0:T(8,128)(2,1)S(1)}, u32[]{:S(2)}, u32[]{:S(2)}) collective-permute-start(bf16[32,3072]{1,0:T(8,128)(2,1)} %param.11), channel_id=1, source_target_pairs={{0,12},{1,13},{2,14},{3,15},{4,0},{5,1},{6,2},{7,3},{8,4},{9,5},{1... | collective-permute-start | bytes 589832 | tf_op jit(solution)/shard_map/ppermute | solution.py:33
  19.9 0.9 select_bitcast_fusion.1
  20.9 2.2 %collective-permute-start.2 = (bf16[2,192,384]{2,1,0:T(8,128)(2,1)S(1)}, bf16[2,192,384]{2,1,0:T(8,128)(2,1)S(1)}, u32[]{:S(2)}, u32[]{:S(2)}) collective-permute-start(bf16[2,192,384]{2,1,0:T(8,128)(2,1)S(1)} %pad_maximum_fusion.3), channel_id=1, source_target_pairs={{0,64},{16,80},{32,96},{48,112},{64,0},{80,16},{96,32},{112,48},{1... | collective-permute-start | bytes 884744 | tf_op jit(solution)/shard_map/ppermute | solution.py:33
  23.1 1.4 collective-permute-start.1
  26.2 3.2 %collective-permute-done.5 = bf16[32,3072]{1,0:T(8,128)(2,1)S(1)} collective-permute-done((bf16[32,3072]{1,0:T(8,128)(2,1)}, bf16[32,3072]{1,0:T(8,128)(2,1)S(1)}, u32[]{:S(2)}, u32[]{:S(2)}) %collective-permute-start.5) | collective-permute-done | bytes 196640 | tf_op jit(solution)/shard_map/ppermute | solution.py:33
  29.5 1.0 pad_maximum_fusion.refs_0_
  30.4 5.7 %collective-permute-done.1 = bf16[2,192,384]{2,1,0:T(8,128)(2,1)S(1)} collective-permute-done((bf16[2,192,384]{2,1,0:T(8,128)(2,1)S(1)}, bf16[2,192,384]{2,1,0:T(8,128)(2,1)S(1)}, u32[]{:S(2)}, u32[]{:S(2)}) %collective-permute-start.1) | collective-permute-done | bytes 294944 | tf_op jit(solution)/shard_map/ppermute | solution.py:33
  37.5 1.7 collective-permute-start.10
  39.1 1.7 collective-permute-start.9
  41.4 0.8 broadcast_in_dim.2
  42.2 6.7 %all-to-all-start = ((bf16[16,32,384]{2,1,0:T(8,128)(2,1)}), bf16[16,32,384]{2,1,0:T(8,128)(2,1)S(1)}, u32[]{:S(2)}, u32[]{:S(2)}) async-start(bf16[16,32,384]{2,1,0:T(8,128)(2,1)} %broadcast_in_dim.2), calls=%async_computation | async-start | bytes 786432 | tf_op jit(solution)/shard_map/all_to_all | solution.py:74
  49.2 1.8 collective-permute-start.13
  51.0 1.2 collective-permute-start.12
  52.2 1.8 collective-permute-start.11
  54.1 2.7 %collective-permute-done.12 = bf16[2,2,32,192]{3,2,1,0:T(8,128)(2,1)S(1)} collective-permute-done((bf16[2,2,32,192]{3,2,1,0:T(8,128)(2,1)S(1)}, bf16[2,2,32,192]{3,2,1,0:T(8,128)(2,1)S(1)}, u32[]{:S(2)}, u32[]{:S(2)}) %collective-permute-start.12) | collective-permute-done | bytes 49184 | tf_op jit(solution)/shard_map/ppermute | solution.py:33
  56.8 5.7 %collective-permute-done.10.refs_4_ = bf16[128,3072]{1,0:T(8,128)(2,1)} collective-permute-done((bf16[128,3072]{1,0:T(8,128)(2,1)}, bf16[128,3072]{1,0:T(8,128)(2,1)}, u32[]{:S(2)}, u32[]{:S(2)}) %collective-permute-start.10) | collective-permute-done | bytes 786464 | tf_op jit(solution)/shard_map/ppermute | solution.py:33
  62.8 1.0 slice.100
  63.8 1.0 slice.101
  64.8 1.6 collective-permute-start.15
  66.5 1.7 collective-permute-start.14
  68.3 5.2 %collective-permute-start.16 = (bf16[2,4,32,192]{3,2,1,0:T(8,128)(2,1)S(1)}, bf16[2,4,32,192]{3,2,1,0:T(8,128)(2,1)S(1)}, u32[]{:S(2)}, u32[]{:S(2)}) collective-permute-start(bf16[2,4,32,192]{3,2,1,0:T(8,128)(2,1)S(1)} %bitcast.142), channel_id=1, source_target_pairs={{0,128},{16,144},{32,160},{48,176},{64,192},{80,208},{96,224},{112... | collective-permute-start | bytes 294920 | tf_op jit(solution)/shard_map/ppermute | solution.py:33
  73.4 2.3 %copy-done = bf16[3072,768]{1,0:T(8,128)(2,1)S(1)} copy-done((bf16[3072,768]{1,0:T(8,128)(2,1)S(1)}, bf16[3072,768]{1,0:T(8,128)(2,1)}, u32[]{:S(2)}) %copy-start) | copy-done | bytes 4718616
  75.8 5.6 %shard_map.101.tied = bf16[384,768]{1,0:T(8,128)(2,1)S(1)} custom-call(s32[6]{0:T(128)S(1)} %stack.110.at, bf16[8,192,384]{2,1,0:T(8,128)(2,1)S(1)} %bitcast.130, bf16[8,192,384]{2,1,0:T(8,128)(2,1)S(1)} %bitcast.132, bf16[3072,768]{1,0:T(8,128)(2,1)S(1)} %copy-done), custom_call_target="tpu_custom_call" | custom-call | flops 1811939328 | bytes 9437184 | tf_op jit(solution)/shard_map/pallas_call | solution.py:249
  81.4 0.8 copy-done.2
  82.2 0.8 copy-done.20
  83.0 0.8 copy-done.15
  83.8 14.4 %shard_map.102 = (bf16[4,2,192,768]{3,2,1,0:T(8,128)(2,1)}, bf16[4,2,192,768]{3,2,1,0:T(8,128)(2,1)}, bf16[16,32,384]{2,1,0:T(8,128)(2,1)}, bf16[2,4,48,768]{3,2,1,0:T(8,128)(2,1)}) custom-call(s32[6]{0:T(128)} %copy-done.3, bf16[16,32,384]{2,1,0:T(8,128)(2,1)} %copy-done.15, bf16[384,768]{1,0:T(8,128)(2,1)} %copy-done.2, bf16[3072,768]{1,0:T(8,128)(2,1)} %w_down.1, ...), custom_call_target="tpu_custom_call" | custom-call | flops 5435817984 | bytes 17301504 | tf_op jit(solution)/shard_map/pallas_call | solution.py:191
  98.4 1.7 slice_bitcast_fusion
  101.3 6.7 %all-to-all-start.1 = ((bf16[16,32,384]{2,1,0:T(8,128)(2,1)}), bf16[16,32,384]{2,1,0:T(8,128)(2,1)S(1)}, u32[]{:S(2)}, u32[]{:S(2)}) async-start(bf16[16,32,384]{2,1,0:T(8,128)(2,1)} %get-tuple-element.64), calls=%async_computation.1 | async-start | bytes 786432 | tf_op jit(solution)/shard_map/all_to_all | solution.py:80
  108.1 1.0 fusion.1
  109.2 2.9 %fusion.21 = (bf16[1,192,768]{2,1,0:T(8,128)(2,1)}, bf16[1,192,768]{2,1,0:T(8,128)(2,1)}, bf16[192,768]{1,0:T(8,128)(2,1)}, bf16[192,768]{1,0:T(8,128)(2,1)}) fusion(bf16[4,2,192,768]{3,2,1,0:T(8,128)(2,1)} %collective-permute-done.17, bf16[4,2,192,768]{3,2,1,0:T(8,128)(2,1)} %get-tuple-element.58), kind=kLoop, calls=%fused_computation.49 | loop fusion | flops 2359296 | bytes 3538944 | tf_op jit(solution)/shard_map/convert_element_type | solution.py:392
  112.8 1.5 collective-permute-start.21
  114.8 2.1 %collective-permute-start.22 = (bf16[48,768]{1,0:T(8,128)(2,1)}, bf16[48,768]{1,0:T(8,128)(2,1)}, u32[]{:S(2)}, u32[]{:S(2)}) collective-permute-start(bf16[48,768]{1,0:T(8,128)(2,1)} %get-tuple-element.93), channel_id=1, source_target_pairs={{0,64},{16,80},{32,96},{48,112},{64,0},{80,16},{96,32},{112,48},{1... | collective-permute-start | bytes 221192 | tf_op jit(solution)/shard_map/ppermute | solution.py:33
  116.9 2.6 %collective-permute-start.19 = (bf16[192,768]{1,0:T(8,128)(2,1)}, bf16[192,768]{1,0:T(8,128)(2,1)}, u32[]{:S(2)}, u32[]{:S(2)}) collective-permute-start(bf16[192,768]{1,0:T(8,128)(2,1)} %get-tuple-element.61), channel_id=1, source_target_pairs={{0,32},{16,48},{32,64},{48,80},{64,96},{80,112},{96,0},{112,16},{1... | collective-permute-start | bytes 884744 | tf_op jit(solution)/shard_map/ppermute | solution.py:33
  119.6 1.8 all-to-all-done.1
  122.1 1.1 fusion.24
  123.2 3.2 %collective-permute-done.19 = bf16[192,768]{1,0:T(8,128)(2,1)} collective-permute-done((bf16[192,768]{1,0:T(8,128)(2,1)}, bf16[192,768]{1,0:T(8,128)(2,1)}, u32[]{:S(2)}, u32[]{:S(2)}) %collective-permute-start.19) | collective-permute-done | bytes 294944 | tf_op jit(solution)/shard_map/ppermute | solution.py:33
  126.4 1.2 collective-permute-done.20
  127.5 0.7 fusion.37
  128.3 1.8 fusion.23
  130.2 0.8 collective-permute-start.26
  131.7 1.3 collective-permute-start.25
  133.1 1.7 fusion.36
  134.8 4.1 %collective-permute-done.26 = bf16[64,768]{1,0:T(8,128)(2,1)S(1)} collective-permute-done((bf16[64,768]{1,0:T(8,128)(2,1)S(1)}, bf16[64,768]{1,0:T(8,128)(2,1)S(1)}, u32[]{:S(2)}, u32[]{:S(2)}) %collective-permute-start.26) | collective-permute-done | bytes 98336 | tf_op jit(solution)/shard_map/ppermute | solution.py:33
  138.9 2.0 %collective-permute-start.29 = (bf16[80,768]{1,0:T(8,128)(2,1)S(1)}, bf16[80,768]{1,0:T(8,128)(2,1)S(1)}, u32[]{:S(2)}, u32[]{:S(2)}) collective-permute-start(bf16[80,768]{1,0:T(8,128)(2,1)S(1)} %pad_maximum_fusion.6.refs_0_), channel_id=1, source_target_pairs={{0,32},{16,48},{32,64},{48,80},{64,96},{80,112},{96,0},{112,16},{1... | collective-permute-start | bytes 368648 | tf_op jit(solution)/shard_map/ppermute | solution.py:33
  141.0 2.0 %collective-permute-start.28 = (bf16[80,768]{1,0:T(8,128)(2,1)S(1)}, bf16[80,768]{1,0:T(8,128)(2,1)S(1)}, u32[]{:S(2)}, u32[]{:S(2)}) collective-permute-start(bf16[80,768]{1,0:T(8,128)(2,1)S(1)} %pad_maximum_fusion.6.refs_0_), channel_id=1, source_target_pairs={{0,64},{16,80},{32,96},{48,112},{64,0},{80,16},{96,32},{112,48},{1... | collective-permute-start | bytes 368648 | tf_op jit(solution)/shard_map/ppermute | solution.py:33
  143.0 1.1 collective-permute-start.27
  144.1 4.7 %collective-permute-done.29.refs_3_ = bf16[80,768]{1,0:T(8,128)(2,1)S(1)} collective-permute-done((bf16[80,768]{1,0:T(8,128)(2,1)S(1)}, bf16[80,768]{1,0:T(8,128)(2,1)S(1)}, u32[]{:S(2)}, u32[]{:S(2)}) %collective-permute-start.29) | collective-permute-done | bytes 122912 | tf_op jit(solution)/shard_map/ppermute | solution.py:33
  148.9 1.8 collective-permute-done.28.refs_2_
  151.8 1.2 fusion.2
  153.0 5.3 %collective-permute-start.34 = (bf16[192,768]{1,0:T(8,128)(2,1)S(1)}, bf16[192,768]{1,0:T(8,128)(2,1)S(1)}, u32[]{:S(2)}, u32[]{:S(2)}) collective-permute-start(bf16[192,768]{1,0:T(8,128)(2,1)S(1)} %fusion.2), channel_id=1, source_target_pairs={{0,128},{16,144},{32,160},{48,176},{64,192},{80,208},{96,224},{112... | collective-permute-start | bytes 884744 | tf_op jit(solution)/shard_map/ppermute | solution.py:33
  158.4 2.1 %shard_map.103 = (bf16[16,12,768]{2,1,0:T(8,128)(2,1)}, f32[192,768]{1,0:T(8,128)}) custom-call(s32[6]{0:T(128)S(1)} %copy-done.4, bf16[512,192]{1,0:T(8,128)(2,1)S(1)} %bitcast.133, bf16[3072,768]{1,0:T(8,128)(2,1)S(1)} %bitcast.127, bf16[192,384]{1,0:T(8,128)(2,1)S(1)} %copy-done.1, bf16[80,768]{1,0:T(8,128)(2,1)S(1)} %pad_maximum_fusion.6.refs_0_, ...), custom_call_target="tpu_custom_call" | custom-call | flops 301989888 | bytes 1081344 | tf_op jit(solution)/shard_map/pallas_call | solution.py:305
  160.5 7.1 %all-to-all-start.2 = ((bf16[16,12,768]{2,1,0:T(8,128)(2,1)}), bf16[16,12,768]{2,1,0:T(8,128)(2,1)S(1)}, u32[]{:S(2)}, u32[]{:S(2)}) async-start(bf16[16,12,768]{2,1,0:T(8,128)(2,1)} %get-tuple-element.80), calls=%async_computation.2 | async-start | bytes 786432 | tf_op jit(solution)/shard_map/all_to_all | solution.py:408
  167.6 0.9 fusion.16
  168.5 2.2 %fusion.3 = f32[192,768]{1,0:T(8,128)} fusion(bf16[192,768]{1,0:T(8,128)(2,1)S(1)} %collective-permute-done.34, bf16[4,2,192,768]{3,2,1,0:T(8,128)(2,1)} %collective-permute-done.17, bf16[2,192,768]{2,1,0:T(8,128)(2,1)} %copy-done.14, bf16[2,192,768]{2,1,0:T(8,128)(2,1)} %copy-done.13, bf16[4,2,192,768]{3,2,1,0:T(8,128)(2,1)} %get-tuple-element.58), kind=kLoop, calls=%fused_computation.15 | loop fusion | flops 1327104 | bytes 2064384 | tf_op jit(solution)/shard_map/add | solution.py:405
  170.7 11.7 %all-to-all-done.2 = bf16[16,12,768]{2,1,0:T(8,128)(2,1)S(1)} async-done(((bf16[16,12,768]{2,1,0:T(8,128)(2,1)}), bf16[16,12,768]{2,1,0:T(8,128)(2,1)S(1)}, u32[]{:S(2)}, u32[]{:S(2)}) %all-to-all-start.2) | async-done | bytes 294944 | tf_op jit(solution)/shard_map/all_to_all | solution.py:408
  182.4 0.7 multiply_reduce_fusion
  (127 shorter events, 10.3 us)
Async XLA Ops:
  0.6 11.4 %collective-permute-start = (bf16[192,384]{1,0:T(8,128)(2,1)}, bf16[192,384]{1,0:T(8,128)(2,1)S(1)}, u32[]{:S(2)}, u32[]{:S(2)}) collective-permute-start(bf16[192,384]{1,0:T(8,128)(2,1)} %encoder.1), channel_id=1, source_target_pairs={{0,128},{16,144},{32,160},{48,176},{64,192},{80,208},{96,224},{112... | collective-permute-start | bytes 442376 | tf_op jit(solution)/shard_map/ppermute | solution.py:33
  10.1 19.3 %copy-start.10 = (bf16[32,3072]{1,0:T(8,128)(2,1)S(1)}, bf16[32,3072]{1,0:T(8,128)(2,1)}, u32[]{:S(2)}) copy-start(bf16[32,3072]{1,0:T(8,128)(2,1)} %param.11) | copy-start | bytes 589828
  12.1 13.5 %collective-permute-start.6 = (bf16[32,3072]{1,0:T(8,128)(2,1)}, bf16[32,3072]{1,0:T(8,128)(2,1)S(1)}, u32[]{:S(2)}, u32[]{:S(2)}) collective-permute-start(bf16[32,3072]{1,0:T(8,128)(2,1)} %param.11), channel_id=1, source_target_pairs={{0,4},{1,5},{2,6},{3,7},{4,8},{5,9},{6,10},{7,11},{8,12},{9,13},{1... | collective-permute-start | bytes 589832 | tf_op jit(solution)/shard_map/ppermute | solution.py:33
  16.2 13.3 %collective-permute-start.5 = (bf16[32,3072]{1,0:T(8,128)(2,1)}, bf16[32,3072]{1,0:T(8,128)(2,1)S(1)}, u32[]{:S(2)}, u32[]{:S(2)}) collective-permute-start(bf16[32,3072]{1,0:T(8,128)(2,1)} %param.11), channel_id=1, source_target_pairs={{0,8},{1,9},{2,10},{3,11},{4,12},{5,13},{6,14},{7,15},{8,0},{9,1},... | collective-permute-start | bytes 589832 | tf_op jit(solution)/shard_map/ppermute | solution.py:33
  17.6 11.8 %collective-permute-start.4 = (bf16[32,3072]{1,0:T(8,128)(2,1)}, bf16[32,3072]{1,0:T(8,128)(2,1)S(1)}, u32[]{:S(2)}, u32[]{:S(2)}) collective-permute-start(bf16[32,3072]{1,0:T(8,128)(2,1)} %param.11), channel_id=1, source_target_pairs={{0,12},{1,13},{2,14},{3,15},{4,0},{5,1},{6,2},{7,3},{8,4},{9,5},{1... | collective-permute-start | bytes 589832 | tf_op jit(solution)/shard_map/ppermute | solution.py:33
  20.9 15.3 %collective-permute-start.2 = (bf16[2,192,384]{2,1,0:T(8,128)(2,1)S(1)}, bf16[2,192,384]{2,1,0:T(8,128)(2,1)S(1)}, u32[]{:S(2)}, u32[]{:S(2)}) collective-permute-start(bf16[2,192,384]{2,1,0:T(8,128)(2,1)S(1)} %pad_maximum_fusion.3), channel_id=1, source_target_pairs={{0,64},{16,80},{32,96},{48,112},{64,0},{80,16},{96,32},{112,48},{1... | collective-permute-start | bytes 884744 | tf_op jit(solution)/shard_map/ppermute | solution.py:33
  23.1 13.0 %collective-permute-start.1 = (bf16[2,192,384]{2,1,0:T(8,128)(2,1)S(1)}, bf16[2,192,384]{2,1,0:T(8,128)(2,1)S(1)}, u32[]{:S(2)}, u32[]{:S(2)}) collective-permute-start(bf16[2,192,384]{2,1,0:T(8,128)(2,1)S(1)} %pad_maximum_fusion.3), channel_id=1, source_target_pairs={{0,96},{16,112},{32,0},{48,16},{64,32},{80,48},{96,64},{112,80},{1... | collective-permute-start | bytes 884744 | tf_op jit(solution)/shard_map/ppermute | solution.py:33
  25.6 10.7 %collective-permute-start.3 = (bf16[2,192,384]{2,1,0:T(8,128)(2,1)S(1)}, bf16[2,192,384]{2,1,0:T(8,128)(2,1)S(1)}, u32[]{:S(2)}, u32[]{:S(2)}) collective-permute-start(bf16[2,192,384]{2,1,0:T(8,128)(2,1)S(1)} %pad_maximum_fusion.3), channel_id=1, source_target_pairs={{0,32},{16,48},{32,64},{48,80},{64,96},{80,112},{96,0},{112,16},{1... | collective-permute-start | bytes 884744 | tf_op jit(solution)/shard_map/ppermute | solution.py:33
  29.5 7.2 %collective-permute-start.7 = (bf16[4,2,32,192]{3,2,1,0:T(8,128)(2,1)S(1)}, bf16[4,2,32,192]{3,2,1,0:T(8,128)(2,1)S(1)}, u32[]{:S(2)}, u32[]{:S(2)}) collective-permute-start(bf16[4,2,32,192]{3,2,1,0:T(8,128)(2,1)S(1)} %bitcast.141), channel_id=1, source_target_pairs={{0,16},{16,0},{32,48},{48,32},{64,80},{80,64},{96,112},{112,96},{1... | collective-permute-start | bytes 294920 | tf_op jit(solution)/shard_map/ppermute | solution.py:33
  36.6 4.2 %collective-permute-start.8 = (bf16[1536,384]{1,0:T(8,128)(2,1)S(1)}, bf16[1536,384]{1,0:T(8,128)(2,1)S(1)}, u32[]{:S(2)}, u32[]{:S(2)}) collective-permute-start(bf16[1536,384]{1,0:T(8,128)(2,1)S(1)} %bitcast.128), channel_id=1, source_target_pairs={{0,16},{16,0},{32,48},{48,32},{64,80},{80,64},{96,112},{112,96},{1... | collective-permute-start | bytes 3538952 | tf_op jit(solution)/shard_map/ppermute | solution.py:33
  37.5 25.0 %collective-permute-start.10 = (bf16[128,3072]{1,0:T(8,128)(2,1)}, bf16[128,3072]{1,0:T(8,128)(2,1)}, u32[]{:S(2)}, u32[]{:S(2)}) collective-permute-start(bf16[128,3072]{1,0:T(8,128)(2,1)} %pad_maximum_fusion.refs_0_), channel_id=1, source_target_pairs={{0,1},{1,2},{2,3},{3,0},{4,5},{5,6},{6,7},{7,4},{8,9},{9,10},{10,1... | collective-permute-start | bytes 2359304 | tf_op jit(solution)/shard_map/ppermute | solution.py:33
  39.1 23.7 %collective-permute-start.9 = (bf16[128,3072]{1,0:T(8,128)(2,1)}, bf16[128,3072]{1,0:T(8,128)(2,1)}, u32[]{:S(2)}, u32[]{:S(2)}) collective-permute-start(bf16[128,3072]{1,0:T(8,128)(2,1)} %pad_maximum_fusion.refs_0_), channel_id=1, source_target_pairs={{0,3},{1,0},{2,1},{3,2},{4,7},{5,4},{6,5},{7,6},{8,11},{9,8},{10,9... | collective-permute-start | bytes 2359304 | tf_op jit(solution)/shard_map/ppermute | solution.py:33
  42.2 40.8 %all-to-all-start = ((bf16[16,32,384]{2,1,0:T(8,128)(2,1)}), bf16[16,32,384]{2,1,0:T(8,128)(2,1)S(1)}, u32[]{:S(2)}, u32[]{:S(2)}) async-start(bf16[16,32,384]{2,1,0:T(8,128)(2,1)} %broadcast_in_dim.2), calls=%async_computation | async-start | bytes 786432 | tf_op jit(solution)/shard_map/all_to_all | solution.py:74
  49.2 4.9 %collective-permute-start.13 = (bf16[2,2,32,192]{3,2,1,0:T(8,128)(2,1)S(1)}, bf16[2,2,32,192]{3,2,1,0:T(8,128)(2,1)S(1)}, u32[]{:S(2)}, u32[]{:S(2)}) collective-permute-start(bf16[2,2,32,192]{3,2,1,0:T(8,128)(2,1)S(1)} %bitcast.147), channel_id=1, source_target_pairs={{0,96},{16,112},{32,0},{48,16},{64,32},{80,48},{96,64},{112,80},{1... | collective-permute-start | bytes 147464 | tf_op jit(solution)/shard_map/ppermute | solution.py:33
  51.0 5.8 %collective-permute-start.12 = (bf16[2,2,32,192]{3,2,1,0:T(8,128)(2,1)S(1)}, bf16[2,2,32,192]{3,2,1,0:T(8,128)(2,1)S(1)}, u32[]{:S(2)}, u32[]{:S(2)}) collective-permute-start(bf16[2,2,32,192]{3,2,1,0:T(8,128)(2,1)S(1)} %bitcast.146), channel_id=1, source_target_pairs={{0,64},{16,80},{32,96},{48,112},{64,0},{80,16},{96,32},{112,48},{1... | collective-permute-start | bytes 147464 | tf_op jit(solution)/shard_map/ppermute | solution.py:33
  52.2 4.6 %collective-permute-start.11 = (bf16[2,2,32,192]{3,2,1,0:T(8,128)(2,1)S(1)}, bf16[2,2,32,192]{3,2,1,0:T(8,128)(2,1)S(1)}, u32[]{:S(2)}, u32[]{:S(2)}) collective-permute-start(bf16[2,2,32,192]{3,2,1,0:T(8,128)(2,1)S(1)} %bitcast.145), channel_id=1, source_target_pairs={{0,32},{16,48},{32,64},{48,80},{64,96},{80,112},{96,0},{112,16},{1... | collective-permute-start | bytes 147464 | tf_op jit(solution)/shard_map/ppermute | solution.py:33
  54.1 27.3 %copy-start.3 = (s32[6]{0:T(128)}, s32[6]{0:T(128)S(1)}, u32[]{:S(2)}) copy-start(s32[6]{0:T(128)S(1)} %stack.110.at) | copy-start | bytes 76
  64.8 17.4 %collective-permute-start.15 = (bf16[64,3072]{1,0:T(8,128)(2,1)S(1)}, bf16[64,3072]{1,0:T(8,128)(2,1)S(1)}, u32[]{:S(2)}, u32[]{:S(2)}) collective-permute-start(bf16[64,3072]{1,0:T(8,128)(2,1)S(1)} %slice.101), channel_id=1, source_target_pairs={{0,1},{1,2},{2,3},{3,0},{4,5},{5,6},{6,7},{7,4},{8,9},{9,10},{10,1... | collective-permute-start | bytes 1179656 | tf_op jit(solution)/shard_map/ppermute | solution.py:33
  66.5 16.6 %collective-permute-start.14 = (bf16[64,3072]{1,0:T(8,128)(2,1)S(1)}, bf16[64,3072]{1,0:T(8,128)(2,1)}, u32[]{:S(2)}, u32[]{:S(2)}) collective-permute-start(bf16[64,3072]{1,0:T(8,128)(2,1)S(1)} %slice.100), channel_id=1, source_target_pairs={{0,3},{1,0},{2,1},{3,2},{4,7},{5,4},{6,5},{7,6},{8,11},{9,8},{10,9... | collective-permute-start | bytes 1179656 | tf_op jit(solution)/shard_map/ppermute | solution.py:33
  68.3 13.9 %collective-permute-start.16 = (bf16[2,4,32,192]{3,2,1,0:T(8,128)(2,1)S(1)}, bf16[2,4,32,192]{3,2,1,0:T(8,128)(2,1)S(1)}, u32[]{:S(2)}, u32[]{:S(2)}) collective-permute-start(bf16[2,4,32,192]{3,2,1,0:T(8,128)(2,1)S(1)} %bitcast.142), channel_id=1, source_target_pairs={{0,128},{16,144},{32,160},{48,176},{64,192},{80,208},{96,224},{112... | collective-permute-start | bytes 294920 | tf_op jit(solution)/shard_map/ppermute | solution.py:33
  73.4 2.3 %copy-start = (bf16[3072,768]{1,0:T(8,128)(2,1)S(1)}, bf16[3072,768]{1,0:T(8,128)(2,1)}, u32[]{:S(2)}) copy-start(bf16[3072,768]{1,0:T(8,128)(2,1)} %w_up.3) | copy-start | bytes 14155780
  81.4 0.8 copy-start.2
  82.2 16.1 %copy-start.17 = (bf16[2,4,32,192]{3,2,1,0:T(8,128)(2,1)}, bf16[2,4,32,192]{3,2,1,0:T(8,128)(2,1)S(1)}, u32[]{:S(2)}) copy-start(bf16[2,4,32,192]{3,2,1,0:T(8,128)(2,1)S(1)} %collective-permute-done.16) | copy-start | bytes 294916
  82.2 0.8 copy-start.20
  83.0 0.8 copy-start.15
  98.3 10.9 %collective-permute-start.17 = (bf16[4,2,192,768]{3,2,1,0:T(8,128)(2,1)}, bf16[4,2,192,768]{3,2,1,0:T(8,128)(2,1)}, u32[]{:S(2)}, u32[]{:S(2)}) collective-permute-start(bf16[4,2,192,768]{3,2,1,0:T(8,128)(2,1)} %get-tuple-element.59), channel_id=1, source_target_pairs={{0,16},{16,0},{32,48},{48,32},{64,80},{80,64},{96,112},{112,96},{1... | collective-permute-start | bytes 7077896 | tf_op jit(solution)/shard_map/ppermute | solution.py:33
  100.1 8.0 %collective-permute-start.18 = (bf16[4,48,768]{2,1,0:T(8,128)(2,1)}, bf16[4,48,768]{2,1,0:T(8,128)(2,1)}, u32[]{:S(2)}, u32[]{:S(2)}) collective-permute-start(bf16[4,48,768]{2,1,0:T(8,128)(2,1)} %slice_bitcast_fusion), channel_id=1, source_target_pairs={{0,16},{16,0},{32,48},{48,32},{64,80},{80,64},{96,112},{112,96},{1... | collective-permute-start | bytes 884744 | tf_op jit(solution)/shard_map/ppermute | solution.py:33
  101.1 7.0 %copy-start.12 = (bf16[2,4,48,768]{3,2,1,0:T(8,128)(2,1)S(1)}, bf16[2,4,48,768]{3,2,1,0:T(8,128)(2,1)}, u32[]{:S(2)}) copy-start(bf16[2,4,48,768]{3,2,1,0:T(8,128)(2,1)} %get-tuple-element.60) | copy-start | bytes 1769476
  101.3 20.0 %all-to-all-start.1 = ((bf16[16,32,384]{2,1,0:T(8,128)(2,1)}), bf16[16,32,384]{2,1,0:T(8,128)(2,1)S(1)}, u32[]{:S(2)}, u32[]{:S(2)}) async-start(bf16[16,32,384]{2,1,0:T(8,128)(2,1)} %get-tuple-element.64), calls=%async_computation.1 | async-start | bytes 786432 | tf_op jit(solution)/shard_map/all_to_all | solution.py:80
  109.1 10.5 %copy-start.9 = (bf16[4,48,768]{2,1,0:T(8,128)(2,1)}, bf16[4,48,768]{2,1,0:T(8,128)(2,1)S(1)}, u32[]{:S(2)}) copy-start(bf16[4,48,768]{2,1,0:T(8,128)(2,1)S(1)} %fusion.1) | copy-start | bytes 884740
  109.1 10.4 %copy-start.18 = (bf16[2,4,32,192]{3,2,1,0:T(8,128)(2,1)S(1)}, bf16[2,4,32,192]{3,2,1,0:T(8,128)(2,1)}, u32[]{:S(2)}) copy-start(bf16[2,4,32,192]{3,2,1,0:T(8,128)(2,1)} %copy-done.17) | copy-start | bytes 294916
  109.2 49.2 %slice-start = ((s8[4718592]{0:T(1024)(128)(4,1)}), s8[524288]{0:T(1024)(128)(4,1)S(1)}, s32[]{:S(2)}) async-start(s8[4718592]{0:T(1024)(128)(4,1)} %bitcast.126), calls=%async_computation.3 | async-start | bytes 1048576
  112.8 9.3 %collective-permute-start.21 = (bf16[48,768]{1,0:T(8,128)(2,1)}, bf16[48,768]{1,0:T(8,128)(2,1)}, u32[]{:S(2)}, u32[]{:S(2)}) collective-permute-start(bf16[48,768]{1,0:T(8,128)(2,1)} %get-tuple-element.91), channel_id=1, source_target_pairs={{0,32},{16,48},{32,64},{48,80},{64,96},{80,112},{96,0},{112,16},{1... | collective-permute-start | bytes 221192 | tf_op jit(solution)/shard_map/ppermute | solution.py:33
  114.3 7.8 %collective-permute-start.23 = (bf16[48,768]{1,0:T(8,128)(2,1)}, bf16[48,768]{1,0:T(8,128)(2,1)}, u32[]{:S(2)}, u32[]{:S(2)}) collective-permute-start(bf16[48,768]{1,0:T(8,128)(2,1)} %get-tuple-element.92), channel_id=1, source_target_pairs={{0,96},{16,112},{32,0},{48,16},{64,32},{80,48},{96,64},{112,80},{1... | collective-permute-start | bytes 221192 | tf_op jit(solution)/shard_map/ppermute | solution.py:33
  114.8 7.2 %collective-permute-start.22 = (bf16[48,768]{1,0:T(8,128)(2,1)}, bf16[48,768]{1,0:T(8,128)(2,1)}, u32[]{:S(2)}, u32[]{:S(2)}) collective-permute-start(bf16[48,768]{1,0:T(8,128)(2,1)} %get-tuple-element.93), channel_id=1, source_target_pairs={{0,64},{16,80},{32,96},{48,112},{64,0},{80,16},{96,32},{112,48},{1... | collective-permute-start | bytes 221192 | tf_op jit(solution)/shard_map/ppermute | solution.py:33
  116.9 9.4 %collective-permute-start.19 = (bf16[192,768]{1,0:T(8,128)(2,1)}, bf16[192,768]{1,0:T(8,128)(2,1)}, u32[]{:S(2)}, u32[]{:S(2)}) collective-permute-start(bf16[192,768]{1,0:T(8,128)(2,1)} %get-tuple-element.61), channel_id=1, source_target_pairs={{0,32},{16,48},{32,64},{48,80},{64,96},{80,112},{96,0},{112,16},{1... | collective-permute-start | bytes 884744 | tf_op jit(solution)/shard_map/ppermute | solution.py:33
  119.5 8.0 %collective-permute-start.20 = (bf16[192,768]{1,0:T(8,128)(2,1)}, bf16[192,768]{1,0:T(8,128)(2,1)}, u32[]{:S(2)}, u32[]{:S(2)}) collective-permute-start(bf16[192,768]{1,0:T(8,128)(2,1)} %get-tuple-element.62), channel_id=1, source_target_pairs={{0,96},{16,112},{32,0},{48,16},{64,32},{80,48},{96,64},{112,80},{1... | collective-permute-start | bytes 884744 | tf_op jit(solution)/shard_map/ppermute | solution.py:33
  122.1 8.0 %copy-start.7 = (bf16[1,192,768]{2,1,0:T(8,128)(2,1)S(1)}, bf16[1,192,768]{2,1,0:T(8,128)(2,1)}, u32[]{:S(2)}) copy-start(bf16[1,192,768]{2,1,0:T(8,128)(2,1)} %get-tuple-element.83) | copy-start | bytes 884740
  122.1 8.0 %copy-start.8 = (bf16[1,192,768]{2,1,0:T(8,128)(2,1)S(1)}, bf16[1,192,768]{2,1,0:T(8,128)(2,1)}, u32[]{:S(2)}) copy-start(bf16[1,192,768]{2,1,0:T(8,128)(2,1)} %get-tuple-element.84) | copy-start | bytes 884740
  128.3 4.8 %copy-start.5 = (bf16[32,3072]{1,0:T(8,128)(2,1)S(1)}, bf16[32,3072]{1,0:T(8,128)(2,1)}, u32[]{:S(2)}) copy-start(bf16[32,3072]{1,0:T(8,128)(2,1)} %param.6) | copy-start | bytes 589828
  128.3 4.8 %copy-start.16 = (bf16[32,384]{1,0:T(8,128)(2,1)S(1)}, bf16[32,384]{1,0:T(8,128)(2,1)}, u32[]{:S(2)}) copy-start(bf16[32,384]{1,0:T(8,128)(2,1)} %reduce_sum.68) | copy-start | bytes 73732
  128.3 4.7 %copy-start.19 = (f32[3072]{0:T(1024)S(1)}, f32[3072]{0:T(1024)}, u32[]{:S(2)}) copy-start(f32[3072]{0:T(1024)} %param.7) | copy-start | bytes 36868
  128.3 30.1 %slice-start.1 = ((s8[4718592]{0:T(1024)(128)(4,1)}), s8[4194304]{0:T(1024)(128)(4,1)S(1)}, s32[]{:S(2)}) async-start(s8[4718592]{0:T(1024)(128)(4,1)} %bitcast.126), calls=%async_computation.4 | async-start | bytes 8388608
  130.2 8.7 %collective-permute-start.26 = (bf16[64,768]{1,0:T(8,128)(2,1)S(1)}, bf16[64,768]{1,0:T(8,128)(2,1)S(1)}, u32[]{:S(2)}, u32[]{:S(2)}) collective-permute-start(bf16[64,768]{1,0:T(8,128)(2,1)S(1)} %maximum_maximum_fusion), channel_id=1, source_target_pairs={{0,128},{16,144},{32,160},{48,176},{64,192},{80,208},{96,224},{112... | collective-permute-start | bytes 294920 | tf_op jit(solution)/shard_map/ppermute | solution.py:33
  131.0 19.7 %collective-permute-start.24 = (bf16[2,192,768]{2,1,0:T(8,128)(2,1)S(1)}, bf16[2,192,768]{2,1,0:T(8,128)(2,1)S(1)}, u32[]{:S(2)}, u32[]{:S(2)}) collective-permute-start(bf16[2,192,768]{2,1,0:T(8,128)(2,1)S(1)} %get-tuple-element.70), channel_id=1, source_target_pairs={{0,32},{16,48},{32,64},{48,80},{64,96},{80,112},{96,0},{112,16},{1... | collective-permute-start | bytes 1769480 | tf_op jit(solution)/shard_map/ppermute | solution.py:33
  131.7 18.9 %collective-permute-start.25 = (bf16[2,192,768]{2,1,0:T(8,128)(2,1)S(1)}, bf16[2,192,768]{2,1,0:T(8,128)(2,1)S(1)}, u32[]{:S(2)}, u32[]{:S(2)}) collective-permute-start(bf16[2,192,768]{2,1,0:T(8,128)(2,1)S(1)} %get-tuple-element.71), channel_id=1, source_target_pairs={{0,96},{16,112},{32,0},{48,16},{64,32},{80,48},{96,64},{112,80},{1... | collective-permute-start | bytes 1769480 | tf_op jit(solution)/shard_map/ppermute | solution.py:33
  133.0 25.4 %copy-start.1 = (bf16[192,384]{1,0:T(8,128)(2,1)S(1)}, bf16[192,384]{1,0:T(8,128)(2,1)}, u32[]{:S(2)}) copy-start(bf16[192,384]{1,0:T(8,128)(2,1)} %encoder.1) | copy-start | bytes 442372
  133.0 25.4 %copy-start.4 = (s32[6]{0:T(128)S(1)}, s32[6]{0:T(128)}, u32[]{:S(2)}) copy-start(s32[6]{0:T(128)} %copy-done.3) | copy-start | bytes 76
  138.9 9.9 %collective-permute-start.29 = (bf16[80,768]{1,0:T(8,128)(2,1)S(1)}, bf16[80,768]{1,0:T(8,128)(2,1)S(1)}, u32[]{:S(2)}, u32[]{:S(2)}) collective-permute-start(bf16[80,768]{1,0:T(8,128)(2,1)S(1)} %pad_maximum_fusion.6.refs_0_), channel_id=1, source_target_pairs={{0,32},{16,48},{32,64},{48,80},{64,96},{80,112},{96,0},{112,16},{1... | collective-permute-start | bytes 368648 | tf_op jit(solution)/shard_map/ppermute | solution.py:33
  141.0 9.7 %collective-permute-start.28 = (bf16[80,768]{1,0:T(8,128)(2,1)S(1)}, bf16[80,768]{1,0:T(8,128)(2,1)S(1)}, u32[]{:S(2)}, u32[]{:S(2)}) collective-permute-start(bf16[80,768]{1,0:T(8,128)(2,1)S(1)} %pad_maximum_fusion.6.refs_0_), channel_id=1, source_target_pairs={{0,64},{16,80},{32,96},{48,112},{64,0},{80,16},{96,32},{112,48},{1... | collective-permute-start | bytes 368648 | tf_op jit(solution)/shard_map/ppermute | solution.py:33
  143.0 7.7 %collective-permute-start.27 = (bf16[80,768]{1,0:T(8,128)(2,1)S(1)}, bf16[80,768]{1,0:T(8,128)(2,1)S(1)}, u32[]{:S(2)}, u32[]{:S(2)}) collective-permute-start(bf16[80,768]{1,0:T(8,128)(2,1)S(1)} %pad_maximum_fusion.6.refs_0_), channel_id=1, source_target_pairs={{0,96},{16,112},{32,0},{48,16},{64,32},{80,48},{96,64},{112,80},{1... | collective-permute-start | bytes 368648 | tf_op jit(solution)/shard_map/ppermute | solution.py:33
  150.7 9.8 %copy-start.13 = (bf16[2,192,768]{2,1,0:T(8,128)(2,1)}, bf16[2,192,768]{2,1,0:T(8,128)(2,1)S(1)}, u32[]{:S(2)}) copy-start(bf16[2,192,768]{2,1,0:T(8,128)(2,1)S(1)} %collective-permute-done.24) | copy-start | bytes 1769476
  150.7 9.8 %copy-start.14 = (bf16[2,192,768]{2,1,0:T(8,128)(2,1)}, bf16[2,192,768]{2,1,0:T(8,128)(2,1)S(1)}, u32[]{:S(2)}) copy-start(bf16[2,192,768]{2,1,0:T(8,128)(2,1)S(1)} %collective-permute-done.25) | copy-start | bytes 1769476
  150.7 7.7 %collective-permute-start.30 = (bf16[80,768]{1,0:T(8,128)(2,1)S(1)}, bf16[80,768]{1,0:T(8,128)(2,1)S(1)}, u32[]{:S(2)}, u32[]{:S(2)}) collective-permute-start(bf16[80,768]{1,0:T(8,128)(2,1)S(1)} %pad_maximum_fusion.6.refs_0_), channel_id=1, source_target_pairs={{0,16},{16,0},{32,48},{48,32},{64,80},{80,64},{96,112},{112,96},{1... | collective-permute-start | bytes 368648 | tf_op jit(solution)/shard_map/ppermute | solution.py:33
  150.8 7.6 %collective-permute-start.31 = (bf16[80,768]{1,0:T(8,128)(2,1)S(1)}, bf16[80,768]{1,0:T(8,128)(2,1)S(1)}, u32[]{:S(2)}, u32[]{:S(2)}) collective-permute-start(bf16[80,768]{1,0:T(8,128)(2,1)S(1)} %collective-permute-done.27.refs_1_), channel_id=1, source_target_pairs={{0,16},{16,0},{32,48},{48,32},{64,80},{80,64},{96,112},{112,96},{1... | collective-permute-start | bytes 368648 | tf_op jit(solution)/shard_map/ppermute | solution.py:33
  151.3 7.1 %collective-permute-start.32 = (bf16[80,768]{1,0:T(8,128)(2,1)S(1)}, bf16[80,768]{1,0:T(8,128)(2,1)S(1)}, u32[]{:S(2)}, u32[]{:S(2)}) collective-permute-start(bf16[80,768]{1,0:T(8,128)(2,1)S(1)} %collective-permute-done.28.refs_2_), channel_id=1, source_target_pairs={{0,16},{16,0},{32,48},{48,32},{64,80},{80,64},{96,112},{112,96},{1... | collective-permute-start | bytes 368648 | tf_op jit(solution)/shard_map/ppermute | solution.py:33
  151.4 7.0 %collective-permute-start.33 = (bf16[80,768]{1,0:T(8,128)(2,1)S(1)}, bf16[80,768]{1,0:T(8,128)(2,1)S(1)}, u32[]{:S(2)}, u32[]{:S(2)}) collective-permute-start(bf16[80,768]{1,0:T(8,128)(2,1)S(1)} %collective-permute-done.29.refs_3_), channel_id=1, source_target_pairs={{0,16},{16,0},{32,48},{48,32},{64,80},{80,64},{96,112},{112,96},{1... | collective-permute-start | bytes 368648 | tf_op jit(solution)/shard_map/ppermute | solution.py:33
  153.0 15.4 %collective-permute-start.34 = (bf16[192,768]{1,0:T(8,128)(2,1)S(1)}, bf16[192,768]{1,0:T(8,128)(2,1)S(1)}, u32[]{:S(2)}, u32[]{:S(2)}) collective-permute-start(bf16[192,768]{1,0:T(8,128)(2,1)S(1)} %fusion.2), channel_id=1, source_target_pairs={{0,128},{16,144},{32,160},{48,176},{64,192},{80,208},{96,224},{112... | collective-permute-start | bytes 884744 | tf_op jit(solution)/shard_map/ppermute | solution.py:33
  158.4 9.2 %copy-start.6 = (f32[32,3072]{1,0:T(8,128)S(1)}, f32[32,3072]{1,0:T(8,128)}, u32[]{:S(2)}) copy-start(f32[32,3072]{1,0:T(8,128)} %get-tuple-element.108) | copy-start | bytes 1179652
  158.4 9.1 %copy-start.11 = (bf16[32,3072]{1,0:T(8,128)(2,1)S(1)}, bf16[32,3072]{1,0:T(8,128)(2,1)}, u32[]{:S(2)}) copy-start(bf16[32,3072]{1,0:T(8,128)(2,1)} %param.11) | copy-start | bytes 589828
  160.5 21.9 %all-to-all-start.2 = ((bf16[16,12,768]{2,1,0:T(8,128)(2,1)}), bf16[16,12,768]{2,1,0:T(8,128)(2,1)S(1)}, u32[]{:S(2)}, u32[]{:S(2)}) async-start(bf16[16,12,768]{2,1,0:T(8,128)(2,1)} %get-tuple-element.80), calls=%async_computation.2 | async-start | bytes 786432 | tf_op jit(solution)/shard_map/all_to_all | solution.py:408

commit v4 on v3

--- a/solution.py
+++ b/solution.py
@@ -111,8 +111,8 @@
 
 
 def mlp_kernel(at, codes, tied, w_down, *refs):
-    pieces, (keep, give, codes_part, inner) = refs[:5], refs[5:9]
-    rows, hidden, slope, total, upstream, weights, sems = refs[9:]
+    pieces, (keep, give, codes_part, inner, inner_give) = refs[:5], refs[5:10]
+    rows, hidden, slope, total, upstream, weights, sems = refs[10:]
     step = pl.program_id(0)
     span = 2 * keep.shape[2]
     here = pl.ds(pl.multiple_of(step * span, span), span)
@@ -169,9 +169,12 @@
             rows[...], d_act, (((0,), (0,)), ((), ())), preferred_element_type=F32
         ).astype(BF16)
         piece = outer.shape[0] // 8
-        for k in range(8):
-            to_core = (k // 4 + at[2]) % 2
-            inner[to_core, (k % 4 + 4 - at[3]) % 4] = outer[k * piece : (k + 1) * piece, :]
+        lower = at[2] == 0
+        for k in range(4):
+            first = outer[k * piece : (k + 1) * piece, :]
+            second = outer[(k + 4) * piece : (k + 5) * piece, :]
+            inner[(k + 4 - at[3]) % 4] = jnp.where(lower, first, second)
+            inner_give[(k + 4 - at[3]) % 4] = jnp.where(lower, second, first)
 
 
 def mlp_call(at, codes, tied, w_down, pieces):
@@ -186,7 +189,8 @@
     out = [jax.ShapeDtypeStruct((4, 2, span // 2, units), BF16)] * 2
     out += [
         jax.ShapeDtypeStruct(codes.shape, BF16),
-        jax.ShapeDtypeStruct((2, 4, width // 8, units), BF16),
+        jax.ShapeDtypeStruct((4, width // 8, units), BF16),
+        jax.ShapeDtypeStruct((4, width // 8, units), BF16),
     ]
     return pl.pallas_call(
         mlp_kernel,
@@ -364,47 +368,52 @@
     all_codes = gather_codes(code_rows)
     blocks = jnp.stack([pick(blocks, core, 0), got], axis=2)
     got = [send(pick(blocks, (x + k) % 4, 0), "dp", step_x(k)) for k in (1, 2, 3)]
-    after, before, _, *got = tie((after, before, code_rows, *got))
+    at = jnp.stack([z, y, core, x, far, dp_at]).astype(jnp.int32)
+    tied_up = tied_call(at, along, across, w_up)
+    after, before, tied_up, _, *got = tie((after, before, tied_up, code_rows, *got))
     blocks = jnp.stack([pick(blocks, x, 0), *got], axis=2)
     half = line.shape[0] // 2
     far_a = send(after[:half], "mp", step_y(-1))
     far_b = send(before[half:], "mp", step_y(1))
     got = send(pick(blocks, 1 - far, 0), "dp", step_far)
-    at = jnp.stack([z, y, core, x, far, dp_at]).astype(jnp.int32)
-    tied_up = tied_call(at, along, across, w_up)
     all_codes, tied_up, far_a, far_b, got = tie((all_codes, tied_up, far_a, far_b, got))
     normed_cols = jnp.stack([pick(blocks, far, 0), got], axis=2).reshape(-1, rows)
     pieces = (line, after, far_a, far_b, before)
-    keep, give, codes_part, inner = mlp_call(at, all_codes, tied_up, w_down, pieces)
+    keep, give, codes_part, inner, inner_give = mlp_call(at, all_codes, tied_up, w_down, pieces)
     sent = send(give, "dp", step_core)
     grad_codes = scatter_codes(codes_part).astype(BF16)
-    inner = add(inner[0], send(inner[1], "dp", step_core)).astype(BF16)
+    inner = add(inner, send(inner_give, "dp", step_core)).astype(BF16)
     first, second = [add(keep[2, k], sent[2, k]).astype(BF16) for k in (0, 1)]
     first, second, inner = tie((first, second, inner))
     got_a = send(first, "dp", step_x(1))
     got_b = send(second, "dp", step_x(-1))
     got = [send(inner[k], "dp", step_x(k)) for k in (1, 2, 3)]
+    got_a, got_b, grad_codes, *got = tie((got_a, got_b, grad_codes, *got))
     inner = (inner[0].astype(F32) + sum(g.astype(F32) for g in got)).astype(BF16)
-    got_a, got_b, inner, grad_codes = tie((got_a, got_b, inner, grad_codes))
-    up = [add(keep[1, 0], sent[1, 0]) + got_a.astype(F32), add(keep[1, 1], sent[1, 1])]
-    down = [add(keep[3, 0], sent[3, 0]), add(keep[3, 1], sent[3, 1]) + got_b.astype(F32)]
-    up = jnp.stack([u.astype(BF16) for u in up])
-    down = jnp.stack([d.astype(BF16) for d in down])
     count, cols = inner.shape
     halves = jnp.split(grad_codes, 2)
     mine = jnp.concatenate([inner, jnp.concatenate(halves, axis=1)])
+    up = add(keep[1, 1], sent[1, 1]).astype(BF16)
+    down = (add(keep[3, 1], sent[3, 1]) + got_b.astype(F32)).astype(BF16)
     up, down, mine = tie((up, down, mine))
     other = send(mine, "dp", step_far)
     up = send(up, "dp", step_x(1))
     down = send(down, "dp", step_x(-1))
+    up, down, other = tie((up, down, other))
     inner = add(inner, other[:count]).astype(BF16)
     mine = jnp.concatenate([inner, mine[count:], other[count:]])
     parts = gather_parts(mine, "dp", step_x)
-    up, down, *parts = tie((up, down, *parts))
-    total = [add(keep[0, k], sent[0, k]) + add(up[k], down[k]) for k in (0, 1)]
-    grad_down = total[0] + send(total[1].astype(BF16), "dp", step_far).astype(F32)
+    total = (add(keep[0, 1], sent[0, 1]) + add(up, down)).astype(BF16)
+    across_far = send(total, "dp", step_far)
+    up = (add(keep[1, 0], sent[1, 0]) + got_a.astype(F32)).astype(BF16)
+    down = add(keep[3, 0], sent[3, 0]).astype(BF16)
+    up = send(up, "dp", step_x(1))
+    down = send(down, "dp", step_x(-1))
+    parts = list(tie(tuple(parts)))
     others = [send(p, "dp", step_core) for p in parts]
     both, grad_up = rows_call(at, normed_cols, w_up, encoder, parts, others)
+    both, across_far = tie((both, across_far))
+    grad_down = add(keep[0, 0], sent[0, 0]) + add(up, down) + across_far.astype(F32)
     both = lax.all_to_all(both, "mp", split_axis=0, concat_axis=0)
     both = jnp.sum(both.astype(F32), axis=0)
     own_encoder = lax.dynamic_slice_in_dim(encoder, mp_at * own, own, 0).astype(F32)

time: 187 us -> 176 us (0.941); the launches traced: 184 us -> 175 us
  waiting for transfers between devices: 46.8 us -> 35.1 us
  starting transfers between devices: 78.4 us -> 84 us
    ppermute x35 -> x37, waiting for transfers between devices: 33.4 us -> 24.9 us  [send(): return lax.ppermute(value, axis, [(i, target(i)) for i in range(16)])]
    ppermute x35 -> x37, starting transfers between devices: 57.9 us -> 62.8 us  [send(): return lax.ppermute(value, axis, [(i, target(i)) for i in range(16)])]
    all_to_all x1, waiting for transfers between devices: 11.7 us -> 8.17 us  [on_device(): both = lax.all_to_all(both, 'mp', split_axis=0, concat_axis=0)]
    another operation x2 -> x0, other arithmetic: 1.88 us -> none  [the longest x1 1.77 us: on_device(): down = jnp.stack([d.astype(BF16) for d in down])]
    convert_element_type x3 -> x4, other arithmetic: 5.17 us -> 6.75 us  [the longest x1 2.78 us: on_device(): down = add(keep[3, 0], sent[3, 0]).astype(BF16)]
    unnamed x52 -> x42, local copies, waits for them, and re-layouts: 5.22 us -> 6.19 us
  transfers between devices with their start and end apart: 38 -> 40, of which waited for: 13 -> 11; matrix products, arithmetic and copies ran while one was open for 14% -> 13% of each run, Pallas kernels for 4% -> 4%
where the time goes in v4:
time: 176 us; the launch traced here: 175 us
  starting transfers between devices  84 us (48%)
  waiting for transfers between devices  35.1 us (20%)
  Pallas kernels  22.1 us (13%)
  other arithmetic  19.1 us (11%)
  local copies, waits for them, and re-layouts  11.9 us (7%)
    ppermute x37, starting transfers between devices, send(): return lax.ppermute(value, axis, [(i, target(i)) for i in range(16)])  62.8 us
    ppermute x37, waiting for transfers between devices, send(): return lax.ppermute(value, axis, [(i, target(i)) for i in range(16)])  24.9 us
    pallas_call x1, Pallas kernels, mlp_call(): pl.pallas_call(mlp_kernel, grid_spec=pltpu.PrefetchScalarGridSpec(num_sca...  14.4 us
    all_to_all x1, waiting for transfers between devices, on_device(): both = lax.all_to_all(both, 'mp', split_axis=0, concat_axis=0)  8.17 us
    all_to_all x1, starting transfers between devices, scatter_codes(): got = lax.all_to_all(part, 'mp', split_axis=0, concat_axis=0)  7.47 us
    all_to_all x1, starting transfers between devices, on_device(): both = lax.all_to_all(both, 'mp', split_axis=0, concat_axis=0)  6.91 us
    all_to_all x1, starting transfers between devices, gather_codes(): lax.all_to_all(jnp.broadcast_to(code_rows, (16, count, width)), 'mp', spl...  6.77 us
    unnamed x42, local copies, waits for them, and re-layouts  6.19 us
  transfers between devices with their start and end apart: 40, of which 11 were waited for; matrix products, arithmetic and copies ran while one was open for 13% of the time, Pallas kernels for 4%

profile of v4, /device:TPU:2, one launch (start us, length us, event | category | flops | bytes accessed | tf_op | source)
XLA Modules:
  0.0 175.1 jit_solution(17886992141129431488)
XLA Ops:
  0.6 7.3 %collective-permute-start = (bf16[192,384]{1,0:T(8,128)(2,1)}, bf16[192,384]{1,0:T(8,128)(2,1)S(1)}, u32[]{:S(2)}, u32[]{:S(2)}) collective-permute-start(bf16[192,384]{1,0:T(8,128)(2,1)} %encoder.1), channel_id=1, source_target_pairs={{0,128},{16,144},{32,160},{48,176},{64,192},{80,208},{96,224},{112... | collective-permute-start | bytes 442376 | tf_op jit(solution)/shard_map/ppermute | solution.py:33
  7.9 1.1 convert_reduce_fusion.1
  9.0 1.2 fusion.16
  10.2 1.1 fusion.10
  11.3 0.7 collective-permute-done
  12.1 4.1 %collective-permute-start.6 = (bf16[32,3072]{1,0:T(8,128)(2,1)}, bf16[32,3072]{1,0:T(8,128)(2,1)S(1)}, u32[]{:S(2)}, u32[]{:S(2)}) collective-permute-start(bf16[32,3072]{1,0:T(8,128)(2,1)} %param.11), channel_id=1, source_target_pairs={{0,4},{1,5},{2,6},{3,7},{4,8},{5,9},{6,10},{7,11},{8,12},{9,13},{1... | collective-permute-start | bytes 589832 | tf_op jit(solution)/shard_map/ppermute | solution.py:33
  16.2 1.5 collective-permute-start.5
  17.6 2.3 %collective-permute-start.4 = (bf16[32,3072]{1,0:T(8,128)(2,1)}, bf16[32,3072]{1,0:T(8,128)(2,1)S(1)}, u32[]{:S(2)}, u32[]{:S(2)}) collective-permute-start(bf16[32,3072]{1,0:T(8,128)(2,1)} %param.11), channel_id=1, source_target_pairs={{0,12},{1,13},{2,14},{3,15},{4,0},{5,1},{6,2},{7,3},{8,4},{9,5},{1... | collective-permute-start | bytes 589832 | tf_op jit(solution)/shard_map/ppermute | solution.py:33
  19.9 0.9 select_bitcast_fusion.1
  20.9 2.2 %collective-permute-start.2 = (bf16[2,192,384]{2,1,0:T(8,128)(2,1)S(1)}, bf16[2,192,384]{2,1,0:T(8,128)(2,1)S(1)}, u32[]{:S(2)}, u32[]{:S(2)}) collective-permute-start(bf16[2,192,384]{2,1,0:T(8,128)(2,1)S(1)} %pad_maximum_fusion.1), channel_id=1, source_target_pairs={{0,64},{16,80},{32,96},{48,112},{64,0},{80,16},{96,32},{112,48},{1... | collective-permute-start | bytes 884744 | tf_op jit(solution)/shard_map/ppermute | solution.py:33
  23.1 1.4 collective-permute-start.1
  25.6 0.7 collective-permute-start.3
  26.2 3.2 %collective-permute-done.5 = bf16[32,3072]{1,0:T(8,128)(2,1)S(1)} collective-permute-done((bf16[32,3072]{1,0:T(8,128)(2,1)}, bf16[32,3072]{1,0:T(8,128)(2,1)S(1)}, u32[]{:S(2)}, u32[]{:S(2)}) %collective-permute-start.5) | collective-permute-done | bytes 196640 | tf_op jit(solution)/shard_map/ppermute | solution.py:33
  29.5 0.9 pad_maximum_fusion.refs_0_
  30.4 5.7 %collective-permute-done.1 = bf16[2,192,384]{2,1,0:T(8,128)(2,1)S(1)} collective-permute-done((bf16[2,192,384]{2,1,0:T(8,128)(2,1)S(1)}, bf16[2,192,384]{2,1,0:T(8,128)(2,1)S(1)}, u32[]{:S(2)}, u32[]{:S(2)}) %collective-permute-start.1) | collective-permute-done | bytes 294944 | tf_op jit(solution)/shard_map/ppermute | solution.py:33
  38.0 1.7 collective-permute-start.10
  39.7 1.7 collective-permute-start.9
  42.0 0.8 broadcast_in_dim.2
  42.8 6.8 %all-to-all-start = ((bf16[16,32,384]{2,1,0:T(8,128)(2,1)}), bf16[16,32,384]{2,1,0:T(8,128)(2,1)}, u32[]{:S(2)}, u32[]{:S(2)}) async-start(bf16[16,32,384]{2,1,0:T(8,128)(2,1)} %broadcast_in_dim.2), calls=%async_computation | async-start | bytes 786432 | tf_op jit(solution)/shard_map/all_to_all | solution.py:74
  49.9 1.8 %collective-permute-start.13 = (bf16[2,2,32,192]{3,2,1,0:T(8,128)(2,1)S(1)}, bf16[2,2,32,192]{3,2,1,0:T(8,128)(2,1)S(1)}, u32[]{:S(2)}, u32[]{:S(2)}) collective-permute-start(bf16[2,2,32,192]{3,2,1,0:T(8,128)(2,1)S(1)} %bitcast.130), channel_id=1, source_target_pairs={{0,96},{16,112},{32,0},{48,16},{64,32},{80,48},{96,64},{112,80},{1... | collective-permute-start | bytes 147464 | tf_op jit(solution)/shard_map/ppermute | solution.py:33
  51.7 1.2 collective-permute-start.12
  52.9 1.8 %collective-permute-start.11 = (bf16[2,2,32,192]{3,2,1,0:T(8,128)(2,1)S(1)}, bf16[2,2,32,192]{3,2,1,0:T(8,128)(2,1)S(1)}, u32[]{:S(2)}, u32[]{:S(2)}) collective-permute-start(bf16[2,2,32,192]{3,2,1,0:T(8,128)(2,1)S(1)} %bitcast.128), channel_id=1, source_target_pairs={{0,32},{16,48},{32,64},{48,80},{64,96},{80,112},{96,0},{112,16},{1... | collective-permute-start | bytes 147464 | tf_op jit(solution)/shard_map/ppermute | solution.py:33
  54.8 2.3 %copy-done = bf16[3072,768]{1,0:T(8,128)(2,1)S(1)} copy-done((bf16[3072,768]{1,0:T(8,128)(2,1)S(1)}, bf16[3072,768]{1,0:T(8,128)(2,1)}, u32[]{:S(2)}) %copy-start) | copy-done | bytes 4718616
  57.1 5.6 %shard_map.101.tied = bf16[384,768]{1,0:T(8,128)(2,1)S(1)} custom-call(s32[6]{0:T(128)S(1)} %stack.96.at, bf16[8,192,384]{2,1,0:T(8,128)(2,1)S(1)} %bitcast.113, bf16[8,192,384]{2,1,0:T(8,128)(2,1)S(1)} %bitcast.115, bf16[3072,768]{1,0:T(8,128)(2,1)S(1)} %copy-done), custom_call_target="tpu_custom_call" | custom-call | flops 1811939328 | bytes 9437184 | tf_op jit(solution)/shard_map/pallas_call | solution.py:253
  62.7 0.8 copy-done.2
  64.2 1.0 slice.82
  65.2 1.0 slice.83
  66.2 1.9 %collective-permute-start.15 = (bf16[64,3072]{1,0:T(8,128)(2,1)S(1)}, bf16[64,3072]{1,0:T(8,128)(2,1)}, u32[]{:S(2)}, u32[]{:S(2)}) collective-permute-start(bf16[64,3072]{1,0:T(8,128)(2,1)S(1)} %slice.83), channel_id=1, source_target_pairs={{0,1},{1,2},{2,3},{3,0},{4,5},{5,6},{6,7},{7,4},{8,9},{9,10},{10,1... | collective-permute-start | bytes 1179656 | tf_op jit(solution)/shard_map/ppermute | solution.py:33
  68.1 1.4 collective-permute-start.14
  69.6 0.9 pad_maximum_fusion.2
  70.6 5.3 %collective-permute-start.16 = (bf16[2,4,32,192]{3,2,1,0:T(8,128)(2,1)S(1)}, bf16[2,4,32,192]{3,2,1,0:T(8,128)(2,1)S(1)}, u32[]{:S(2)}, u32[]{:S(2)}) collective-permute-start(bf16[2,4,32,192]{3,2,1,0:T(8,128)(2,1)S(1)} %bitcast.125), channel_id=1, source_target_pairs={{0,128},{16,144},{32,160},{48,176},{64,192},{80,208},{96,224},{112... | collective-permute-start | bytes 294920 | tf_op jit(solution)/shard_map/ppermute | solution.py:33
  75.8 3.8 %collective-permute-done.16 = bf16[2,4,32,192]{3,2,1,0:T(8,128)(2,1)S(1)} collective-permute-done((bf16[2,4,32,192]{3,2,1,0:T(8,128)(2,1)S(1)}, bf16[2,4,32,192]{3,2,1,0:T(8,128)(2,1)S(1)}, u32[]{:S(2)}, u32[]{:S(2)}) %collective-permute-start.16) | collective-permute-done | bytes 98336 | tf_op jit(solution)/shard_map/ppermute | solution.py:33
  80.3 14.4 %shard_map.102 = (bf16[4,2,192,768]{3,2,1,0:T(8,128)(2,1)}, bf16[4,2,192,768]{3,2,1,0:T(8,128)(2,1)}, bf16[16,32,384]{2,1,0:T(8,128)(2,1)}, bf16[4,48,768]{2,1,0:T(8,128)(2,1)}, bf16[4,48,768]{2,1,0:T(8,128)(2,1)}) custom-call(s32[6]{0:T(128)} %copy-done.3, bf16[16,32,384]{2,1,0:T(8,128)(2,1)} %all-to-all-done.codes, bf16[384,768]{1,0:T(8,128)(2,1)} %copy-done.2, ...), custom_call_target="tpu_custom_call" | custom-call | flops 5435817984 | bytes 17301504 | tf_op jit(solution)/shard_map/pallas_call | solution.py:195
  95.3 7.5 %all-to-all-start.1 = ((bf16[16,32,384]{2,1,0:T(8,128)(2,1)}), bf16[16,32,384]{2,1,0:T(8,128)(2,1)S(1)}, u32[]{:S(2)}, u32[]{:S(2)}) async-start(bf16[16,32,384]{2,1,0:T(8,128)(2,1)} %get-tuple-element.72), calls=%async_computation.1 | async-start | bytes 786432 | tf_op jit(solution)/shard_map/all_to_all | solution.py:80
  102.8 0.7 copy-done.8
  103.5 1.1 add_convert_fusion.2
  104.6 2.8 %fusion.20 = (bf16[192,768]{1,0:T(8,128)(2,1)}, bf16[192,768]{1,0:T(8,128)(2,1)}, bf16[192,768]{1,0:T(8,128)(2,1)}, bf16[192,768]{1,0:T(8,128)(2,1)}) fusion(bf16[4,2,192,768]{3,2,1,0:T(8,128)(2,1)} %collective-permute-done.17, bf16[4,2,192,768]{3,2,1,0:T(8,128)(2,1)} %get-tuple-element.66), kind=kLoop, calls=%fused_computation.46 | loop fusion | flops 2359296 | bytes 3538944 | tf_op jit(solution)/shard_map/convert_element_type | solution.py:409
  107.4 1.1 collective-permute-start.19
  108.5 0.9 collective-permute-start.20
  110.1 1.6 collective-permute-start.23
  111.7 1.0 collective-permute-start.22
  112.6 1.5 collective-permute-start.21
  114.1 2.0 %all-to-all-done.1 = bf16[16,32,384]{2,1,0:T(8,128)(2,1)S(1)} async-done(((bf16[16,32,384]{2,1,0:T(8,128)(2,1)}), bf16[16,32,384]{2,1,0:T(8,128)(2,1)S(1)}, u32[]{:S(2)}, u32[]{:S(2)}) %all-to-all-start.1) | async-done | bytes 393248 | tf_op jit(solution)/shard_map/all_to_all | solution.py:80
  116.2 3.4 %collective-permute-done.23 = bf16[48,768]{1,0:T(8,128)(2,1)} collective-permute-done((bf16[48,768]{1,0:T(8,128)(2,1)}, bf16[48,768]{1,0:T(8,128)(2,1)}, u32[]{:S(2)}, u32[]{:S(2)}) %collective-permute-start.23) | collective-permute-done | bytes 73760 | tf_op jit(solution)/shard_map/ppermute | solution.py:33
  119.6 1.1 collective-permute-done.22
  120.8 1.0 fusion.21
  121.8 1.3 fusion.4
  123.4 2.0 %collective-permute-start.25 = (bf16[192,768]{1,0:T(8,128)(2,1)S(1)}, bf16[192,768]{1,0:T(8,128)(2,1)S(1)}, u32[]{:S(2)}, u32[]{:S(2)}) collective-permute-start(bf16[192,768]{1,0:T(8,128)(2,1)S(1)} %fusion.4), channel_id=1, source_target_pairs={{0,96},{16,112},{32,0},{48,16},{64,32},{80,48},{96,64},{112,80},{1... | collective-permute-start | bytes 884744 | tf_op jit(solution)/shard_map/ppermute | solution.py:33
  126.2 4.6 %collective-permute-start.26 = (bf16[64,768]{1,0:T(8,128)(2,1)S(1)}, bf16[64,768]{1,0:T(8,128)(2,1)S(1)}, u32[]{:S(2)}, u32[]{:S(2)}) collective-permute-start(bf16[64,768]{1,0:T(8,128)(2,1)S(1)} %maximum_maximum_fusion), channel_id=1, source_target_pairs={{0,128},{16,144},{32,160},{48,176},{64,192},{80,208},{96,224},{112... | collective-permute-start | bytes 294920 | tf_op jit(solution)/shard_map/ppermute | solution.py:33
  130.9 4.1 %collective-permute-done.26 = bf16[64,768]{1,0:T(8,128)(2,1)S(1)} collective-permute-done((bf16[64,768]{1,0:T(8,128)(2,1)S(1)}, bf16[64,768]{1,0:T(8,128)(2,1)S(1)}, u32[]{:S(2)}, u32[]{:S(2)}) %collective-permute-start.26) | collective-permute-done | bytes 98336 | tf_op jit(solution)/shard_map/ppermute | solution.py:33
  135.1 0.9 collective-permute-start.29
  135.9 3.1 %collective-permute-start.28 = (bf16[80,768]{1,0:T(8,128)(2,1)S(1)}, bf16[80,768]{1,0:T(8,128)(2,1)S(1)}, u32[]{:S(2)}, u32[]{:S(2)}) collective-permute-start(bf16[80,768]{1,0:T(8,128)(2,1)S(1)} %pad_maximum_fusion.4.refs_0_), channel_id=1, source_target_pairs={{0,64},{16,80},{32,96},{48,112},{64,0},{80,16},{96,32},{112,48},{1... | collective-permute-start | bytes 368648 | tf_op jit(solution)/shard_map/ppermute | solution.py:33
  139.0 1.0 collective-permute-start.27
  140.0 1.6 fusion.2
  141.7 5.0 %collective-permute-start.36 = (bf16[192,768]{1,0:T(8,128)(2,1)S(1)}, bf16[192,768]{1,0:T(8,128)(2,1)S(1)}, u32[]{:S(2)}, u32[]{:S(2)}) collective-permute-start(bf16[192,768]{1,0:T(8,128)(2,1)S(1)} %get-tuple-element.98), channel_id=1, source_target_pairs={{0,128},{16,144},{32,160},{48,176},{64,192},{80,208},{96,224},{112... | collective-permute-start | bytes 884744 | tf_op jit(solution)/shard_map/ppermute | solution.py:33
  146.7 0.9 fusion.33
  149.7 1.4 collective-permute-start.34
  151.1 2.1 %shard_map.103 = (bf16[16,12,768]{2,1,0:T(8,128)(2,1)}, f32[192,768]{1,0:T(8,128)}) custom-call(s32[6]{0:T(128)S(1)} %copy-done.4, bf16[512,192]{1,0:T(8,128)(2,1)S(1)} %bitcast.116, bf16[3072,768]{1,0:T(8,128)(2,1)S(1)} %bitcast.110, bf16[192,384]{1,0:T(8,128)(2,1)S(1)} %copy-done.1, bf16[80,768]{1,0:T(8,128)(2,1)S(1)} %pad_maximum_fusion.4.refs_0_, ...), custom_call_target="tpu_custom_call" | custom-call | flops 301989888 | bytes 1081344 | tf_op jit(solution)/shard_map/pallas_call | solution.py:309
  153.2 2.4 %collective-permute-done.36 = bf16[192,768]{1,0:T(8,128)(2,1)S(1)} collective-permute-done((bf16[192,768]{1,0:T(8,128)(2,1)S(1)}, bf16[192,768]{1,0:T(8,128)(2,1)S(1)}, u32[]{:S(2)}, u32[]{:S(2)}) %collective-permute-start.36) | collective-permute-done | bytes 294944 | tf_op jit(solution)/shard_map/ppermute | solution.py:33
  155.6 6.9 %all-to-all-start.2 = ((bf16[16,12,768]{2,1,0:T(8,128)(2,1)}), bf16[16,12,768]{2,1,0:T(8,128)(2,1)S(1)}, u32[]{:S(2)}, u32[]{:S(2)}) async-start(bf16[16,12,768]{2,1,0:T(8,128)(2,1)} %get-tuple-element.94), calls=%async_computation.2 | async-start | bytes 786432 | tf_op jit(solution)/shard_map/all_to_all | solution.py:417
  162.5 0.9 fusion.15
  163.4 2.1 %fusion.3 = f32[192,768]{1,0:T(8,128)} fusion(bf16[192,768]{1,0:T(8,128)(2,1)S(1)} %collective-permute-done.36, bf16[192,768]{1,0:T(8,128)(2,1)S(1)} %collective-permute-done.35, bf16[192,768]{1,0:T(8,128)(2,1)} %collective-permute-done.34, bf16[4,2,192,768]{3,2,1,0:T(8,128)(2,1)} %collective-permute-done.17, bf16[4,2,192,768]{3,2,1,0:T(8,128)(2,1)} %get-tuple-element.66), kind=kLoop, calls=%fused_computation.13 | loop fusion | flops 1327104 | bytes 2064384 | tf_op jit(solution)/shard_map/add | solution.py:416
  165.5 8.2 %all-to-all-done.2 = bf16[16,12,768]{2,1,0:T(8,128)(2,1)S(1)} async-done(((bf16[16,12,768]{2,1,0:T(8,128)(2,1)}), bf16[16,12,768]{2,1,0:T(8,128)(2,1)S(1)}, u32[]{:S(2)}, u32[]{:S(2)}) %all-to-all-start.2) | async-done | bytes 294944 | tf_op jit(solution)/shard_map/all_to_all | solution.py:417
  173.8 0.7 multiply_reduce_fusion
  (119 shorter events, 10.3 us)
Async XLA Ops:
  0.6 11.4 %collective-permute-start = (bf16[192,384]{1,0:T(8,128)(2,1)}, bf16[192,384]{1,0:T(8,128)(2,1)S(1)}, u32[]{:S(2)}, u32[]{:S(2)}) collective-permute-start(bf16[192,384]{1,0:T(8,128)(2,1)} %encoder.1), channel_id=1, source_target_pairs={{0,128},{16,144},{32,160},{48,176},{64,192},{80,208},{96,224},{112... | collective-permute-start | bytes 442376 | tf_op jit(solution)/shard_map/ppermute | solution.py:33
  10.1 19.3 %copy-start.6 = (bf16[32,3072]{1,0:T(8,128)(2,1)S(1)}, bf16[32,3072]{1,0:T(8,128)(2,1)}, u32[]{:S(2)}) copy-start(bf16[32,3072]{1,0:T(8,128)(2,1)} %param.11) | copy-start | bytes 589828
  12.1 13.5 %collective-permute-start.6 = (bf16[32,3072]{1,0:T(8,128)(2,1)}, bf16[32,3072]{1,0:T(8,128)(2,1)S(1)}, u32[]{:S(2)}, u32[]{:S(2)}) collective-permute-start(bf16[32,3072]{1,0:T(8,128)(2,1)} %param.11), channel_id=1, source_target_pairs={{0,4},{1,5},{2,6},{3,7},{4,8},{5,9},{6,10},{7,11},{8,12},{9,13},{1... | collective-permute-start | bytes 589832 | tf_op jit(solution)/shard_map/ppermute | solution.py:33
  16.2 13.3 %collective-permute-start.5 = (bf16[32,3072]{1,0:T(8,128)(2,1)}, bf16[32,3072]{1,0:T(8,128)(2,1)S(1)}, u32[]{:S(2)}, u32[]{:S(2)}) collective-permute-start(bf16[32,3072]{1,0:T(8,128)(2,1)} %param.11), channel_id=1, source_target_pairs={{0,8},{1,9},{2,10},{3,11},{4,12},{5,13},{6,14},{7,15},{8,0},{9,1},... | collective-permute-start | bytes 589832 | tf_op jit(solution)/shard_map/ppermute | solution.py:33
  17.6 11.8 %collective-permute-start.4 = (bf16[32,3072]{1,0:T(8,128)(2,1)}, bf16[32,3072]{1,0:T(8,128)(2,1)S(1)}, u32[]{:S(2)}, u32[]{:S(2)}) collective-permute-start(bf16[32,3072]{1,0:T(8,128)(2,1)} %param.11), channel_id=1, source_target_pairs={{0,12},{1,13},{2,14},{3,15},{4,0},{5,1},{6,2},{7,3},{8,4},{9,5},{1... | collective-permute-start | bytes 589832 | tf_op jit(solution)/shard_map/ppermute | solution.py:33
  20.9 15.3 %collective-permute-start.2 = (bf16[2,192,384]{2,1,0:T(8,128)(2,1)S(1)}, bf16[2,192,384]{2,1,0:T(8,128)(2,1)S(1)}, u32[]{:S(2)}, u32[]{:S(2)}) collective-permute-start(bf16[2,192,384]{2,1,0:T(8,128)(2,1)S(1)} %pad_maximum_fusion.1), channel_id=1, source_target_pairs={{0,64},{16,80},{32,96},{48,112},{64,0},{80,16},{96,32},{112,48},{1... | collective-permute-start | bytes 884744 | tf_op jit(solution)/shard_map/ppermute | solution.py:33
  23.1 13.0 %collective-permute-start.1 = (bf16[2,192,384]{2,1,0:T(8,128)(2,1)S(1)}, bf16[2,192,384]{2,1,0:T(8,128)(2,1)S(1)}, u32[]{:S(2)}, u32[]{:S(2)}) collective-permute-start(bf16[2,192,384]{2,1,0:T(8,128)(2,1)S(1)} %pad_maximum_fusion.1), channel_id=1, source_target_pairs={{0,96},{16,112},{32,0},{48,16},{64,32},{80,48},{96,64},{112,80},{1... | collective-permute-start | bytes 884744 | tf_op jit(solution)/shard_map/ppermute | solution.py:33
  25.6 10.7 %collective-permute-start.3 = (bf16[2,192,384]{2,1,0:T(8,128)(2,1)S(1)}, bf16[2,192,384]{2,1,0:T(8,128)(2,1)S(1)}, u32[]{:S(2)}, u32[]{:S(2)}) collective-permute-start(bf16[2,192,384]{2,1,0:T(8,128)(2,1)S(1)} %pad_maximum_fusion.1), channel_id=1, source_target_pairs={{0,32},{16,48},{32,64},{48,80},{64,96},{80,112},{96,0},{112,16},{1... | collective-permute-start | bytes 884744 | tf_op jit(solution)/shard_map/ppermute | solution.py:33
  29.5 7.2 %collective-permute-start.7 = (bf16[4,2,32,192]{3,2,1,0:T(8,128)(2,1)S(1)}, bf16[4,2,32,192]{3,2,1,0:T(8,128)(2,1)S(1)}, u32[]{:S(2)}, u32[]{:S(2)}) collective-permute-start(bf16[4,2,32,192]{3,2,1,0:T(8,128)(2,1)S(1)} %bitcast.124), channel_id=1, source_target_pairs={{0,16},{16,0},{32,48},{48,32},{64,80},{80,64},{96,112},{112,96},{1... | collective-permute-start | bytes 294920 | tf_op jit(solution)/shard_map/ppermute | solution.py:33
  36.6 0.7 copy-start.9
  37.3 4.1 %collective-permute-start.8 = (bf16[1536,384]{1,0:T(8,128)(2,1)S(1)}, bf16[1536,384]{1,0:T(8,128)(2,1)S(1)}, u32[]{:S(2)}, u32[]{:S(2)}) collective-permute-start(bf16[1536,384]{1,0:T(8,128)(2,1)S(1)} %bitcast.111), channel_id=1, source_target_pairs={{0,16},{16,0},{32,48},{48,32},{64,80},{80,64},{96,112},{112,96},{1... | collective-permute-start | bytes 3538952 | tf_op jit(solution)/shard_map/ppermute | solution.py:33
  38.0 11.8 %copy-start.10 = (bf16[4,2,32,192]{3,2,1,0:T(8,128)(2,1)S(1)}, bf16[4,2,32,192]{3,2,1,0:T(8,128)(2,1)}, u32[]{:S(2)}) copy-start(bf16[4,2,32,192]{3,2,1,0:T(8,128)(2,1)} %copy-done.9) | copy-start | bytes 294916
  38.0 25.5 %collective-permute-start.10 = (bf16[128,3072]{1,0:T(8,128)(2,1)}, bf16[128,3072]{1,0:T(8,128)(2,1)}, u32[]{:S(2)}, u32[]{:S(2)}) collective-permute-start(bf16[128,3072]{1,0:T(8,128)(2,1)} %pad_maximum_fusion.refs_0_), channel_id=1, source_target_pairs={{0,1},{1,2},{2,3},{3,0},{4,5},{5,6},{6,7},{7,4},{8,9},{9,10},{10,1... | collective-permute-start | bytes 2359304 | tf_op jit(solution)/shard_map/ppermute | solution.py:33
  39.7 24.5 %collective-permute-start.9 = (bf16[128,3072]{1,0:T(8,128)(2,1)}, bf16[128,3072]{1,0:T(8,128)(2,1)}, u32[]{:S(2)}, u32[]{:S(2)}) collective-permute-start(bf16[128,3072]{1,0:T(8,128)(2,1)} %pad_maximum_fusion.refs_0_), channel_id=1, source_target_pairs={{0,3},{1,0},{2,1},{3,2},{4,7},{5,4},{6,5},{7,6},{8,11},{9,8},{10,9... | collective-permute-start | bytes 2359304 | tf_op jit(solution)/shard_map/ppermute | solution.py:33
  42.8 37.5 %all-to-all-start = ((bf16[16,32,384]{2,1,0:T(8,128)(2,1)}), bf16[16,32,384]{2,1,0:T(8,128)(2,1)}, u32[]{:S(2)}, u32[]{:S(2)}) async-start(bf16[16,32,384]{2,1,0:T(8,128)(2,1)} %broadcast_in_dim.2), calls=%async_computation | async-start | bytes 786432 | tf_op jit(solution)/shard_map/all_to_all | solution.py:74
  49.7 13.0 %copy-start.3 = (s32[6]{0:T(128)}, s32[6]{0:T(128)S(1)}, u32[]{:S(2)}) copy-start(s32[6]{0:T(128)S(1)} %stack.96.at) | copy-start | bytes 76
  49.9 13.6 %collective-permute-start.13 = (bf16[2,2,32,192]{3,2,1,0:T(8,128)(2,1)S(1)}, bf16[2,2,32,192]{3,2,1,0:T(8,128)(2,1)S(1)}, u32[]{:S(2)}, u32[]{:S(2)}) collective-permute-start(bf16[2,2,32,192]{3,2,1,0:T(8,128)(2,1)S(1)} %bitcast.130), channel_id=1, source_target_pairs={{0,96},{16,112},{32,0},{48,16},{64,32},{80,48},{96,64},{112,80},{1... | collective-permute-start | bytes 147464 | tf_op jit(solution)/shard_map/ppermute | solution.py:33
  51.7 11.8 %collective-permute-start.12 = (bf16[2,2,32,192]{3,2,1,0:T(8,128)(2,1)S(1)}, bf16[2,2,32,192]{3,2,1,0:T(8,128)(2,1)S(1)}, u32[]{:S(2)}, u32[]{:S(2)}) collective-permute-start(bf16[2,2,32,192]{3,2,1,0:T(8,128)(2,1)S(1)} %bitcast.129), channel_id=1, source_target_pairs={{0,64},{16,80},{32,96},{48,112},{64,0},{80,16},{96,32},{112,48},{1... | collective-permute-start | bytes 147464 | tf_op jit(solution)/shard_map/ppermute | solution.py:33
  52.9 10.6 %collective-permute-start.11 = (bf16[2,2,32,192]{3,2,1,0:T(8,128)(2,1)S(1)}, bf16[2,2,32,192]{3,2,1,0:T(8,128)(2,1)S(1)}, u32[]{:S(2)}, u32[]{:S(2)}) collective-permute-start(bf16[2,2,32,192]{3,2,1,0:T(8,128)(2,1)S(1)} %bitcast.128), channel_id=1, source_target_pairs={{0,32},{16,48},{32,64},{48,80},{64,96},{80,112},{96,0},{112,16},{1... | collective-permute-start | bytes 147464 | tf_op jit(solution)/shard_map/ppermute | solution.py:33
  54.8 2.3 %copy-start = (bf16[3072,768]{1,0:T(8,128)(2,1)S(1)}, bf16[3072,768]{1,0:T(8,128)(2,1)}, u32[]{:S(2)}) copy-start(bf16[3072,768]{1,0:T(8,128)(2,1)} %w_up.3) | copy-start | bytes 14155780
  62.7 0.8 copy-start.2
  63.5 6.0 %copy-start.13 = (bf16[2,2,32,192]{3,2,1,0:T(8,128)(2,1)}, bf16[2,2,32,192]{3,2,1,0:T(8,128)(2,1)S(1)}, u32[]{:S(2)}) copy-start(bf16[2,2,32,192]{3,2,1,0:T(8,128)(2,1)S(1)} %collective-permute-done.12) | copy-start | bytes 147460
  63.6 0.6 copy-start.14
  66.2 13.4 %collective-permute-start.15 = (bf16[64,3072]{1,0:T(8,128)(2,1)S(1)}, bf16[64,3072]{1,0:T(8,128)(2,1)}, u32[]{:S(2)}, u32[]{:S(2)}) collective-permute-start(bf16[64,3072]{1,0:T(8,128)(2,1)S(1)} %slice.83), channel_id=1, source_target_pairs={{0,1},{1,2},{2,3},{3,0},{4,5},{5,6},{6,7},{7,4},{8,9},{9,10},{10,1... | collective-permute-start | bytes 1179656 | tf_op jit(solution)/shard_map/ppermute | solution.py:33
  68.1 12.2 %collective-permute-start.14 = (bf16[64,3072]{1,0:T(8,128)(2,1)S(1)}, bf16[64,3072]{1,0:T(8,128)(2,1)}, u32[]{:S(2)}, u32[]{:S(2)}) collective-permute-start(bf16[64,3072]{1,0:T(8,128)(2,1)S(1)} %slice.82), channel_id=1, source_target_pairs={{0,3},{1,0},{2,1},{3,2},{4,7},{5,4},{6,5},{7,6},{8,11},{9,8},{10,9... | collective-permute-start | bytes 1179656 | tf_op jit(solution)/shard_map/ppermute | solution.py:33
  70.6 9.1 %collective-permute-start.16 = (bf16[2,4,32,192]{3,2,1,0:T(8,128)(2,1)S(1)}, bf16[2,4,32,192]{3,2,1,0:T(8,128)(2,1)S(1)}, u32[]{:S(2)}, u32[]{:S(2)}) collective-permute-start(bf16[2,4,32,192]{3,2,1,0:T(8,128)(2,1)S(1)} %bitcast.125), channel_id=1, source_target_pairs={{0,128},{16,144},{32,160},{48,176},{64,192},{80,208},{96,224},{112... | collective-permute-start | bytes 294920 | tf_op jit(solution)/shard_map/ppermute | solution.py:33
  79.6 0.7 copy-start.11
  94.7 9.9 %collective-permute-start.17 = (bf16[4,2,192,768]{3,2,1,0:T(8,128)(2,1)}, bf16[4,2,192,768]{3,2,1,0:T(8,128)(2,1)}, u32[]{:S(2)}, u32[]{:S(2)}) collective-permute-start(bf16[4,2,192,768]{3,2,1,0:T(8,128)(2,1)} %get-tuple-element.67), channel_id=1, source_target_pairs={{0,16},{16,0},{32,48},{48,32},{64,80},{80,64},{96,112},{112,96},{1... | collective-permute-start | bytes 7077896 | tf_op jit(solution)/shard_map/ppermute | solution.py:33
  94.8 8.0 %collective-permute-start.18 = (bf16[4,48,768]{2,1,0:T(8,128)(2,1)}, bf16[4,48,768]{2,1,0:T(8,128)(2,1)S(1)}, u32[]{:S(2)}, u32[]{:S(2)}) collective-permute-start(bf16[4,48,768]{2,1,0:T(8,128)(2,1)} %get-tuple-element.69), channel_id=1, source_target_pairs={{0,16},{16,0},{32,48},{48,32},{64,80},{80,64},{96,112},{112,96},{1... | collective-permute-start | bytes 884744 | tf_op jit(solution)/shard_map/ppermute | solution.py:33
  95.3 20.9 %all-to-all-start.1 = ((bf16[16,32,384]{2,1,0:T(8,128)(2,1)}), bf16[16,32,384]{2,1,0:T(8,128)(2,1)S(1)}, u32[]{:S(2)}, u32[]{:S(2)}) async-start(bf16[16,32,384]{2,1,0:T(8,128)(2,1)} %get-tuple-element.72), calls=%async_computation.1 | async-start | bytes 786432 | tf_op jit(solution)/shard_map/all_to_all | solution.py:80
  102.8 0.7 copy-start.8
  107.4 13.3 %collective-permute-start.19 = (bf16[192,768]{1,0:T(8,128)(2,1)}, bf16[192,768]{1,0:T(8,128)(2,1)}, u32[]{:S(2)}, u32[]{:S(2)}) collective-permute-start(bf16[192,768]{1,0:T(8,128)(2,1)} %get-tuple-element.70), channel_id=1, source_target_pairs={{0,32},{16,48},{32,64},{48,80},{64,96},{80,112},{96,0},{112,16},{1... | collective-permute-start | bytes 884744 | tf_op jit(solution)/shard_map/ppermute | solution.py:33
  108.5 12.3 %collective-permute-start.20 = (bf16[192,768]{1,0:T(8,128)(2,1)}, bf16[192,768]{1,0:T(8,128)(2,1)}, u32[]{:S(2)}, u32[]{:S(2)}) collective-permute-start(bf16[192,768]{1,0:T(8,128)(2,1)} %get-tuple-element.71), channel_id=1, source_target_pairs={{0,96},{16,112},{32,0},{48,16},{64,32},{80,48},{96,64},{112,80},{1... | collective-permute-start | bytes 884744 | tf_op jit(solution)/shard_map/ppermute | solution.py:33
  110.1 9.5 %collective-permute-start.23 = (bf16[48,768]{1,0:T(8,128)(2,1)}, bf16[48,768]{1,0:T(8,128)(2,1)}, u32[]{:S(2)}, u32[]{:S(2)}) collective-permute-start(bf16[48,768]{1,0:T(8,128)(2,1)} %get-tuple-element.105), channel_id=1, source_target_pairs={{0,96},{16,112},{32,0},{48,16},{64,32},{80,48},{96,64},{112,80},{1... | collective-permute-start | bytes 221192 | tf_op jit(solution)/shard_map/ppermute | solution.py:33
  111.7 9.1 %collective-permute-start.22 = (bf16[48,768]{1,0:T(8,128)(2,1)S(1)}, bf16[48,768]{1,0:T(8,128)(2,1)}, u32[]{:S(2)}, u32[]{:S(2)}) collective-permute-start(bf16[48,768]{1,0:T(8,128)(2,1)S(1)} %get-tuple-element.106), channel_id=1, source_target_pairs={{0,64},{16,80},{32,96},{48,112},{64,0},{80,16},{96,32},{112,48},{1... | collective-permute-start | bytes 221192 | tf_op jit(solution)/shard_map/ppermute | solution.py:33
  112.6 8.1 %collective-permute-start.21 = (bf16[48,768]{1,0:T(8,128)(2,1)S(1)}, bf16[48,768]{1,0:T(8,128)(2,1)}, u32[]{:S(2)}, u32[]{:S(2)}) collective-permute-start(bf16[48,768]{1,0:T(8,128)(2,1)S(1)} %get-tuple-element.107), channel_id=1, source_target_pairs={{0,32},{16,48},{32,64},{48,80},{64,96},{80,112},{96,0},{112,16},{1... | collective-permute-start | bytes 221192 | tf_op jit(solution)/shard_map/ppermute | solution.py:33
  123.0 12.0 %collective-permute-start.24 = (bf16[192,768]{1,0:T(8,128)(2,1)}, bf16[192,768]{1,0:T(8,128)(2,1)S(1)}, u32[]{:S(2)}, u32[]{:S(2)}) collective-permute-start(bf16[192,768]{1,0:T(8,128)(2,1)} %get-tuple-element.80), channel_id=1, source_target_pairs={{0,32},{16,48},{32,64},{48,80},{64,96},{80,112},{96,0},{112,16},{1... | collective-permute-start | bytes 884744 | tf_op jit(solution)/shard_map/ppermute | solution.py:33
  123.4 11.7 %collective-permute-start.25 = (bf16[192,768]{1,0:T(8,128)(2,1)S(1)}, bf16[192,768]{1,0:T(8,128)(2,1)S(1)}, u32[]{:S(2)}, u32[]{:S(2)}) collective-permute-start(bf16[192,768]{1,0:T(8,128)(2,1)S(1)} %fusion.4), channel_id=1, source_target_pairs={{0,96},{16,112},{32,0},{48,16},{64,32},{80,48},{96,64},{112,80},{1... | collective-permute-start | bytes 884744 | tf_op jit(solution)/shard_map/ppermute | solution.py:33
  125.6 25.5 %slice-start = ((s8[4718592]{0:T(1024)(128)(4,1)}), s8[4194304]{0:T(1024)(128)(4,1)S(1)}, s32[]{:S(2)}) async-start(s8[4718592]{0:T(1024)(128)(4,1)} %bitcast.109), calls=%async_computation.3 | async-start | bytes 8388608
  125.9 4.9 %copy-start.12 = (bf16[2,4,32,192]{3,2,1,0:T(8,128)(2,1)S(1)}, bf16[2,4,32,192]{3,2,1,0:T(8,128)(2,1)}, u32[]{:S(2)}) copy-start(bf16[2,4,32,192]{3,2,1,0:T(8,128)(2,1)} %copy-done.11) | copy-start | bytes 294916
  125.9 25.2 %slice-start.1 = ((s8[4718592]{0:T(1024)(128)(4,1)}), s8[524288]{0:T(1024)(128)(4,1)S(1)}, s32[]{:S(2)}) async-start(s8[4718592]{0:T(1024)(128)(4,1)} %bitcast.109), calls=%async_computation.4 | async-start | bytes 1048576
  126.2 8.8 %collective-permute-start.26 = (bf16[64,768]{1,0:T(8,128)(2,1)S(1)}, bf16[64,768]{1,0:T(8,128)(2,1)S(1)}, u32[]{:S(2)}, u32[]{:S(2)}) collective-permute-start(bf16[64,768]{1,0:T(8,128)(2,1)S(1)} %maximum_maximum_fusion), channel_id=1, source_target_pairs={{0,128},{16,144},{32,160},{48,176},{64,192},{80,208},{96,224},{112... | collective-permute-start | bytes 294920 | tf_op jit(solution)/shard_map/ppermute | solution.py:33
  130.8 15.9 %copy-start.5 = (bf16[32,3072]{1,0:T(8,128)(2,1)S(1)}, bf16[32,3072]{1,0:T(8,128)(2,1)}, u32[]{:S(2)}) copy-start(bf16[32,3072]{1,0:T(8,128)(2,1)} %param.6) | copy-start | bytes 589828
  130.8 15.9 %copy-start.15 = (f32[3072]{0:T(1024)S(1)}, f32[3072]{0:T(1024)}, u32[]{:S(2)}) copy-start(f32[3072]{0:T(1024)} %param.7) | copy-start | bytes 36868
  135.1 12.5 %collective-permute-start.29 = (bf16[80,768]{1,0:T(8,128)(2,1)S(1)}, bf16[80,768]{1,0:T(8,128)(2,1)S(1)}, u32[]{:S(2)}, u32[]{:S(2)}) collective-permute-start(bf16[80,768]{1,0:T(8,128)(2,1)S(1)} %pad_maximum_fusion.4.refs_0_), channel_id=1, source_target_pairs={{0,32},{16,48},{32,64},{48,80},{64,96},{80,112},{96,0},{112,16},{1... | collective-permute-start | bytes 368648 | tf_op jit(solution)/shard_map/ppermute | solution.py:33
  135.9 11.7 %collective-permute-start.28 = (bf16[80,768]{1,0:T(8,128)(2,1)S(1)}, bf16[80,768]{1,0:T(8,128)(2,1)S(1)}, u32[]{:S(2)}, u32[]{:S(2)}) collective-permute-start(bf16[80,768]{1,0:T(8,128)(2,1)S(1)} %pad_maximum_fusion.4.refs_0_), channel_id=1, source_target_pairs={{0,64},{16,80},{32,96},{48,112},{64,0},{80,16},{96,32},{112,48},{1... | collective-permute-start | bytes 368648 | tf_op jit(solution)/shard_map/ppermute | solution.py:33
  139.0 8.6 %collective-permute-start.27 = (bf16[80,768]{1,0:T(8,128)(2,1)S(1)}, bf16[80,768]{1,0:T(8,128)(2,1)S(1)}, u32[]{:S(2)}, u32[]{:S(2)}) collective-permute-start(bf16[80,768]{1,0:T(8,128)(2,1)S(1)} %pad_maximum_fusion.4.refs_0_), channel_id=1, source_target_pairs={{0,96},{16,112},{32,0},{48,16},{64,32},{80,48},{96,64},{112,80},{1... | collective-permute-start | bytes 368648 | tf_op jit(solution)/shard_map/ppermute | solution.py:33
  141.6 7.4 %copy-start.7 = (bf16[192,768]{1,0:T(8,128)(2,1)S(1)}, bf16[192,768]{1,0:T(8,128)(2,1)}, u32[]{:S(2)}) copy-start(bf16[192,768]{1,0:T(8,128)(2,1)} %get-tuple-element.99) | copy-start | bytes 884740
  141.6 9.5 %copy-start.1 = (bf16[192,384]{1,0:T(8,128)(2,1)S(1)}, bf16[192,384]{1,0:T(8,128)(2,1)}, u32[]{:S(2)}) copy-start(bf16[192,384]{1,0:T(8,128)(2,1)} %encoder.1) | copy-start | bytes 442372
  141.6 9.5 %copy-start.4 = (s32[6]{0:T(128)S(1)}, s32[6]{0:T(128)}, u32[]{:S(2)}) copy-start(s32[6]{0:T(128)} %copy-done.3) | copy-start | bytes 76
  141.7 14.0 %collective-permute-start.36 = (bf16[192,768]{1,0:T(8,128)(2,1)S(1)}, bf16[192,768]{1,0:T(8,128)(2,1)S(1)}, u32[]{:S(2)}, u32[]{:S(2)}) collective-permute-start(bf16[192,768]{1,0:T(8,128)(2,1)S(1)} %get-tuple-element.98), channel_id=1, source_target_pairs={{0,128},{16,144},{32,160},{48,176},{64,192},{80,208},{96,224},{112... | collective-permute-start | bytes 884744 | tf_op jit(solution)/shard_map/ppermute | solution.py:33
  147.6 1.4 collective-permute-start.30
  147.7 1.9 %collective-permute-start.31 = (bf16[80,768]{1,0:T(8,128)(2,1)S(1)}, bf16[80,768]{1,0:T(8,128)(2,1)S(1)}, u32[]{:S(2)}, u32[]{:S(2)}) collective-permute-start(bf16[80,768]{1,0:T(8,128)(2,1)S(1)} %collective-permute-done.27.refs_1_), channel_id=1, source_target_pairs={{0,16},{16,0},{32,48},{48,32},{64,80},{80,64},{96,112},{112,96},{1... | collective-permute-start | bytes 368648 | tf_op jit(solution)/shard_map/ppermute | solution.py:33
  148.2 2.9 %collective-permute-start.32 = (bf16[80,768]{1,0:T(8,128)(2,1)S(1)}, bf16[80,768]{1,0:T(8,128)(2,1)S(1)}, u32[]{:S(2)}, u32[]{:S(2)}) collective-permute-start(bf16[80,768]{1,0:T(8,128)(2,1)S(1)} %collective-permute-done.28.refs_2_), channel_id=1, source_target_pairs={{0,16},{16,0},{32,48},{48,32},{64,80},{80,64},{96,112},{112,96},{1... | collective-permute-start | bytes 368648 | tf_op jit(solution)/shard_map/ppermute | solution.py:33
  148.3 2.8 %collective-permute-start.33 = (bf16[80,768]{1,0:T(8,128)(2,1)S(1)}, bf16[80,768]{1,0:T(8,128)(2,1)S(1)}, u32[]{:S(2)}, u32[]{:S(2)}) collective-permute-start(bf16[80,768]{1,0:T(8,128)(2,1)S(1)} %collective-permute-done.29.refs_3_), channel_id=1, source_target_pairs={{0,16},{16,0},{32,48},{48,32},{64,80},{80,64},{96,112},{112,96},{1... | collective-permute-start | bytes 368648 | tf_op jit(solution)/shard_map/ppermute | solution.py:33
  149.1 14.3 %collective-permute-start.35 = (bf16[192,768]{1,0:T(8,128)(2,1)S(1)}, bf16[192,768]{1,0:T(8,128)(2,1)S(1)}, u32[]{:S(2)}, u32[]{:S(2)}) collective-permute-start(bf16[192,768]{1,0:T(8,128)(2,1)S(1)} %copy-done.7), channel_id=1, source_target_pairs={{0,96},{16,112},{32,0},{48,16},{64,32},{80,48},{96,64},{112,80},{1... | collective-permute-start | bytes 884744 | tf_op jit(solution)/shard_map/ppermute | solution.py:33
  149.7 13.7 %collective-permute-start.34 = (bf16[192,768]{1,0:T(8,128)(2,1)S(1)}, bf16[192,768]{1,0:T(8,128)(2,1)}, u32[]{:S(2)}, u32[]{:S(2)}) collective-permute-start(bf16[192,768]{1,0:T(8,128)(2,1)S(1)} %get-tuple-element.97), channel_id=1, source_target_pairs={{0,32},{16,48},{32,64},{48,80},{64,96},{80,112},{96,0},{112,16},{1... | collective-permute-start | bytes 884744 | tf_op jit(solution)/shard_map/ppermute | solution.py:33
  155.6 18.1 %all-to-all-start.2 = ((bf16[16,12,768]{2,1,0:T(8,128)(2,1)}), bf16[16,12,768]{2,1,0:T(8,128)(2,1)S(1)}, u32[]{:S(2)}, u32[]{:S(2)}) async-start(bf16[16,12,768]{2,1,0:T(8,128)(2,1)} %get-tuple-element.94), calls=%async_computation.2 | async-start | bytes 786432 | tf_op jit(solution)/shard_map/all_to_all | solution.py:417

commit v5 on v4

--- a/solution.py
+++ b/solution.py
@@ -74,11 +74,6 @@
     return lax.all_to_all(
         jnp.broadcast_to(code_rows, (16, count, width)), "mp", split_axis=0, concat_axis=0
     )
-
-
-def scatter_codes(part):
-    got = lax.all_to_all(part, "mp", split_axis=0, concat_axis=0)
-    return jnp.sum(got.astype(F32), axis=0)
 
 
 VMEM = 58 * 1024 * 1024
@@ -126,7 +121,7 @@
         copies = row_copies(pieces, upstream, sems)
         for c in copies:
             c.start()
-        for k in range(8):
+        for k in range(2):
             weight_copy(k).start()
         fill_rows(at, codes, rows)
         pre_act = jnp.dot(rows[...], tied[...], preferred_element_type=F32)
@@ -136,6 +131,8 @@
         total[...] = jnp.zeros_like(total)
         for c in copies:
             c.wait()
+        for k in range(2, 8):
+            weight_copy(k).start()
 
     weight_copy(step).wait()
     part = upstream[:, here]
@@ -381,14 +378,15 @@
     pieces = (line, after, far_a, far_b, before)
     keep, give, codes_part, inner, inner_give = mlp_call(at, all_codes, tied_up, w_down, pieces)
     sent = send(give, "dp", step_core)
-    grad_codes = scatter_codes(codes_part).astype(BF16)
+    grad_codes = lax.all_to_all(codes_part, "mp", split_axis=0, concat_axis=0)
     inner = add(inner, send(inner_give, "dp", step_core)).astype(BF16)
     first, second = [add(keep[2, k], sent[2, k]).astype(BF16) for k in (0, 1)]
-    first, second, inner = tie((first, second, inner))
+    first, second, inner, keep, sent = tie((first, second, inner, keep, sent))
     got_a = send(first, "dp", step_x(1))
     got_b = send(second, "dp", step_x(-1))
     got = [send(inner[k], "dp", step_x(k)) for k in (1, 2, 3)]
     got_a, got_b, grad_codes, *got = tie((got_a, got_b, grad_codes, *got))
+    grad_codes = jnp.sum(grad_codes.astype(F32), axis=0).astype(BF16)
     inner = (inner[0].astype(F32) + sum(g.astype(F32) for g in got)).astype(BF16)
     count, cols = inner.shape
     halves = jnp.split(grad_codes, 2)

time: 176 us -> 175 us (level)
  waiting for transfers between devices: 35.1 us -> 33 us
    convert_element_type x0 -> x1, other arithmetic: none -> 2.19 us  [on_device(): first, second = [add(keep[2, k], sent[2, k]).astype(BF16) for k in (0, 1)]]
  transfers between devices with their start and end apart: 40 -> 40, of which waited for: 11 -> 11; matrix products, arithmetic and copies ran while one was open for 13% -> 14% of each run, Pallas kernels for 4% -> 4%
where the time goes in v5:
time: 175 us
  starting transfers between devices  84 us (48%)
  waiting for transfers between devices  33 us (19%)
  Pallas kernels  22 us (13%)
  other arithmetic  20.7 us (12%)
  local copies, waits for them, and re-layouts  11.9 us (7%)
    ppermute x37, starting transfers between devices, send(): return lax.ppermute(value, axis, [(i, target(i)) for i in range(16)])  62.8 us
    ppermute x37, waiting for transfers between devices, send(): return lax.ppermute(value, axis, [(i, target(i)) for i in range(16)])  24.4 us
    pallas_call x1, Pallas kernels, mlp_call(): pl.pallas_call(mlp_kernel, grid_spec=pltpu.PrefetchScalarGridSpec(num_sca...  14.4 us
    all_to_all x1, waiting for transfers between devices, on_device(): both = lax.all_to_all(both, 'mp', split_axis=0, concat_axis=0)  8.17 us
    all_to_all x1, starting transfers between devices, on_device(): grad_codes = lax.all_to_all(codes_part, 'mp', split_axis=0, concat_axis=0)  7.47 us
    all_to_all x1, starting transfers between devices, on_device(): both = lax.all_to_all(both, 'mp', split_axis=0, concat_axis=0)  6.91 us
    all_to_all x1, starting transfers between devices, gather_codes(): lax.all_to_all(jnp.broadcast_to(code_rows, (16, count, width)), 'mp', spl...  6.77 us
    unnamed x42, local copies, waits for them, and re-layouts  6.19 us
  transfers between devices with their start and end apart: 40, of which 11 were waited for; matrix products, arithmetic and copies ran while one was open for 14% of the time, Pallas kernels for 4%

profile of v5, /device:TPU:2, one launch (start us, length us, event | category | flops | bytes accessed | tf_op | source)
XLA Modules:
  0.0 174.6 jit_solution(7281075883801681734)
XLA Ops:
  0.6 7.3 %collective-permute-start = (bf16[192,384]{1,0:T(8,128)(2,1)}, bf16[192,384]{1,0:T(8,128)(2,1)S(1)}, u32[]{:S(2)}, u32[]{:S(2)}) collective-permute-start(bf16[192,384]{1,0:T(8,128)(2,1)} %encoder.1), channel_id=1, source_target_pairs={{0,128},{16,144},{32,160},{48,176},{64,192},{80,208},{96,224},{112... | collective-permute-start | bytes 442376 | tf_op jit(solution)/shard_map/ppermute | solution.py:33
  7.9 1.1 convert_reduce_fusion.1
  9.0 1.2 fusion.16
  10.2 1.1 fusion.10
  11.3 0.7 collective-permute-done
  12.1 4.1 %collective-permute-start.6 = (bf16[32,3072]{1,0:T(8,128)(2,1)}, bf16[32,3072]{1,0:T(8,128)(2,1)S(1)}, u32[]{:S(2)}, u32[]{:S(2)}) collective-permute-start(bf16[32,3072]{1,0:T(8,128)(2,1)} %param.11), channel_id=1, source_target_pairs={{0,4},{1,5},{2,6},{3,7},{4,8},{5,9},{6,10},{7,11},{8,12},{9,13},{1... | collective-permute-start | bytes 589832 | tf_op jit(solution)/shard_map/ppermute | solution.py:33
  16.2 1.5 collective-permute-start.5
  17.6 2.3 %collective-permute-start.4 = (bf16[32,3072]{1,0:T(8,128)(2,1)}, bf16[32,3072]{1,0:T(8,128)(2,1)S(1)}, u32[]{:S(2)}, u32[]{:S(2)}) collective-permute-start(bf16[32,3072]{1,0:T(8,128)(2,1)} %param.11), channel_id=1, source_target_pairs={{0,12},{1,13},{2,14},{3,15},{4,0},{5,1},{6,2},{7,3},{8,4},{9,5},{1... | collective-permute-start | bytes 589832 | tf_op jit(solution)/shard_map/ppermute | solution.py:33
  19.9 0.9 select_bitcast_fusion.1
  20.9 2.2 %collective-permute-start.2 = (bf16[2,192,384]{2,1,0:T(8,128)(2,1)S(1)}, bf16[2,192,384]{2,1,0:T(8,128)(2,1)S(1)}, u32[]{:S(2)}, u32[]{:S(2)}) collective-permute-start(bf16[2,192,384]{2,1,0:T(8,128)(2,1)S(1)} %pad_maximum_fusion.1), channel_id=1, source_target_pairs={{0,64},{16,80},{32,96},{48,112},{64,0},{80,16},{96,32},{112,48},{1... | collective-permute-start | bytes 884744 | tf_op jit(solution)/shard_map/ppermute | solution.py:33
  23.1 1.4 collective-permute-start.1
  25.6 0.7 collective-permute-start.3
  26.2 3.2 %collective-permute-done.5 = bf16[32,3072]{1,0:T(8,128)(2,1)S(1)} collective-permute-done((bf16[32,3072]{1,0:T(8,128)(2,1)}, bf16[32,3072]{1,0:T(8,128)(2,1)S(1)}, u32[]{:S(2)}, u32[]{:S(2)}) %collective-permute-start.5) | collective-permute-done | bytes 196640 | tf_op jit(solution)/shard_map/ppermute | solution.py:33
  29.5 0.9 pad_maximum_fusion.refs_0_
  30.4 5.7 %collective-permute-done.1 = bf16[2,192,384]{2,1,0:T(8,128)(2,1)S(1)} collective-permute-done((bf16[2,192,384]{2,1,0:T(8,128)(2,1)S(1)}, bf16[2,192,384]{2,1,0:T(8,128)(2,1)S(1)}, u32[]{:S(2)}, u32[]{:S(2)}) %collective-permute-start.1) | collective-permute-done | bytes 294944 | tf_op jit(solution)/shard_map/ppermute | solution.py:33
  38.0 1.7 collective-permute-start.10
  39.7 1.7 collective-permute-start.9
  42.0 0.8 broadcast_in_dim.2
  42.8 6.8 %all-to-all-start = ((bf16[16,32,384]{2,1,0:T(8,128)(2,1)}), bf16[16,32,384]{2,1,0:T(8,128)(2,1)}, u32[]{:S(2)}, u32[]{:S(2)}) async-start(bf16[16,32,384]{2,1,0:T(8,128)(2,1)} %broadcast_in_dim.2), calls=%async_computation | async-start | bytes 786432 | tf_op jit(solution)/shard_map/all_to_all | solution.py:74
  49.9 1.8 %collective-permute-start.13 = (bf16[2,2,32,192]{3,2,1,0:T(8,128)(2,1)S(1)}, bf16[2,2,32,192]{3,2,1,0:T(8,128)(2,1)S(1)}, u32[]{:S(2)}, u32[]{:S(2)}) collective-permute-start(bf16[2,2,32,192]{3,2,1,0:T(8,128)(2,1)S(1)} %bitcast.130), channel_id=1, source_target_pairs={{0,96},{16,112},{32,0},{48,16},{64,32},{80,48},{96,64},{112,80},{1... | collective-permute-start | bytes 147464 | tf_op jit(solution)/shard_map/ppermute | solution.py:33
  51.7 1.2 collective-permute-start.12
  52.9 1.8 %collective-permute-start.11 = (bf16[2,2,32,192]{3,2,1,0:T(8,128)(2,1)S(1)}, bf16[2,2,32,192]{3,2,1,0:T(8,128)(2,1)S(1)}, u32[]{:S(2)}, u32[]{:S(2)}) collective-permute-start(bf16[2,2,32,192]{3,2,1,0:T(8,128)(2,1)S(1)} %bitcast.128), channel_id=1, source_target_pairs={{0,32},{16,48},{32,64},{48,80},{64,96},{80,112},{96,0},{112,16},{1... | collective-permute-start | bytes 147464 | tf_op jit(solution)/shard_map/ppermute | solution.py:33
  54.8 2.3 %copy-done = bf16[3072,768]{1,0:T(8,128)(2,1)S(1)} copy-done((bf16[3072,768]{1,0:T(8,128)(2,1)S(1)}, bf16[3072,768]{1,0:T(8,128)(2,1)}, u32[]{:S(2)}) %copy-start) | copy-done | bytes 4718616
  57.1 5.6 %shard_map.101.tied = bf16[384,768]{1,0:T(8,128)(2,1)S(1)} custom-call(s32[6]{0:T(128)S(1)} %stack.96.at, bf16[8,192,384]{2,1,0:T(8,128)(2,1)S(1)} %bitcast.113, bf16[8,192,384]{2,1,0:T(8,128)(2,1)S(1)} %bitcast.115, bf16[3072,768]{1,0:T(8,128)(2,1)S(1)} %copy-done), custom_call_target="tpu_custom_call" | custom-call | flops 1811939328 | bytes 9437184 | tf_op jit(solution)/shard_map/pallas_call | solution.py:250
  62.7 0.8 copy-done.2
  64.2 1.0 slice.82
  65.2 1.0 slice.83
  66.2 1.9 %collective-permute-start.15 = (bf16[64,3072]{1,0:T(8,128)(2,1)S(1)}, bf16[64,3072]{1,0:T(8,128)(2,1)}, u32[]{:S(2)}, u32[]{:S(2)}) collective-permute-start(bf16[64,3072]{1,0:T(8,128)(2,1)S(1)} %slice.83), channel_id=1, source_target_pairs={{0,1},{1,2},{2,3},{3,0},{4,5},{5,6},{6,7},{7,4},{8,9},{9,10},{10,1... | collective-permute-start | bytes 1179656 | tf_op jit(solution)/shard_map/ppermute | solution.py:33
  68.1 1.4 collective-permute-start.14
  69.6 0.9 pad_maximum_fusion.2
  70.6 5.3 %collective-permute-start.16 = (bf16[2,4,32,192]{3,2,1,0:T(8,128)(2,1)S(1)}, bf16[2,4,32,192]{3,2,1,0:T(8,128)(2,1)S(1)}, u32[]{:S(2)}, u32[]{:S(2)}) collective-permute-start(bf16[2,4,32,192]{3,2,1,0:T(8,128)(2,1)S(1)} %bitcast.125), channel_id=1, source_target_pairs={{0,128},{16,144},{32,160},{48,176},{64,192},{80,208},{96,224},{112... | collective-permute-start | bytes 294920 | tf_op jit(solution)/shard_map/ppermute | solution.py:33
  75.8 3.8 %collective-permute-done.16 = bf16[2,4,32,192]{3,2,1,0:T(8,128)(2,1)S(1)} collective-permute-done((bf16[2,4,32,192]{3,2,1,0:T(8,128)(2,1)S(1)}, bf16[2,4,32,192]{3,2,1,0:T(8,128)(2,1)S(1)}, u32[]{:S(2)}, u32[]{:S(2)}) %collective-permute-start.16) | collective-permute-done | bytes 98336 | tf_op jit(solution)/shard_map/ppermute | solution.py:33
  80.3 14.4 %shard_map.102 = (bf16[4,2,192,768]{3,2,1,0:T(8,128)(2,1)}, bf16[4,2,192,768]{3,2,1,0:T(8,128)(2,1)}, bf16[16,32,384]{2,1,0:T(8,128)(2,1)}, bf16[4,48,768]{2,1,0:T(8,128)(2,1)}, bf16[4,48,768]{2,1,0:T(8,128)(2,1)}) custom-call(s32[6]{0:T(128)} %copy-done.3, bf16[16,32,384]{2,1,0:T(8,128)(2,1)} %all-to-all-done.codes, bf16[384,768]{1,0:T(8,128)(2,1)} %copy-done.2, ...), custom_call_target="tpu_custom_call" | custom-call | flops 5435817984 | bytes 17301504 | tf_op jit(solution)/shard_map/pallas_call | solution.py:192
  95.3 7.5 %all-to-all-start.1 = ((bf16[16,32,384]{2,1,0:T(8,128)(2,1)}), bf16[16,32,384]{2,1,0:T(8,128)(2,1)S(1)}, u32[]{:S(2)}, u32[]{:S(2)}) async-start(bf16[16,32,384]{2,1,0:T(8,128)(2,1)} %get-tuple-element.74), calls=%async_computation.1 | async-start | bytes 786432 | tf_op jit(solution)/shard_map/all_to_all | solution.py:381
  102.8 0.7 copy-done.8
  103.5 1.1 add_convert_fusion.2
  104.6 2.2 %fusion.18 = (bf16[192,768]{1,0:T(8,128)(2,1)}, bf16[192,768]{1,0:T(8,128)(2,1)}) fusion(bf16[4,2,192,768]{3,2,1,0:T(8,128)(2,1)} %collective-permute-done.17, bf16[4,2,192,768]{3,2,1,0:T(8,128)(2,1)} %get-tuple-element.81), kind=kLoop, calls=%fused_computation.44 | loop fusion | flops 1179648 | bytes 1769472 | tf_op jit(solution)/shard_map/convert_element_type | solution.py:383
  106.8 1.1 collective-permute-start.19
  107.9 0.9 collective-permute-start.20
  109.5 1.6 collective-permute-start.23
  111.1 1.0 collective-permute-start.22
  112.0 1.5 collective-permute-start.21
  113.5 2.2 %fusion.20 = (bf16[192,768]{1,0:T(8,128)(2,1)}, bf16[192,768]{1,0:T(8,128)(2,1)}) fusion(bf16[4,2,192,768]{3,2,1,0:T(8,128)(2,1)} %collective-permute-done.17, bf16[4,2,192,768]{3,2,1,0:T(8,128)(2,1)} %get-tuple-element.81), kind=kLoop, calls=%fused_computation.46 | loop fusion | flops 1179648 | bytes 1769472 | tf_op jit(solution)/shard_map/convert_element_type | solution.py:407
  116.2 2.9 %collective-permute-done.23 = bf16[48,768]{1,0:T(8,128)(2,1)} collective-permute-done((bf16[48,768]{1,0:T(8,128)(2,1)}, bf16[48,768]{1,0:T(8,128)(2,1)}, u32[]{:S(2)}, u32[]{:S(2)}) %collective-permute-start.23) | collective-permute-done | bytes 73760 | tf_op jit(solution)/shard_map/ppermute | solution.py:33
  119.0 1.1 collective-permute-done.22
  120.2 1.3 fusion.4
  121.5 1.0 fusion.21
  122.8 2.0 %collective-permute-start.25 = (bf16[192,768]{1,0:T(8,128)(2,1)S(1)}, bf16[192,768]{1,0:T(8,128)(2,1)S(1)}, u32[]{:S(2)}, u32[]{:S(2)}) collective-permute-start(bf16[192,768]{1,0:T(8,128)(2,1)S(1)} %fusion.4), channel_id=1, source_target_pairs={{0,96},{16,112},{32,0},{48,16},{64,32},{80,48},{96,64},{112,80},{1... | collective-permute-start | bytes 884744 | tf_op jit(solution)/shard_map/ppermute | solution.py:33
  125.7 4.6 %collective-permute-start.26 = (bf16[64,768]{1,0:T(8,128)(2,1)S(1)}, bf16[64,768]{1,0:T(8,128)(2,1)S(1)}, u32[]{:S(2)}, u32[]{:S(2)}) collective-permute-start(bf16[64,768]{1,0:T(8,128)(2,1)S(1)} %maximum_maximum_fusion), channel_id=1, source_target_pairs={{0,128},{16,144},{32,160},{48,176},{64,192},{80,208},{96,224},{112... | collective-permute-start | bytes 294920 | tf_op jit(solution)/shard_map/ppermute | solution.py:33
  130.3 4.1 %collective-permute-done.26 = bf16[64,768]{1,0:T(8,128)(2,1)S(1)} collective-permute-done((bf16[64,768]{1,0:T(8,128)(2,1)S(1)}, bf16[64,768]{1,0:T(8,128)(2,1)S(1)}, u32[]{:S(2)}, u32[]{:S(2)}) %collective-permute-start.26) | collective-permute-done | bytes 98336 | tf_op jit(solution)/shard_map/ppermute | solution.py:33
  134.5 0.9 collective-permute-start.29
  135.4 3.1 %collective-permute-start.28 = (bf16[80,768]{1,0:T(8,128)(2,1)S(1)}, bf16[80,768]{1,0:T(8,128)(2,1)S(1)}, u32[]{:S(2)}, u32[]{:S(2)}) collective-permute-start(bf16[80,768]{1,0:T(8,128)(2,1)S(1)} %pad_maximum_fusion.4.refs_0_), channel_id=1, source_target_pairs={{0,64},{16,80},{32,96},{48,112},{64,0},{80,16},{96,32},{112,48},{1... | collective-permute-start | bytes 368648 | tf_op jit(solution)/shard_map/ppermute | solution.py:33
  138.5 1.0 collective-permute-start.27
  139.5 1.6 fusion.2
  141.1 5.0 %collective-permute-start.36 = (bf16[192,768]{1,0:T(8,128)(2,1)S(1)}, bf16[192,768]{1,0:T(8,128)(2,1)S(1)}, u32[]{:S(2)}, u32[]{:S(2)}) collective-permute-start(bf16[192,768]{1,0:T(8,128)(2,1)S(1)} %get-tuple-element.102), channel_id=1, source_target_pairs={{0,128},{16,144},{32,160},{48,176},{64,192},{80,208},{96,224},{112... | collective-permute-start | bytes 884744 | tf_op jit(solution)/shard_map/ppermute | solution.py:33
  146.1 0.9 fusion.33
  149.1 1.4 collective-permute-start.34
  150.6 2.1 %shard_map.103 = (bf16[16,12,768]{2,1,0:T(8,128)(2,1)}, f32[192,768]{1,0:T(8,128)}) custom-call(s32[6]{0:T(128)S(1)} %copy-done.4, bf16[512,192]{1,0:T(8,128)(2,1)S(1)} %bitcast.116, bf16[3072,768]{1,0:T(8,128)(2,1)S(1)} %bitcast.110, bf16[192,384]{1,0:T(8,128)(2,1)S(1)} %copy-done.1, bf16[80,768]{1,0:T(8,128)(2,1)S(1)} %pad_maximum_fusion.4.refs_0_, ...), custom_call_target="tpu_custom_call" | custom-call | flops 301989888 | bytes 1081344 | tf_op jit(solution)/shard_map/pallas_call | solution.py:306
  152.7 2.4 %collective-permute-done.36 = bf16[192,768]{1,0:T(8,128)(2,1)S(1)} collective-permute-done((bf16[192,768]{1,0:T(8,128)(2,1)S(1)}, bf16[192,768]{1,0:T(8,128)(2,1)S(1)}, u32[]{:S(2)}, u32[]{:S(2)}) %collective-permute-start.36) | collective-permute-done | bytes 294944 | tf_op jit(solution)/shard_map/ppermute | solution.py:33
  155.1 6.9 %all-to-all-start.2 = ((bf16[16,12,768]{2,1,0:T(8,128)(2,1)}), bf16[16,12,768]{2,1,0:T(8,128)(2,1)S(1)}, u32[]{:S(2)}, u32[]{:S(2)}) async-start(bf16[16,12,768]{2,1,0:T(8,128)(2,1)} %get-tuple-element.98), calls=%async_computation.2 | async-start | bytes 786432 | tf_op jit(solution)/shard_map/all_to_all | solution.py:415
  162.0 0.9 fusion.15
  162.9 2.1 %fusion.3 = f32[192,768]{1,0:T(8,128)} fusion(bf16[192,768]{1,0:T(8,128)(2,1)S(1)} %collective-permute-done.36, bf16[192,768]{1,0:T(8,128)(2,1)S(1)} %collective-permute-done.35, bf16[192,768]{1,0:T(8,128)(2,1)} %collective-permute-done.34, bf16[4,2,192,768]{3,2,1,0:T(8,128)(2,1)} %collective-permute-done.17, bf16[4,2,192,768]{3,2,1,0:T(8,128)(2,1)} %get-tuple-element.81), kind=kLoop, calls=%fused_computation.13 | loop fusion | flops 1327104 | bytes 2064384 | tf_op jit(solution)/shard_map/add | solution.py:414
  165.0 8.2 %all-to-all-done.2 = bf16[16,12,768]{2,1,0:T(8,128)(2,1)S(1)} async-done(((bf16[16,12,768]{2,1,0:T(8,128)(2,1)}), bf16[16,12,768]{2,1,0:T(8,128)(2,1)S(1)}, u32[]{:S(2)}, u32[]{:S(2)}) %all-to-all-start.2) | async-done | bytes 294944 | tf_op jit(solution)/shard_map/all_to_all | solution.py:415
  173.2 0.7 multiply_reduce_fusion
  (120 shorter events, 10.8 us)
Async XLA Ops:
  0.6 11.4 %collective-permute-start = (bf16[192,384]{1,0:T(8,128)(2,1)}, bf16[192,384]{1,0:T(8,128)(2,1)S(1)}, u32[]{:S(2)}, u32[]{:S(2)}) collective-permute-start(bf16[192,384]{1,0:T(8,128)(2,1)} %encoder.1), channel_id=1, source_target_pairs={{0,128},{16,144},{32,160},{48,176},{64,192},{80,208},{96,224},{112... | collective-permute-start | bytes 442376 | tf_op jit(solution)/shard_map/ppermute | solution.py:33
  10.1 19.3 %copy-start.6 = (bf16[32,3072]{1,0:T(8,128)(2,1)S(1)}, bf16[32,3072]{1,0:T(8,128)(2,1)}, u32[]{:S(2)}) copy-start(bf16[32,3072]{1,0:T(8,128)(2,1)} %param.11) | copy-start | bytes 589828
  12.1 13.5 %collective-permute-start.6 = (bf16[32,3072]{1,0:T(8,128)(2,1)}, bf16[32,3072]{1,0:T(8,128)(2,1)S(1)}, u32[]{:S(2)}, u32[]{:S(2)}) collective-permute-start(bf16[32,3072]{1,0:T(8,128)(2,1)} %param.11), channel_id=1, source_target_pairs={{0,4},{1,5},{2,6},{3,7},{4,8},{5,9},{6,10},{7,11},{8,12},{9,13},{1... | collective-permute-start | bytes 589832 | tf_op jit(solution)/shard_map/ppermute | solution.py:33
  16.2 13.3 %collective-permute-start.5 = (bf16[32,3072]{1,0:T(8,128)(2,1)}, bf16[32,3072]{1,0:T(8,128)(2,1)S(1)}, u32[]{:S(2)}, u32[]{:S(2)}) collective-permute-start(bf16[32,3072]{1,0:T(8,128)(2,1)} %param.11), channel_id=1, source_target_pairs={{0,8},{1,9},{2,10},{3,11},{4,12},{5,13},{6,14},{7,15},{8,0},{9,1},... | collective-permute-start | bytes 589832 | tf_op jit(solution)/shard_map/ppermute | solution.py:33
  17.6 11.8 %collective-permute-start.4 = (bf16[32,3072]{1,0:T(8,128)(2,1)}, bf16[32,3072]{1,0:T(8,128)(2,1)S(1)}, u32[]{:S(2)}, u32[]{:S(2)}) collective-permute-start(bf16[32,3072]{1,0:T(8,128)(2,1)} %param.11), channel_id=1, source_target_pairs={{0,12},{1,13},{2,14},{3,15},{4,0},{5,1},{6,2},{7,3},{8,4},{9,5},{1... | collective-permute-start | bytes 589832 | tf_op jit(solution)/shard_map/ppermute | solution.py:33
  20.9 15.3 %collective-permute-start.2 = (bf16[2,192,384]{2,1,0:T(8,128)(2,1)S(1)}, bf16[2,192,384]{2,1,0:T(8,128)(2,1)S(1)}, u32[]{:S(2)}, u32[]{:S(2)}) collective-permute-start(bf16[2,192,384]{2,1,0:T(8,128)(2,1)S(1)} %pad_maximum_fusion.1), channel_id=1, source_target_pairs={{0,64},{16,80},{32,96},{48,112},{64,0},{80,16},{96,32},{112,48},{1... | collective-permute-start | bytes 884744 | tf_op jit(solution)/shard_map/ppermute | solution.py:33
  23.1 13.0 %collective-permute-start.1 = (bf16[2,192,384]{2,1,0:T(8,128)(2,1)S(1)}, bf16[2,192,384]{2,1,0:T(8,128)(2,1)S(1)}, u32[]{:S(2)}, u32[]{:S(2)}) collective-permute-start(bf16[2,192,384]{2,1,0:T(8,128)(2,1)S(1)} %pad_maximum_fusion.1), channel_id=1, source_target_pairs={{0,96},{16,112},{32,0},{48,16},{64,32},{80,48},{96,64},{112,80},{1... | collective-permute-start | bytes 884744 | tf_op jit(solution)/shard_map/ppermute | solution.py:33
  25.6 10.7 %collective-permute-start.3 = (bf16[2,192,384]{2,1,0:T(8,128)(2,1)S(1)}, bf16[2,192,384]{2,1,0:T(8,128)(2,1)S(1)}, u32[]{:S(2)}, u32[]{:S(2)}) collective-permute-start(bf16[2,192,384]{2,1,0:T(8,128)(2,1)S(1)} %pad_maximum_fusion.1), channel_id=1, source_target_pairs={{0,32},{16,48},{32,64},{48,80},{64,96},{80,112},{96,0},{112,16},{1... | collective-permute-start | bytes 884744 | tf_op jit(solution)/shard_map/ppermute | solution.py:33
  29.5 7.2 %collective-permute-start.7 = (bf16[4,2,32,192]{3,2,1,0:T(8,128)(2,1)S(1)}, bf16[4,2,32,192]{3,2,1,0:T(8,128)(2,1)S(1)}, u32[]{:S(2)}, u32[]{:S(2)}) collective-permute-start(bf16[4,2,32,192]{3,2,1,0:T(8,128)(2,1)S(1)} %bitcast.124), channel_id=1, source_target_pairs={{0,16},{16,0},{32,48},{48,32},{64,80},{80,64},{96,112},{112,96},{1... | collective-permute-start | bytes 294920 | tf_op jit(solution)/shard_map/ppermute | solution.py:33
  36.6 0.7 copy-start.9
  37.3 4.1 %collective-permute-start.8 = (bf16[1536,384]{1,0:T(8,128)(2,1)S(1)}, bf16[1536,384]{1,0:T(8,128)(2,1)S(1)}, u32[]{:S(2)}, u32[]{:S(2)}) collective-permute-start(bf16[1536,384]{1,0:T(8,128)(2,1)S(1)} %bitcast.111), channel_id=1, source_target_pairs={{0,16},{16,0},{32,48},{48,32},{64,80},{80,64},{96,112},{112,96},{1... | collective-permute-start | bytes 3538952 | tf_op jit(solution)/shard_map/ppermute | solution.py:33
  38.0 11.8 %copy-start.10 = (bf16[4,2,32,192]{3,2,1,0:T(8,128)(2,1)S(1)}, bf16[4,2,32,192]{3,2,1,0:T(8,128)(2,1)}, u32[]{:S(2)}) copy-start(bf16[4,2,32,192]{3,2,1,0:T(8,128)(2,1)} %copy-done.9) | copy-start | bytes 294916
  38.0 25.5 %collective-permute-start.10 = (bf16[128,3072]{1,0:T(8,128)(2,1)}, bf16[128,3072]{1,0:T(8,128)(2,1)}, u32[]{:S(2)}, u32[]{:S(2)}) collective-permute-start(bf16[128,3072]{1,0:T(8,128)(2,1)} %pad_maximum_fusion.refs_0_), channel_id=1, source_target_pairs={{0,1},{1,2},{2,3},{3,0},{4,5},{5,6},{6,7},{7,4},{8,9},{9,10},{10,1... | collective-permute-start | bytes 2359304 | tf_op jit(solution)/shard_map/ppermute | solution.py:33
  39.7 24.5 %collective-permute-start.9 = (bf16[128,3072]{1,0:T(8,128)(2,1)}, bf16[128,3072]{1,0:T(8,128)(2,1)}, u32[]{:S(2)}, u32[]{:S(2)}) collective-permute-start(bf16[128,3072]{1,0:T(8,128)(2,1)} %pad_maximum_fusion.refs_0_), channel_id=1, source_target_pairs={{0,3},{1,0},{2,1},{3,2},{4,7},{5,4},{6,5},{7,6},{8,11},{9,8},{10,9... | collective-permute-start | bytes 2359304 | tf_op jit(solution)/shard_map/ppermute | solution.py:33
  42.8 37.5 %all-to-all-start = ((bf16[16,32,384]{2,1,0:T(8,128)(2,1)}), bf16[16,32,384]{2,1,0:T(8,128)(2,1)}, u32[]{:S(2)}, u32[]{:S(2)}) async-start(bf16[16,32,384]{2,1,0:T(8,128)(2,1)} %broadcast_in_dim.2), calls=%async_computation | async-start | bytes 786432 | tf_op jit(solution)/shard_map/all_to_all | solution.py:74
  49.7 13.0 %copy-start.3 = (s32[6]{0:T(128)}, s32[6]{0:T(128)S(1)}, u32[]{:S(2)}) copy-start(s32[6]{0:T(128)S(1)} %stack.96.at) | copy-start | bytes 76
  49.9 13.6 %collective-permute-start.13 = (bf16[2,2,32,192]{3,2,1,0:T(8,128)(2,1)S(1)}, bf16[2,2,32,192]{3,2,1,0:T(8,128)(2,1)S(1)}, u32[]{:S(2)}, u32[]{:S(2)}) collective-permute-start(bf16[2,2,32,192]{3,2,1,0:T(8,128)(2,1)S(1)} %bitcast.130), channel_id=1, source_target_pairs={{0,96},{16,112},{32,0},{48,16},{64,32},{80,48},{96,64},{112,80},{1... | collective-permute-start | bytes 147464 | tf_op jit(solution)/shard_map/ppermute | solution.py:33
  51.7 11.8 %collective-permute-start.12 = (bf16[2,2,32,192]{3,2,1,0:T(8,128)(2,1)S(1)}, bf16[2,2,32,192]{3,2,1,0:T(8,128)(2,1)S(1)}, u32[]{:S(2)}, u32[]{:S(2)}) collective-permute-start(bf16[2,2,32,192]{3,2,1,0:T(8,128)(2,1)S(1)} %bitcast.129), channel_id=1, source_target_pairs={{0,64},{16,80},{32,96},{48,112},{64,0},{80,16},{96,32},{112,48},{1... | collective-permute-start | bytes 147464 | tf_op jit(solution)/shard_map/ppermute | solution.py:33
  52.9 10.6 %collective-permute-start.11 = (bf16[2,2,32,192]{3,2,1,0:T(8,128)(2,1)S(1)}, bf16[2,2,32,192]{3,2,1,0:T(8,128)(2,1)S(1)}, u32[]{:S(2)}, u32[]{:S(2)}) collective-permute-start(bf16[2,2,32,192]{3,2,1,0:T(8,128)(2,1)S(1)} %bitcast.128), channel_id=1, source_target_pairs={{0,32},{16,48},{32,64},{48,80},{64,96},{80,112},{96,0},{112,16},{1... | collective-permute-start | bytes 147464 | tf_op jit(solution)/shard_map/ppermute | solution.py:33
  54.8 2.3 %copy-start = (bf16[3072,768]{1,0:T(8,128)(2,1)S(1)}, bf16[3072,768]{1,0:T(8,128)(2,1)}, u32[]{:S(2)}) copy-start(bf16[3072,768]{1,0:T(8,128)(2,1)} %w_up.3) | copy-start | bytes 14155780
  62.7 0.8 copy-start.2
  63.5 6.0 %copy-start.13 = (bf16[2,2,32,192]{3,2,1,0:T(8,128)(2,1)}, bf16[2,2,32,192]{3,2,1,0:T(8,128)(2,1)S(1)}, u32[]{:S(2)}) copy-start(bf16[2,2,32,192]{3,2,1,0:T(8,128)(2,1)S(1)} %collective-permute-done.12) | copy-start | bytes 147460
  63.6 0.6 copy-start.14
  66.2 13.4 %collective-permute-start.15 = (bf16[64,3072]{1,0:T(8,128)(2,1)S(1)}, bf16[64,3072]{1,0:T(8,128)(2,1)}, u32[]{:S(2)}, u32[]{:S(2)}) collective-permute-start(bf16[64,3072]{1,0:T(8,128)(2,1)S(1)} %slice.83), channel_id=1, source_target_pairs={{0,1},{1,2},{2,3},{3,0},{4,5},{5,6},{6,7},{7,4},{8,9},{9,10},{10,1... | collective-permute-start | bytes 1179656 | tf_op jit(solution)/shard_map/ppermute | solution.py:33
  68.1 12.2 %collective-permute-start.14 = (bf16[64,3072]{1,0:T(8,128)(2,1)S(1)}, bf16[64,3072]{1,0:T(8,128)(2,1)}, u32[]{:S(2)}, u32[]{:S(2)}) collective-permute-start(bf16[64,3072]{1,0:T(8,128)(2,1)S(1)} %slice.82), channel_id=1, source_target_pairs={{0,3},{1,0},{2,1},{3,2},{4,7},{5,4},{6,5},{7,6},{8,11},{9,8},{10,9... | collective-permute-start | bytes 1179656 | tf_op jit(solution)/shard_map/ppermute | solution.py:33
  70.6 9.1 %collective-permute-start.16 = (bf16[2,4,32,192]{3,2,1,0:T(8,128)(2,1)S(1)}, bf16[2,4,32,192]{3,2,1,0:T(8,128)(2,1)S(1)}, u32[]{:S(2)}, u32[]{:S(2)}) collective-permute-start(bf16[2,4,32,192]{3,2,1,0:T(8,128)(2,1)S(1)} %bitcast.125), channel_id=1, source_target_pairs={{0,128},{16,144},{32,160},{48,176},{64,192},{80,208},{96,224},{112... | collective-permute-start | bytes 294920 | tf_op jit(solution)/shard_map/ppermute | solution.py:33
  79.6 0.7 copy-start.11
  94.7 9.9 %collective-permute-start.17 = (bf16[4,2,192,768]{3,2,1,0:T(8,128)(2,1)}, bf16[4,2,192,768]{3,2,1,0:T(8,128)(2,1)}, u32[]{:S(2)}, u32[]{:S(2)}) collective-permute-start(bf16[4,2,192,768]{3,2,1,0:T(8,128)(2,1)} %get-tuple-element.69), channel_id=1, source_target_pairs={{0,16},{16,0},{32,48},{48,32},{64,80},{80,64},{96,112},{112,96},{1... | collective-permute-start | bytes 7077896 | tf_op jit(solution)/shard_map/ppermute | solution.py:33
  94.8 8.0 %collective-permute-start.18 = (bf16[4,48,768]{2,1,0:T(8,128)(2,1)}, bf16[4,48,768]{2,1,0:T(8,128)(2,1)S(1)}, u32[]{:S(2)}, u32[]{:S(2)}) collective-permute-start(bf16[4,48,768]{2,1,0:T(8,128)(2,1)} %get-tuple-element.71), channel_id=1, source_target_pairs={{0,16},{16,0},{32,48},{48,32},{64,80},{80,64},{96,112},{112,96},{1... | collective-permute-start | bytes 884744 | tf_op jit(solution)/shard_map/ppermute | solution.py:33
  95.3 20.9 %all-to-all-start.1 = ((bf16[16,32,384]{2,1,0:T(8,128)(2,1)}), bf16[16,32,384]{2,1,0:T(8,128)(2,1)S(1)}, u32[]{:S(2)}, u32[]{:S(2)}) async-start(bf16[16,32,384]{2,1,0:T(8,128)(2,1)} %get-tuple-element.74), calls=%async_computation.1 | async-start | bytes 786432 | tf_op jit(solution)/shard_map/all_to_all | solution.py:381
  102.8 0.7 copy-start.8
  106.8 13.3 %collective-permute-start.19 = (bf16[192,768]{1,0:T(8,128)(2,1)}, bf16[192,768]{1,0:T(8,128)(2,1)}, u32[]{:S(2)}, u32[]{:S(2)}) collective-permute-start(bf16[192,768]{1,0:T(8,128)(2,1)} %get-tuple-element.72), channel_id=1, source_target_pairs={{0,32},{16,48},{32,64},{48,80},{64,96},{80,112},{96,0},{112,16},{1... | collective-permute-start | bytes 884744 | tf_op jit(solution)/shard_map/ppermute | solution.py:33
  107.9 12.3 %collective-permute-start.20 = (bf16[192,768]{1,0:T(8,128)(2,1)}, bf16[192,768]{1,0:T(8,128)(2,1)}, u32[]{:S(2)}, u32[]{:S(2)}) collective-permute-start(bf16[192,768]{1,0:T(8,128)(2,1)} %get-tuple-element.73), channel_id=1, source_target_pairs={{0,96},{16,112},{32,0},{48,16},{64,32},{80,48},{96,64},{112,80},{1... | collective-permute-start | bytes 884744 | tf_op jit(solution)/shard_map/ppermute | solution.py:33
  109.5 9.6 %collective-permute-start.23 = (bf16[48,768]{1,0:T(8,128)(2,1)}, bf16[48,768]{1,0:T(8,128)(2,1)}, u32[]{:S(2)}, u32[]{:S(2)}) collective-permute-start(bf16[48,768]{1,0:T(8,128)(2,1)} %get-tuple-element.109), channel_id=1, source_target_pairs={{0,96},{16,112},{32,0},{48,16},{64,32},{80,48},{96,64},{112,80},{1... | collective-permute-start | bytes 221192 | tf_op jit(solution)/shard_map/ppermute | solution.py:33
  111.1 9.1 %collective-permute-start.22 = (bf16[48,768]{1,0:T(8,128)(2,1)S(1)}, bf16[48,768]{1,0:T(8,128)(2,1)}, u32[]{:S(2)}, u32[]{:S(2)}) collective-permute-start(bf16[48,768]{1,0:T(8,128)(2,1)S(1)} %get-tuple-element.110), channel_id=1, source_target_pairs={{0,64},{16,80},{32,96},{48,112},{64,0},{80,16},{96,32},{112,48},{1... | collective-permute-start | bytes 221192 | tf_op jit(solution)/shard_map/ppermute | solution.py:33
  112.0 8.1 %collective-permute-start.21 = (bf16[48,768]{1,0:T(8,128)(2,1)S(1)}, bf16[48,768]{1,0:T(8,128)(2,1)}, u32[]{:S(2)}, u32[]{:S(2)}) collective-permute-start(bf16[48,768]{1,0:T(8,128)(2,1)S(1)} %get-tuple-element.111), channel_id=1, source_target_pairs={{0,32},{16,48},{32,64},{48,80},{64,96},{80,112},{96,0},{112,16},{1... | collective-permute-start | bytes 221192 | tf_op jit(solution)/shard_map/ppermute | solution.py:33
  122.5 12.0 %collective-permute-start.24 = (bf16[192,768]{1,0:T(8,128)(2,1)}, bf16[192,768]{1,0:T(8,128)(2,1)S(1)}, u32[]{:S(2)}, u32[]{:S(2)}) collective-permute-start(bf16[192,768]{1,0:T(8,128)(2,1)} %get-tuple-element.84), channel_id=1, source_target_pairs={{0,32},{16,48},{32,64},{48,80},{64,96},{80,112},{96,0},{112,16},{1... | collective-permute-start | bytes 884744 | tf_op jit(solution)/shard_map/ppermute | solution.py:33
  122.8 11.7 %collective-permute-start.25 = (bf16[192,768]{1,0:T(8,128)(2,1)S(1)}, bf16[192,768]{1,0:T(8,128)(2,1)S(1)}, u32[]{:S(2)}, u32[]{:S(2)}) collective-permute-start(bf16[192,768]{1,0:T(8,128)(2,1)S(1)} %fusion.4), channel_id=1, source_target_pairs={{0,96},{16,112},{32,0},{48,16},{64,32},{80,48},{96,64},{112,80},{1... | collective-permute-start | bytes 884744 | tf_op jit(solution)/shard_map/ppermute | solution.py:33
  125.1 25.5 %slice-start = ((s8[4718592]{0:T(1024)(128)(4,1)}), s8[4194304]{0:T(1024)(128)(4,1)S(1)}, s32[]{:S(2)}) async-start(s8[4718592]{0:T(1024)(128)(4,1)} %bitcast.109), calls=%async_computation.3 | async-start | bytes 8388608
  125.4 4.9 %copy-start.12 = (bf16[2,4,32,192]{3,2,1,0:T(8,128)(2,1)S(1)}, bf16[2,4,32,192]{3,2,1,0:T(8,128)(2,1)}, u32[]{:S(2)}) copy-start(bf16[2,4,32,192]{3,2,1,0:T(8,128)(2,1)} %copy-done.11) | copy-start | bytes 294916
  125.4 25.2 %slice-start.1 = ((s8[4718592]{0:T(1024)(128)(4,1)}), s8[524288]{0:T(1024)(128)(4,1)S(1)}, s32[]{:S(2)}) async-start(s8[4718592]{0:T(1024)(128)(4,1)} %bitcast.109), calls=%async_computation.4 | async-start | bytes 1048576
  125.7 8.8 %collective-permute-start.26 = (bf16[64,768]{1,0:T(8,128)(2,1)S(1)}, bf16[64,768]{1,0:T(8,128)(2,1)S(1)}, u32[]{:S(2)}, u32[]{:S(2)}) collective-permute-start(bf16[64,768]{1,0:T(8,128)(2,1)S(1)} %maximum_maximum_fusion), channel_id=1, source_target_pairs={{0,128},{16,144},{32,160},{48,176},{64,192},{80,208},{96,224},{112... | collective-permute-start | bytes 294920 | tf_op jit(solution)/shard_map/ppermute | solution.py:33
  130.2 15.9 %copy-start.5 = (bf16[32,3072]{1,0:T(8,128)(2,1)S(1)}, bf16[32,3072]{1,0:T(8,128)(2,1)}, u32[]{:S(2)}) copy-start(bf16[32,3072]{1,0:T(8,128)(2,1)} %param.6) | copy-start | bytes 589828
  130.3 15.9 %copy-start.15 = (f32[3072]{0:T(1024)S(1)}, f32[3072]{0:T(1024)}, u32[]{:S(2)}) copy-start(f32[3072]{0:T(1024)} %param.7) | copy-start | bytes 36868
  134.5 12.5 %collective-permute-start.29 = (bf16[80,768]{1,0:T(8,128)(2,1)S(1)}, bf16[80,768]{1,0:T(8,128)(2,1)S(1)}, u32[]{:S(2)}, u32[]{:S(2)}) collective-permute-start(bf16[80,768]{1,0:T(8,128)(2,1)S(1)} %pad_maximum_fusion.4.refs_0_), channel_id=1, source_target_pairs={{0,32},{16,48},{32,64},{48,80},{64,96},{80,112},{96,0},{112,16},{1... | collective-permute-start | bytes 368648 | tf_op jit(solution)/shard_map/ppermute | solution.py:33
  135.4 11.7 %collective-permute-start.28 = (bf16[80,768]{1,0:T(8,128)(2,1)S(1)}, bf16[80,768]{1,0:T(8,128)(2,1)S(1)}, u32[]{:S(2)}, u32[]{:S(2)}) collective-permute-start(bf16[80,768]{1,0:T(8,128)(2,1)S(1)} %pad_maximum_fusion.4.refs_0_), channel_id=1, source_target_pairs={{0,64},{16,80},{32,96},{48,112},{64,0},{80,16},{96,32},{112,48},{1... | collective-permute-start | bytes 368648 | tf_op jit(solution)/shard_map/ppermute | solution.py:33
  138.5 8.6 %collective-permute-start.27 = (bf16[80,768]{1,0:T(8,128)(2,1)S(1)}, bf16[80,768]{1,0:T(8,128)(2,1)S(1)}, u32[]{:S(2)}, u32[]{:S(2)}) collective-permute-start(bf16[80,768]{1,0:T(8,128)(2,1)S(1)} %pad_maximum_fusion.4.refs_0_), channel_id=1, source_target_pairs={{0,96},{16,112},{32,0},{48,16},{64,32},{80,48},{96,64},{112,80},{1... | collective-permute-start | bytes 368648 | tf_op jit(solution)/shard_map/ppermute | solution.py:33
  141.1 7.4 %copy-start.7 = (bf16[192,768]{1,0:T(8,128)(2,1)S(1)}, bf16[192,768]{1,0:T(8,128)(2,1)}, u32[]{:S(2)}) copy-start(bf16[192,768]{1,0:T(8,128)(2,1)} %get-tuple-element.103) | copy-start | bytes 884740
  141.1 9.5 %copy-start.1 = (bf16[192,384]{1,0:T(8,128)(2,1)S(1)}, bf16[192,384]{1,0:T(8,128)(2,1)}, u32[]{:S(2)}) copy-start(bf16[192,384]{1,0:T(8,128)(2,1)} %encoder.1) | copy-start | bytes 442372
  141.1 9.5 %copy-start.4 = (s32[6]{0:T(128)S(1)}, s32[6]{0:T(128)}, u32[]{:S(2)}) copy-start(s32[6]{0:T(128)} %copy-done.3) | copy-start | bytes 76
  141.1 14.0 %collective-permute-start.36 = (bf16[192,768]{1,0:T(8,128)(2,1)S(1)}, bf16[192,768]{1,0:T(8,128)(2,1)S(1)}, u32[]{:S(2)}, u32[]{:S(2)}) collective-permute-start(bf16[192,768]{1,0:T(8,128)(2,1)S(1)} %get-tuple-element.102), channel_id=1, source_target_pairs={{0,128},{16,144},{32,160},{48,176},{64,192},{80,208},{96,224},{112... | collective-permute-start | bytes 884744 | tf_op jit(solution)/shard_map/ppermute | solution.py:33
  147.1 1.4 collective-permute-start.30
  147.2 1.9 %collective-permute-start.31 = (bf16[80,768]{1,0:T(8,128)(2,1)S(1)}, bf16[80,768]{1,0:T(8,128)(2,1)S(1)}, u32[]{:S(2)}, u32[]{:S(2)}) collective-permute-start(bf16[80,768]{1,0:T(8,128)(2,1)S(1)} %collective-permute-done.27.refs_1_), channel_id=1, source_target_pairs={{0,16},{16,0},{32,48},{48,32},{64,80},{80,64},{96,112},{112,96},{1... | collective-permute-start | bytes 368648 | tf_op jit(solution)/shard_map/ppermute | solution.py:33
  147.7 2.9 %collective-permute-start.32 = (bf16[80,768]{1,0:T(8,128)(2,1)S(1)}, bf16[80,768]{1,0:T(8,128)(2,1)S(1)}, u32[]{:S(2)}, u32[]{:S(2)}) collective-permute-start(bf16[80,768]{1,0:T(8,128)(2,1)S(1)} %collective-permute-done.28.refs_2_), channel_id=1, source_target_pairs={{0,16},{16,0},{32,48},{48,32},{64,80},{80,64},{96,112},{112,96},{1... | collective-permute-start | bytes 368648 | tf_op jit(solution)/shard_map/ppermute | solution.py:33
  147.8 2.8 %collective-permute-start.33 = (bf16[80,768]{1,0:T(8,128)(2,1)S(1)}, bf16[80,768]{1,0:T(8,128)(2,1)S(1)}, u32[]{:S(2)}, u32[]{:S(2)}) collective-permute-start(bf16[80,768]{1,0:T(8,128)(2,1)S(1)} %collective-permute-done.29.refs_3_), channel_id=1, source_target_pairs={{0,16},{16,0},{32,48},{48,32},{64,80},{80,64},{96,112},{112,96},{1... | collective-permute-start | bytes 368648 | tf_op jit(solution)/shard_map/ppermute | solution.py:33
  148.5 14.3 %collective-permute-start.35 = (bf16[192,768]{1,0:T(8,128)(2,1)S(1)}, bf16[192,768]{1,0:T(8,128)(2,1)S(1)}, u32[]{:S(2)}, u32[]{:S(2)}) collective-permute-start(bf16[192,768]{1,0:T(8,128)(2,1)S(1)} %copy-done.7), channel_id=1, source_target_pairs={{0,96},{16,112},{32,0},{48,16},{64,32},{80,48},{96,64},{112,80},{1... | collective-permute-start | bytes 884744 | tf_op jit(solution)/shard_map/ppermute | solution.py:33
  149.1 13.7 %collective-permute-start.34 = (bf16[192,768]{1,0:T(8,128)(2,1)S(1)}, bf16[192,768]{1,0:T(8,128)(2,1)}, u32[]{:S(2)}, u32[]{:S(2)}) collective-permute-start(bf16[192,768]{1,0:T(8,128)(2,1)S(1)} %get-tuple-element.101), channel_id=1, source_target_pairs={{0,32},{16,48},{32,64},{48,80},{64,96},{80,112},{96,0},{112,16},{1... | collective-permute-start | bytes 884744 | tf_op jit(solution)/shard_map/ppermute | solution.py:33
  155.1 18.1 %all-to-all-start.2 = ((bf16[16,12,768]{2,1,0:T(8,128)(2,1)}), bf16[16,12,768]{2,1,0:T(8,128)(2,1)S(1)}, u32[]{:S(2)}, u32[]{:S(2)}) async-start(bf16[16,12,768]{2,1,0:T(8,128)(2,1)} %get-tuple-element.98), calls=%async_computation.2 | async-start | bytes 786432 | tf_op jit(solution)/shard_map/all_to_all | solution.py:415
